TPU v7x, 32 devices: a whole 2x2x4 slice. The times are simulated.
32 devices in a mesh: band: 16 (over z, y, x), sample: 2 (over core).
Axes of the slice: x: 2, y: 2, z: 4, core: 2. Of those that a mesh axis runs over, the one named last changes fastest.
Arguments:
- features: bfloat16 [80, 768, 1024], P('band', 'sample'), may hold values from 0 to 20
- w_point: bfloat16 [1024, 256], replicated, may hold values from -0.1875 to 0.1875
- w_atrous: bfloat16 [3, 3, 3, 1024, 256], replicated, may hold values from -0.0625 to 0.0625
- w_pool: bfloat16 [1024, 256], replicated, may hold values from -0.1875 to 0.1875
- branch_gain: float32 [5, 256], replicated, may hold values from 0.1 to 1.9
- branch_bias: float32 [5, 256], replicated, may hold values from -3 to 3
- w_project: bfloat16 [1280, 256], replicated, may hold values from -0.15625 to 0.15625
- project_gain: float32 [256], replicated, may hold values from 0.1 to 1.9
- project_bias: float32 [256], replicated, may hold values from -3 to 3
- pixel_order: int32 [80, 768], P('band', 'sample'), may hold values from 0 to 1919, as said below
Outputs:
- owned: bfloat16 [61440, 256], P(('band', 'sample'))
Inputs may be any that keep to these rules, and one draw needn't show every extreme that they name: `pixel_order`: within the 5 x 384 cells of one block of rows b * 5 to (b + 1) * 5 - 1 and columns h * 384 to (h + 1) * 384 - 1, the values are a permutation of 0 to 1919, each naming a cell of that block counted row by row.
All inputs are finite; a program needn't handle non-finite values.
Results may differ from a plain program's by a relative error of at most 0.0051.
Values may be sent and summed in bfloat16 or wider, within the bound.
No kernel may reach another device: no remote copies, remote signals or barrier semaphores. Data moves between devices by JAX's collectives and lax.ppermute only.
A program may use at most 192 MiB of HBM per device.

v0:
```python
import functools

import jax
import jax.numpy as jnp
from jax import lax
from jax.experimental import pallas as pl
from jax.experimental.pallas import tpu as pltpu
from jax.sharding import PartitionSpec as P

dilation_list = (12, 24, 36)
pad = 48
vmem_limit = 48 * 2**20
levels = 4


def activate(values, gain, shift_term):
    return jnp.maximum(values * gain + shift_term, 0.0).astype(jnp.bfloat16)


def neighbours_columns(features):
    half_count = lax.axis_size("sample")
    width = features.shape[1]
    leading = features[:, :pad]
    last = features[:, width - pad :]
    up = [(i, (i + 1) % half_count) for i in range(half_count)]
    down = [(j, i) for i, j in up]
    if half_count == 2:
        both = lax.ppermute(jnp.concatenate([leading, last], axis=1), "sample", up)
        return both[:, pad:], both[:, :pad]
    return lax.ppermute(last, "sample", up), lax.ppermute(leading, "sample", down)


def passed_along(array, by):
    band_count = lax.axis_size("band")
    half_count = lax.axis_size("sample")
    level = max(band_count // levels, 1)
    first, second = [], []
    for band in range(band_count):
        goal = band + by
        if not 0 <= goal < band_count:
            continue
        along = goal // level * level + band % level
        within = band // level * level + goal % level
        for half in range(half_count):
            middle = along if half % 2 == 0 or by % level == 0 else within
            first.append((band * half_count + half, middle * half_count + half))
            second.append((middle * half_count + half, goal * half_count + half))
    if not first:
        return jnp.zeros_like(array)
    array = lax.ppermute(array, ("band", "sample"), first)
    if by % level != 0:
        array = lax.ppermute(array, ("band", "sample"), second)
    return array


def total_over_devices(values):
    for axis in ("sample", "band"):
        size = lax.axis_size(axis)
        if size & (size - 1):
            values = lax.psum(values, axis)
            continue
        step = 1
        while step < size:
            values = values + lax.ppermute(values, axis, [(i, i ^ step) for i in range(size)])
            step *= 2
    return values


def split_of(offset, row_count):
    band_step = offset // row_count
    return band_step, offset - band_step * row_count


def taps_body(plan, row_count, x_ref, before_ref, after_ref, *refs):
    weights = refs[: len(plan)]
    outs = refs[len(plan) : -1]
    wide = refs[-1]
    width = x_ref.shape[1]
    row = pl.program_id(0)
    wide[0:pad] = before_ref[0]
    wide[pad : pad + width] = x_ref[0]
    wide[pad + width :] = after_ref[0]
    place = 0
    for (branch, row_tap), w_ref in zip(plan, weights):
        dilation = dilation_list[branch]
        summed = None
        for column_tap in range(3):
            start = pad + (column_tap - 1) * dilation
            term = jnp.dot(
                wide[start : start + width],
                w_ref[0, 0, column_tap],
                preferred_element_type=jnp.float32,
            )
            summed = term if summed is None else summed + term
        summed = summed.astype(jnp.bfloat16)
        _, remainder = split_of((row_tap - 1) * dilation, row_count)
        near = outs[place]
        place += 1
        if remainder:
            far = outs[place]
            place += 1

            @pl.when(row >= remainder)
            def _():
                near[0] = summed

            @pl.when(row < remainder)
            def _():
                far[0] = summed
        else:
            near[0] = summed


def row_taps(features, before, after, w_atrous, plan):
    row_count, width, channels = features.shape
    depth = w_atrous.shape[-1]
    in_specs = [
        pl.BlockSpec((1, width, channels), lambda r: (r, 0, 0)),
        pl.BlockSpec((1, pad, channels), lambda r: (r, 0, 0)),
        pl.BlockSpec((1, pad, channels), lambda r: (r, 0, 0)),
    ]
    out_specs, out_shapes = [], []
    for branch, row_tap in plan:
        in_specs.append(
            pl.BlockSpec(
                (1, 1, 3, channels, depth),
                functools.partial(lambda branch, row_tap, r: (branch, row_tap, 0, 0, 0), branch, row_tap),
            )
        )
        _, remainder = split_of((row_tap - 1) * dilation_list[branch], row_count)
        out_specs.append(
            pl.BlockSpec(
                (1, width, depth),
                functools.partial(lambda remainder, r: (jnp.maximum(r - remainder, 0), 0, 0), remainder),
            )
        )
        out_shapes.append(jax.ShapeDtypeStruct((row_count - remainder, width, depth), jnp.bfloat16))
        if remainder:
            out_specs.append(
                pl.BlockSpec(
                    (1, width, depth),
                    functools.partial(lambda remainder, r: (jnp.minimum(r, remainder - 1), 0, 0), remainder),
                )
            )
            out_shapes.append(jax.ShapeDtypeStruct((remainder, width, depth), jnp.bfloat16))
    return pl.pallas_call(
        functools.partial(taps_body, plan, row_count),
        grid=(row_count,),
        in_specs=in_specs,
        out_specs=out_specs,
        out_shape=out_shapes,
        scratch_shapes=[pltpu.VMEM((width + 2 * pad, channels), jnp.bfloat16)],
        compiler_params=pltpu.CompilerParams(vmem_limit_bytes=vmem_limit),
        cost_estimate=pl.CostEstimate(
            flops=len(plan) * 6 * row_count * width * channels * depth,
            bytes_accessed=2 * (row_count * width * channels + len(plan) * 3 * channels * depth),
            transcendentals=0,
        ),
    )(features, before, after, *([w_atrous] * len(plan)))


def own_body(x_ref, before_ref, after_ref, *refs):
    w_atrous = refs[:3]
    w_point, w_project, gain, shift_term, centre_ref, base_ref, wide = refs[3:]
    width = x_ref.shape[1]
    wide[0:pad] = before_ref[0]
    wide[pad : pad + width] = x_ref[0]
    wide[pad + width :] = after_ref[0]
    for branch, dilation in enumerate(dilation_list):
        summed = None
        for column_tap in range(3):
            start = pad + (column_tap - 1) * dilation
            term = jnp.dot(
                wide[start : start + width],
                w_atrous[branch][0, 0, column_tap],
                preferred_element_type=jnp.float32,
            )
            summed = term if summed is None else summed + term
        centre_ref[branch, 0] = summed
    point = jnp.dot(x_ref[0], w_point[...], preferred_element_type=jnp.float32)
    point = activate(point, gain[0:1], shift_term[0:1])
    base_ref[0] = jnp.dot(point, w_project[...], preferred_element_type=jnp.float32)


def own_rows(features, before, after, w_atrous, w_point, w_project, gain, shift_term):
    row_count, width, channels = features.shape
    depth = w_atrous.shape[-1]
    whole = lambda array: pl.BlockSpec(array.shape, lambda r: (0,) * array.ndim)
    return pl.pallas_call(
        own_body,
        grid=(row_count,),
        in_specs=[
            pl.BlockSpec((1, width, channels), lambda r: (r, 0, 0)),
            pl.BlockSpec((1, pad, channels), lambda r: (r, 0, 0)),
            pl.BlockSpec((1, pad, channels), lambda r: (r, 0, 0)),
        ]
        + [
            pl.BlockSpec(
                (1, 1, 3, channels, depth),
                functools.partial(lambda branch, r: (branch, 1, 0, 0, 0), branch),
            )
            for branch in range(3)
        ]
        + [
            whole(w_point),
            pl.BlockSpec((depth, depth), lambda r: (0, 0)),
            whole(gain),
            whole(shift_term),
        ],
        out_specs=[
            pl.BlockSpec((3, 1, width, depth), lambda r: (0, r, 0, 0)),
            pl.BlockSpec((1, width, depth), lambda r: (r, 0, 0)),
        ],
        out_shape=[
            jax.ShapeDtypeStruct((3, row_count, width, depth), jnp.float32),
            jax.ShapeDtypeStruct((row_count, width, depth), jnp.float32),
        ],
        scratch_shapes=[pltpu.VMEM((width + 2 * pad, channels), jnp.bfloat16)],
        compiler_params=pltpu.CompilerParams(vmem_limit_bytes=vmem_limit),
        cost_estimate=pl.CostEstimate(
            flops=20 * row_count * width * channels * depth,
            bytes_accessed=2 * (row_count * width * channels + 10 * channels * depth)
            + 16 * row_count * width * depth,
            transcendentals=0,
        ),
    )(features, before, after, *([w_atrous] * 3), w_point, w_project, gain, shift_term)


def join_body(plan, remainders, last, base_ref, w_project, gain, shift_term, *refs):
    row = pl.program_id(0)
    total = base_ref[0]
    place = 0
    for branch in plan:
        summed = refs[place][0, 0]
        place += 1
        for row_tap in (0, 2):
            remainder = remainders[branch, row_tap]
            near = refs[place][0].astype(jnp.float32)
            place += 1
            if remainder:
                far = refs[place][0].astype(jnp.float32)
                place += 1
                own_near = base_ref.shape[0] * pl.num_programs(0) - remainder
                near = jnp.where(row < own_near, near, far)
            summed = summed + near
        value = activate(summed, gain[branch + 1 : branch + 2], shift_term[branch + 1 : branch + 2])
        depth = value.shape[-1]
        total = total + jnp.dot(
            value,
            w_project[(branch + 1) * depth : (branch + 2) * depth],
            preferred_element_type=jnp.float32,
        )
    if last:
        pooled, project_gain, project_bias, out = refs[place:]
        out[0] = activate(total + pooled[...], project_gain[...], project_bias[...])
    else:
        refs[place][0] = total


def join(plan, base, centre, arrived, w_project, gain, shift_term, tail=None):
    row_count, width, depth = base.shape
    whole = lambda array: pl.BlockSpec(array.shape, lambda r: (0,) * array.ndim)
    block = pl.BlockSpec((1, width, depth), lambda r: (r, 0, 0))
    operands = [base, w_project, gain, shift_term]
    in_specs = [block, whole(w_project), whole(gain), whole(shift_term)]
    remainders = {}
    for branch in plan:
        operands.append(centre)
        in_specs.append(
            pl.BlockSpec(
                (1, 1, width, depth),
                functools.partial(lambda branch, r: (branch, r, 0, 0), branch),
            )
        )
        for row_tap in (0, 2):
            _, remainder = split_of((row_tap - 1) * dilation_list[branch], row_count)
            remainders[branch, row_tap] = remainder
            near_count = row_count - remainder
            near, far = arrived[branch, row_tap]
            operands.append(near)
            in_specs.append(
                pl.BlockSpec(
                    (1, width, depth),
                    functools.partial(lambda n, r: (jnp.minimum(r, n - 1), 0, 0), near_count),
                )
            )
            if remainder:
                operands.append(far)
                in_specs.append(
                    pl.BlockSpec(
                        (1, width, depth),
                        functools.partial(lambda n, r: (jnp.maximum(r - n, 0), 0, 0), near_count),
                    )
                )
    out_type = jnp.float32
    if tail is not None:
        operands += list(tail)
        in_specs += [whole(array) for array in tail]
        out_type = jnp.bfloat16
    return pl.pallas_call(
        functools.partial(join_body, plan, remainders, tail is not None),
        grid=(row_count,),
        in_specs=in_specs,
        out_specs=block,
        out_shape=jax.ShapeDtypeStruct((row_count, width, depth), out_type),
        compiler_params=pltpu.CompilerParams(vmem_limit_bytes=vmem_limit),
        cost_estimate=pl.CostEstimate(
            flops=len(plan) * 2 * row_count * width * depth * depth,
            bytes_accessed=row_count * width * depth * (8 + 8 * len(plan)),
            transcendentals=0,
        ),
    )(*operands)


def shards(
    features,
    w_point,
    w_atrous,
    w_pool,
    branch_gain,
    branch_bias,
    w_project,
    project_gain,
    project_bias,
    pixel_order,
):
    row_count, width_local, channels = features.shape
    band_count = lax.axis_size("band")
    half_count = lax.axis_size("sample")
    device_count = band_count * half_count
    before, after = neighbours_columns(features)

    arrived = {}
    for calls in (((2, 0),), ((2, 2),), ((1, 0), (1, 2)), ((0, 0), (0, 2))):
        pieces = list(row_taps(features, before, after, w_atrous, calls))
        for branch, row_tap in calls:
            band_step, remainder = split_of((row_tap - 1) * dilation_list[branch], row_count)
            near = passed_along(pieces.pop(0), -band_step)
            far = passed_along(pieces.pop(0), -band_step - 1) if remainder else None
            arrived[branch, row_tap] = (near, far)

    local_totals = jnp.sum(features, axis=(0, 1), dtype=jnp.float32)
    totals = total_over_devices(local_totals)
    pooled = totals / (row_count * band_count * width_local * half_count)
    pool_input = pooled.astype(jnp.bfloat16)
    pool_value = jnp.dot(pool_input[None, :], w_pool, preferred_element_type=jnp.float32)
    pool_branch = activate(pool_value, branch_gain[4:5], branch_bias[4:5])
    depth = w_project.shape[-1]
    pool_projected = jnp.dot(pool_branch, w_project[4 * depth :], preferred_element_type=jnp.float32)

    centre, base = own_rows(
        features, before, after, w_atrous, w_point, w_project, branch_gain, branch_bias
    )
    base = join((2, 1), base, centre, arrived, w_project, branch_gain, branch_bias)
    tail = (pool_projected, project_gain[None, :], project_bias[None, :])
    projected = join((0,), base, centre, arrived, w_project, branch_gain, branch_bias, tail)

    pixels = row_count * width_local
    per_peer = pixels // device_count
    slots = pixel_order.reshape(pixels)
    outgoing = jnp.take(projected.reshape(pixels, depth), slots, axis=0)
    outgoing = outgoing.reshape(device_count, per_peer, depth)
    owned = lax.all_to_all(outgoing, ("band", "sample"), split_axis=0, concat_axis=0, tiled=True)
    return owned.reshape(device_count * per_peer, depth)


def solution(mesh):
    in_specs = (
        P("band", "sample", None),
        P(),
        P(),
        P(),
        P(),
        P(),
        P(),
        P(),
        P(),
        P("band", "sample"),
    )
    out_specs = P(("band", "sample"), None)
    return jax.shard_map(shards, mesh=mesh, in_specs=in_specs, out_specs=out_specs, check_vma=False)
```

profile of v0, /device:TPU:0, one launch (start us, length us, event | category | flops | bytes accessed | tf_op | source)
XLA Modules:
  0.0 258.4 jit_solution(12553838124451071361)
XLA Ops:
  0.0 1.4 fusion.11
  2.5 0.7 convert_reduce_fusion
  3.7 0.8 collective-permute-done.21
  4.5 2.8 %collective-permute-start.22 = (f32[1024]{0:T(1024)S(1)}, f32[1024]{0:T(1024)S(1)}, u32[]{:S(2)}, u32[]{:S(2)}) collective-permute-start(f32[1024]{0:T(1024)S(1)} %add.42), channel_id=1, source_target_pairs={{0,2},{2,0},{4,6},{6,4},{8,10},{10,8},{12,14},{14,12},{16,18},{18,... | collective-permute-start | bytes 12296 | tf_op jit(solution)/shard_map/ppermute | solution.py:64
  7.3 1.6 collective-permute-done.22
  8.9 2.1 collective-permute-start.23
  11.0 1.6 collective-permute-done.23
  12.6 2.1 collective-permute-start.24
  14.6 1.6 collective-permute-done.24
  16.2 3.0 %collective-permute-start.25 = (f32[1024]{0:T(1024)S(1)}, f32[1024]{0:T(1024)S(1)}, u32[]{:S(2)}, u32[]{:S(2)}) collective-permute-start(f32[1024]{0:T(1024)S(1)} %add.45), channel_id=1, source_target_pairs={{0,16},{2,18},{4,20},{6,22},{8,24},{10,26},{12,28},{14,30},{16,0},... | collective-permute-start | bytes 12296 | tf_op jit(solution)/shard_map/ppermute | solution.py:64
  19.3 16.7 %shard_map.103 = (bf16[4,384,256]{2,1,0:T(8,128)(2,1)}, bf16[1,384,256]{2,1,0:T(8,128)(2,1)S(1)}, bf16[1,384,256]{2,1,0:T(8,128)(2,1)S(1)}, bf16[4,384,256]{2,1,0:T(8,128)(2,1)S(1)}) custom-call(bf16[5,384,1024]{2,1,0:T(8,128)(2,1)} %x_ref.9, bf16[5,48,1024]{2,1,0:T(8,128)(2,1)S(1)} %get-tuple-element.36.before_ref, ...), custom_call_target="tpu_custom_call" | custom-call | flops 6039797760 | bytes 7077888 | tf_op jit(solution)/shard_map/pallas_call | solution.py:146
  36.1 17.0 %shard_map.105 = (bf16[2,384,256]{2,1,0:T(8,128)(2,1)S(1)}, bf16[3,384,256]{2,1,0:T(8,128)(2,1)}, bf16[3,384,256]{2,1,0:T(8,128)(2,1)S(1)}, bf16[2,384,256]{2,1,0:T(8,128)(2,1)}) custom-call(bf16[5,384,1024]{2,1,0:T(8,128)(2,1)} %x_ref.9, bf16[5,48,1024]{2,1,0:T(8,128)(2,1)S(1)} %get-tuple-element.36.before_ref, ...), custom_call_target="tpu_custom_call" | custom-call | flops 6039797760 | bytes 7077888 | tf_op jit(solution)/shard_map/pallas_call | solution.py:146
  53.1 0.8 copy-done.19
  53.9 1.3 collective-permute-start.10
  55.2 4.6 %collective-permute-start.9 = (bf16[1,384,256]{2,1,0:T(8,128)(2,1)S(1)}, bf16[1,384,256]{2,1,0:T(8,128)(2,1)S(1)}, u32[]{:S(2)}, u32[]{:S(2)}) collective-permute-start(bf16[1,384,256]{2,1,0:T(8,128)(2,1)S(1)} %get-tuple-element.26), channel_id=1, source_target_pairs={{0,8},{1,9},{2,10},{3,11},{4,12},{5,13},{6,14},{7,15},{8,16},{9,17... | collective-permute-start | bytes 589832 | tf_op jit(solution)/shard_map/ppermute | solution.py:50
  59.7 6.2 %shard_map.101 = (bf16[1,384,256]{2,1,0:T(8,128)(2,1)S(1)}, bf16[4,384,256]{2,1,0:T(8,128)(2,1)}) custom-call(bf16[5,384,1024]{2,1,0:T(8,128)(2,1)S(1)} %copy-done.2, bf16[5,48,1024]{2,1,0:T(8,128)(2,1)S(1)} %get-tuple-element.36.before_ref, bf16[5,48,1024]{2,1,0:T(8,128)(2,1)S(1)} %get-tuple-element.35.after_ref, bf16[3,3,3,1024,256]{4,3,2,1,0:T(8,128)(2,1)} %refs_1_.5), custom_call_target="tpu_custom_call" | custom-call | flops 3019898880 | bytes 5505024 | tf_op jit(solution)/shard_map/pallas_call | solution.py:146
  65.9 1.3 collective-permute-start.11
  67.2 4.4 %collective-permute-start.7 = (bf16[4,384,256]{2,1,0:T(8,128)(2,1)}, bf16[4,384,256]{2,1,0:T(8,128)(2,1)}, u32[]{:S(2)}, u32[]{:S(2)}) collective-permute-start(bf16[4,384,256]{2,1,0:T(8,128)(2,1)} %get-tuple-element.25), channel_id=1, source_target_pairs={{0,8},{1,3},{2,10},{3,5},{4,12},{5,7},{6,22},{7,1},{8,16},{9,11},{... | collective-permute-start | bytes 2359304 | tf_op jit(solution)/shard_map/ppermute | solution.py:50
  71.6 5.3 %collective-permute-start.2 = (bf16[4,384,256]{2,1,0:T(8,128)(2,1)}, bf16[4,384,256]{2,1,0:T(8,128)(2,1)}, u32[]{:S(2)}, u32[]{:S(2)}) collective-permute-start(bf16[4,384,256]{2,1,0:T(8,128)(2,1)} %get-tuple-element.22), channel_id=1, source_target_pairs={{0,8},{1,7},{2,18},{3,1},{4,20},{5,3},{6,22},{7,5},{8,16},{9,15},{... | collective-permute-start | bytes 2359304 | tf_op jit(solution)/shard_map/ppermute | solution.py:50
  77.0 2.1 collective-permute-start.1
  79.1 1.6 collective-permute-start.13
  80.6 6.2 %shard_map.102 = (bf16[4,384,256]{2,1,0:T(8,128)(2,1)}, bf16[1,384,256]{2,1,0:T(8,128)(2,1)S(1)}) custom-call(bf16[5,384,1024]{2,1,0:T(8,128)(2,1)S(1)} %copy-done.2, bf16[5,48,1024]{2,1,0:T(8,128)(2,1)S(1)} %get-tuple-element.36.before_ref, bf16[5,48,1024]{2,1,0:T(8,128)(2,1)S(1)} %get-tuple-element.35.after_ref, bf16[3,3,3,1024,256]{4,3,2,1,0:T(8,128)(2,1)} %refs_1_.5), custom_call_target="tpu_custom_call" | custom-call | flops 3019898880 | bytes 5505024 | tf_op jit(solution)/shard_map/pallas_call | solution.py:146
  86.8 6.3 %collective-permute-done.1.refs_1_ = bf16[1,384,256]{2,1,0:T(8,128)(2,1)S(1)} collective-permute-done((bf16[1,384,256]{2,1,0:T(8,128)(2,1)S(1)}, bf16[1,384,256]{2,1,0:T(8,128)(2,1)S(1)}, u32[]{:S(2)}, u32[]{:S(2)}) %collective-permute-start.1) | collective-permute-done | bytes 196640 | tf_op jit(solution)/shard_map/ppermute | solution.py:50
  93.7 1.3 collective-permute-start.6
  95.0 7.2 %collective-permute-done.6.refs_4_ = bf16[1,384,256]{2,1,0:T(8,128)(2,1)S(1)} collective-permute-done((bf16[1,384,256]{2,1,0:T(8,128)(2,1)S(1)}, bf16[1,384,256]{2,1,0:T(8,128)(2,1)S(1)}, u32[]{:S(2)}, u32[]{:S(2)}) %collective-permute-start.6) | collective-permute-done | bytes 196640 | tf_op jit(solution)/shard_map/ppermute | solution.py:50
  102.2 0.7 copy-done.13
  102.9 1.3 collective-permute-start.19
  104.2 6.0 %collective-permute-start.15 = (bf16[3,384,256]{2,1,0:T(8,128)(2,1)}, bf16[3,384,256]{2,1,0:T(8,128)(2,1)}, u32[]{:S(2)}, u32[]{:S(2)}) collective-permute-start(bf16[3,384,256]{2,1,0:T(8,128)(2,1)} %get-tuple-element.30), channel_id=1, source_target_pairs={{0,0},{1,5},{2,2},{3,7},{4,12},{5,1},{6,14},{7,3},{8,8},{9,13},{10... | collective-permute-start | bytes 1769480 | tf_op jit(solution)/shard_map/ppermute | solution.py:50
  110.2 6.9 %collective-permute-done.19 = bf16[2,384,256]{2,1,0:T(8,128)(2,1)} collective-permute-done((bf16[2,384,256]{2,1,0:T(8,128)(2,1)}, bf16[2,384,256]{2,1,0:T(8,128)(2,1)}, u32[]{:S(2)}, u32[]{:S(2)}) %collective-permute-start.19) | collective-permute-done | bytes 393248 | tf_op jit(solution)/shard_map/ppermute | solution.py:50
  117.2 1.3 collective-permute-start.4
  118.5 18.2 %collective-permute-start.12 = (bf16[4,384,256]{2,1,0:T(8,128)(2,1)}, bf16[4,384,256]{2,1,0:T(8,128)(2,1)S(1)}, u32[]{:S(2)}, u32[]{:S(2)}) collective-permute-start(bf16[4,384,256]{2,1,0:T(8,128)(2,1)} %collective-permute-done.11), channel_id=1, source_target_pairs={{2,0},{9,1},{4,2},{11,3},{6,4},{13,5},{0,6},{23,7},{10,8},{17,9},{... | collective-permute-start | bytes 2359304 | tf_op jit(solution)/shard_map/ppermute | solution.py:52
  136.7 1.5 collective-permute-start.8
  138.3 1.5 collective-permute-start.3
  139.9 1.3 collective-permute-start.17
  141.6 12.2 %collective-permute-done.17 = bf16[3,384,256]{2,1,0:T(8,128)(2,1)} collective-permute-done((bf16[3,384,256]{2,1,0:T(8,128)(2,1)}, bf16[3,384,256]{2,1,0:T(8,128)(2,1)}, u32[]{:S(2)}, u32[]{:S(2)}) %collective-permute-start.17) | collective-permute-done | bytes 589856 | tf_op jit(solution)/shard_map/ppermute | solution.py:50
  153.8 1.3 collective-permute-start.14
  155.2 14.7 %collective-permute-start.20 = (bf16[2,384,256]{2,1,0:T(8,128)(2,1)}, bf16[2,384,256]{2,1,0:T(8,128)(2,1)S(1)}, u32[]{:S(2)}, u32[]{:S(2)}) collective-permute-start(bf16[2,384,256]{2,1,0:T(8,128)(2,1)} %collective-permute-done.19), channel_id=1, source_target_pairs={{6,0},{1,1},{0,2},{11,3},{2,4},{13,5},{4,6},{15,7},{14,8},{9,9},{8... | collective-permute-start | bytes 1179656 | tf_op jit(solution)/shard_map/ppermute | solution.py:52
  169.9 2.8 %collective-permute-start.16 = (bf16[3,384,256]{2,1,0:T(8,128)(2,1)}, bf16[3,384,256]{2,1,0:T(8,128)(2,1)S(1)}, u32[]{:S(2)}, u32[]{:S(2)}) collective-permute-start(bf16[3,384,256]{2,1,0:T(8,128)(2,1)} %collective-permute-done.15), channel_id=1, source_target_pairs={{0,4},{5,5},{2,6},{7,7},{12,8},{1,9},{14,10},{3,11},{8,12},{13,13}... | collective-permute-start | bytes 1769480 | tf_op jit(solution)/shard_map/ppermute | solution.py:52
  172.7 1.9 collective-permute-start.18
  174.7 2.9 %collective-permute-start.5 = (bf16[4,384,256]{2,1,0:T(8,128)(2,1)}, bf16[4,384,256]{2,1,0:T(8,128)(2,1)S(1)}, u32[]{:S(2)}, u32[]{:S(2)}) collective-permute-start(bf16[4,384,256]{2,1,0:T(8,128)(2,1)} %collective-permute-done.4), channel_id=1, source_target_pairs={{6,0},{9,1},{0,2},{19,3},{2,4},{21,5},{4,6},{23,7},{14,8},{17,9},{... | collective-permute-start | bytes 2359304 | tf_op jit(solution)/shard_map/ppermute | solution.py:52
  177.6 15.2 %shard_map.100 = (f32[3,5,384,256]{3,2,1,0:T(8,128)}, f32[5,384,256]{2,1,0:T(8,128)S(1)}) custom-call(bf16[5,384,1024]{2,1,0:T(8,128)(2,1)} %x_ref.9, bf16[5,48,1024]{2,1,0:T(8,128)(2,1)S(1)} %get-tuple-element.36.before_ref, bf16[5,48,1024]{2,1,0:T(8,128)(2,1)S(1)} %get-tuple-element.35.after_ref, bf16[3,3,3,1024,256]{4,3,2,1,0:T(8,128)(2,1)} %refs_1_.5, ...), custom_call_target="tpu_custom_call" | custom-call | flops 10066329600 | bytes 17039360 | tf_op jit(solution)/shard_map/pallas_call | solution.py:189
  192.8 1.3 copy-done.5
  194.1 6.5 %shard_map.104.base_ref = f32[5,384,256]{2,1,0:T(8,128)} custom-call(f32[5,384,256]{2,1,0:T(8,128)} %copy-done.5, bf16[1280,256]{1,0:T(8,128)(2,1)S(1)} %copy-done.4, f32[5,256]{1,0:T(8,128)S(1)} %copy-done.15, f32[5,256]{1,0:T(8,128)S(1)} %copy-done.16, f32[3,5,384,256]{3,2,1,0:T(8,128)} %get-tuple-element.20.refs_0_.refs_5_, ...), custom_call_target="tpu_custom_call" | custom-call | flops 503316480 | bytes 11796480 | tf_op jit(solution)/shard_map/pallas_call | solution.py:300
  200.7 1.5 copy-done.3
  202.3 3.9 %shard_map.106 = bf16[5,384,256]{2,1,0:T(8,128)(2,1)S(1)} custom-call(f32[5,384,256]{2,1,0:T(8,128)S(1)} %copy-done.3, bf16[1280,256]{1,0:T(8,128)(2,1)S(1)} %copy-done.4, f32[5,256]{1,0:T(8,128)S(1)} %copy-done.15, f32[5,256]{1,0:T(8,128)S(1)} %copy-done.16, f32[3,5,384,256]{3,2,1,0:T(8,128)} %get-tuple-element.20.refs_0_.refs_5_, ...), custom_call_target="tpu_custom_call" | custom-call | flops 251658240 | bytes 7864320 | tf_op jit(solution)/shard_map/pallas_call | solution.py:300
  206.2 6.4 %gather_fusion = bf16[1920,256]{1,0:T(8,128)(2,1)S(1)} fusion(bf16[1920,256]{1,0:T(8,128)(2,1)S(1)} %bitcast.15, s32[2048]{0:T(1024)S(1)} %pad_clamp_fusion), kind=kCustom, calls=%fused_computation | custom fusion | bytes 1973760 | tf_op jit(solution)/shard_map/jit(_take)/gather | solution.py:361
  213.2 44.1 %all_to_all.5 = bf16[32,60,256]{2,1,0:T(8,128)(2,1)S(1)} all-to-all(bf16[32,60,256]{2,1,0:T(8,128)(2,1)S(1)} %broadcast_select_fusion), channel_id=1, replica_groups=mesh['band'=16,'sample'=2] {'band','sample'}, dimensions={0} | all-to-all | bytes 1966080 | tf_op jit(solution)/shard_map/all_to_all | solution.py:363
  257.3 1.1 reshape.63
  (74 shorter events, 3.5 us)
Async XLA Ops:
  0.0 141.2 %copy-start = (bf16[1024,256]{1,0:T(8,128)(2,1)S(1)}, bf16[1024,256]{1,0:T(8,128)(2,1)}, u32[]{:S(2)}) copy-start(bf16[1024,256]{1,0:T(8,128)(2,1)} %param.13) | copy-start | bytes 1572868
  0.0 2.5 copy-start.1
  1.5 17.8 %collective-permute-start = (bf16[5,96,1024]{2,1,0:T(8,128)(2,1)S(1)}, bf16[5,96,1024]{2,1,0:T(8,128)(2,1)S(1)}, u32[]{:S(2)}, u32[]{:S(2)}) collective-permute-start(bf16[5,96,1024]{2,1,0:T(8,128)(2,1)S(1)} %pad_maximum_fusion), channel_id=1, source_target_pairs={{0,1},{1,0},{2,3},{3,2},{4,5},{5,4},{6,7},{7,6},{8,9},{9,8},{10,11... | collective-permute-start | bytes 2949128 | tf_op jit(solution)/shard_map/ppermute | solution.py:28
  3.2 1.3 collective-permute-start.21
  4.5 4.4 %collective-permute-start.22 = (f32[1024]{0:T(1024)S(1)}, f32[1024]{0:T(1024)S(1)}, u32[]{:S(2)}, u32[]{:S(2)}) collective-permute-start(f32[1024]{0:T(1024)S(1)} %add.42), channel_id=1, source_target_pairs={{0,2},{2,0},{4,6},{6,4},{8,10},{10,8},{12,14},{14,12},{16,18},{18,... | collective-permute-start | bytes 12296 | tf_op jit(solution)/shard_map/ppermute | solution.py:64
  8.9 3.6 %collective-permute-start.23 = (f32[1024]{0:T(1024)S(1)}, f32[1024]{0:T(1024)S(1)}, u32[]{:S(2)}, u32[]{:S(2)}) collective-permute-start(f32[1024]{0:T(1024)S(1)} %add.43), channel_id=1, source_target_pairs={{0,4},{2,6},{4,0},{6,2},{8,12},{10,14},{12,8},{14,10},{16,20},{18,... | collective-permute-start | bytes 12296 | tf_op jit(solution)/shard_map/ppermute | solution.py:64
  12.6 3.7 %collective-permute-start.24 = (f32[1024]{0:T(1024)S(1)}, f32[1024]{0:T(1024)S(1)}, u32[]{:S(2)}, u32[]{:S(2)}) collective-permute-start(f32[1024]{0:T(1024)S(1)} %add.44), channel_id=1, source_target_pairs={{0,8},{2,10},{4,12},{6,14},{8,0},{10,2},{12,4},{14,6},{16,24},{18,... | collective-permute-start | bytes 12296 | tf_op jit(solution)/shard_map/ppermute | solution.py:64
  16.2 55.4 %collective-permute-start.25 = (f32[1024]{0:T(1024)S(1)}, f32[1024]{0:T(1024)S(1)}, u32[]{:S(2)}, u32[]{:S(2)}) collective-permute-start(f32[1024]{0:T(1024)S(1)} %add.45), channel_id=1, source_target_pairs={{0,16},{2,18},{4,20},{6,22},{8,24},{10,26},{12,28},{14,30},{16,0},... | collective-permute-start | bytes 12296 | tf_op jit(solution)/shard_map/ppermute | solution.py:64
  36.1 23.7 %copy-start.2 = (bf16[5,384,1024]{2,1,0:T(8,128)(2,1)S(1)}, bf16[5,384,1024]{2,1,0:T(8,128)(2,1)}, u32[]{:S(2)}) copy-start(bf16[5,384,1024]{2,1,0:T(8,128)(2,1)} %x_ref.9) | copy-start | bytes 11796484
  53.1 0.8 copy-start.19
  53.9 23.1 %collective-permute-start.10 = (bf16[1,384,256]{2,1,0:T(8,128)(2,1)S(1)}, bf16[1,384,256]{2,1,0:T(8,128)(2,1)S(1)}, u32[]{:S(2)}, u32[]{:S(2)}) collective-permute-start(bf16[1,384,256]{2,1,0:T(8,128)(2,1)S(1)} %get-tuple-element.27), channel_id=1, source_target_pairs={{8,0},{9,1},{10,2},{11,3},{12,4},{13,5},{14,6},{15,7},{16,8},{17,9... | collective-permute-start | bytes 589832 | tf_op jit(solution)/shard_map/ppermute | solution.py:50
  55.2 23.8 %collective-permute-start.9 = (bf16[1,384,256]{2,1,0:T(8,128)(2,1)S(1)}, bf16[1,384,256]{2,1,0:T(8,128)(2,1)S(1)}, u32[]{:S(2)}, u32[]{:S(2)}) collective-permute-start(bf16[1,384,256]{2,1,0:T(8,128)(2,1)S(1)} %get-tuple-element.26), channel_id=1, source_target_pairs={{0,8},{1,9},{2,10},{3,11},{4,12},{5,13},{6,14},{7,15},{8,16},{9,17... | collective-permute-start | bytes 589832 | tf_op jit(solution)/shard_map/ppermute | solution.py:50
  65.9 52.5 %collective-permute-start.11 = (bf16[4,384,256]{2,1,0:T(8,128)(2,1)S(1)}, bf16[4,384,256]{2,1,0:T(8,128)(2,1)}, u32[]{:S(2)}, u32[]{:S(2)}) collective-permute-start(bf16[4,384,256]{2,1,0:T(8,128)(2,1)S(1)} %get-tuple-element.28), channel_id=1, source_target_pairs={{10,2},{11,9},{12,4},{13,11},{14,6},{15,13},{16,0},{17,23},{18,10}... | collective-permute-start | bytes 2359304 | tf_op jit(solution)/shard_map/ppermute | solution.py:50
  67.2 69.5 %collective-permute-start.7 = (bf16[4,384,256]{2,1,0:T(8,128)(2,1)}, bf16[4,384,256]{2,1,0:T(8,128)(2,1)}, u32[]{:S(2)}, u32[]{:S(2)}) collective-permute-start(bf16[4,384,256]{2,1,0:T(8,128)(2,1)} %get-tuple-element.25), channel_id=1, source_target_pairs={{0,8},{1,3},{2,10},{3,5},{4,12},{5,7},{6,22},{7,1},{8,16},{9,11},{... | collective-permute-start | bytes 2359304 | tf_op jit(solution)/shard_map/ppermute | solution.py:50
  71.6 66.7 %collective-permute-start.2 = (bf16[4,384,256]{2,1,0:T(8,128)(2,1)}, bf16[4,384,256]{2,1,0:T(8,128)(2,1)}, u32[]{:S(2)}, u32[]{:S(2)}) collective-permute-start(bf16[4,384,256]{2,1,0:T(8,128)(2,1)} %get-tuple-element.22), channel_id=1, source_target_pairs={{0,8},{1,7},{2,18},{3,1},{4,20},{5,3},{6,22},{7,5},{8,16},{9,15},{... | collective-permute-start | bytes 2359304 | tf_op jit(solution)/shard_map/ppermute | solution.py:50
  77.0 9.9 %copy-start.7 = (bf16[1,384,256]{2,1,0:T(8,128)(2,1)}, bf16[1,384,256]{2,1,0:T(8,128)(2,1)S(1)}, u32[]{:S(2)}) copy-start(bf16[1,384,256]{2,1,0:T(8,128)(2,1)S(1)} %collective-permute-done.10.refs_8_) | copy-start | bytes 589828
  77.0 16.1 %collective-permute-start.1 = (bf16[1,384,256]{2,1,0:T(8,128)(2,1)S(1)}, bf16[1,384,256]{2,1,0:T(8,128)(2,1)S(1)}, u32[]{:S(2)}, u32[]{:S(2)}) collective-permute-start(bf16[1,384,256]{2,1,0:T(8,128)(2,1)S(1)} %get-tuple-element.21), channel_id=1, source_target_pairs={{0,16},{1,17},{2,18},{3,19},{4,20},{5,21},{6,22},{7,23},{8,24},{9,... | collective-permute-start | bytes 589832 | tf_op jit(solution)/shard_map/ppermute | solution.py:50
  79.0 7.8 %copy-start.9 = (bf16[1,384,256]{2,1,0:T(8,128)(2,1)}, bf16[1,384,256]{2,1,0:T(8,128)(2,1)S(1)}, u32[]{:S(2)}) copy-start(bf16[1,384,256]{2,1,0:T(8,128)(2,1)S(1)} %collective-permute-done.9.refs_7_) | copy-start | bytes 589828
  79.0 31.1 %copy-start.20 = (s32[5,384]{1,0:T(8,128)S(1)}, s32[5,384]{1,0:T(8,128)}, u32[]{:S(2)}) copy-start(s32[5,384]{1,0:T(8,128)} %param.19) | copy-start | bytes 23044
  79.0 62.2 %copy-start.4 = (bf16[1280,256]{1,0:T(8,128)(2,1)S(1)}, bf16[1280,256]{1,0:T(8,128)(2,1)}, u32[]{:S(2)}) copy-start(bf16[1280,256]{1,0:T(8,128)(2,1)} %w_project.3) | copy-start | bytes 1966084
  79.1 62.2 %copy-start.15 = (f32[5,256]{1,0:T(8,128)S(1)}, f32[5,256]{1,0:T(8,128)}, u32[]{:S(2)}) copy-start(f32[5,256]{1,0:T(8,128)} %gain.3) | copy-start | bytes 15364
  79.1 62.2 %copy-start.16 = (f32[5,256]{1,0:T(8,128)S(1)}, f32[5,256]{1,0:T(8,128)}, u32[]{:S(2)}) copy-start(f32[5,256]{1,0:T(8,128)} %shift_term.3) | copy-start | bytes 15364
  79.1 98.5 %copy-start.6 = (bf16[1024,256]{1,0:T(8,128)(2,1)S(1)}, bf16[1024,256]{1,0:T(8,128)(2,1)}, u32[]{:S(2)}) copy-start(bf16[1024,256]{1,0:T(8,128)(2,1)} %refs_3_.1) | copy-start | bytes 1572868
  79.1 25.1 %collective-permute-start.13 = (bf16[2,384,256]{2,1,0:T(8,128)(2,1)S(1)}, bf16[2,384,256]{2,1,0:T(8,128)(2,1)}, u32[]{:S(2)}, u32[]{:S(2)}) collective-permute-start(bf16[2,384,256]{2,1,0:T(8,128)(2,1)S(1)} %get-tuple-element.29), channel_id=1, source_target_pairs={{0,0},{1,7},{2,10},{3,1},{4,12},{5,3},{6,14},{7,5},{8,8},{9,15},{1... | collective-permute-start | bytes 1179656 | tf_op jit(solution)/shard_map/ppermute | solution.py:50
  93.1 0.7 copy-start.11
  93.7 8.5 %collective-permute-start.6 = (bf16[1,384,256]{2,1,0:T(8,128)(2,1)S(1)}, bf16[1,384,256]{2,1,0:T(8,128)(2,1)S(1)}, u32[]{:S(2)}, u32[]{:S(2)}) collective-permute-start(bf16[1,384,256]{2,1,0:T(8,128)(2,1)S(1)} %get-tuple-element.24), channel_id=1, source_target_pairs={{16,0},{17,1},{18,2},{19,3},{20,4},{21,5},{22,6},{23,7},{24,8},{25... | collective-permute-start | bytes 589832 | tf_op jit(solution)/shard_map/ppermute | solution.py:50
  102.2 0.7 copy-start.13
  102.9 14.3 %collective-permute-start.19 = (bf16[2,384,256]{2,1,0:T(8,128)(2,1)}, bf16[2,384,256]{2,1,0:T(8,128)(2,1)}, u32[]{:S(2)}, u32[]{:S(2)}) collective-permute-start(bf16[2,384,256]{2,1,0:T(8,128)(2,1)} %get-tuple-element.32), channel_id=1, source_target_pairs={{6,6},{7,1},{8,0},{9,11},{10,2},{11,13},{12,4},{13,15},{14,14},{15... | collective-permute-start | bytes 1179656 | tf_op jit(solution)/shard_map/ppermute | solution.py:50
  104.2 35.7 %collective-permute-start.15 = (bf16[3,384,256]{2,1,0:T(8,128)(2,1)}, bf16[3,384,256]{2,1,0:T(8,128)(2,1)}, u32[]{:S(2)}, u32[]{:S(2)}) collective-permute-start(bf16[3,384,256]{2,1,0:T(8,128)(2,1)} %get-tuple-element.30), channel_id=1, source_target_pairs={{0,0},{1,5},{2,2},{3,7},{4,12},{5,1},{6,14},{7,3},{8,8},{9,13},{10... | collective-permute-start | bytes 1769480 | tf_op jit(solution)/shard_map/ppermute | solution.py:50
  117.2 38.0 %collective-permute-start.4 = (bf16[4,384,256]{2,1,0:T(8,128)(2,1)}, bf16[4,384,256]{2,1,0:T(8,128)(2,1)}, u32[]{:S(2)}, u32[]{:S(2)}) collective-permute-start(bf16[4,384,256]{2,1,0:T(8,128)(2,1)} %get-tuple-element.23), channel_id=1, source_target_pairs={{14,6},{15,9},{16,0},{17,19},{18,2},{19,21},{20,4},{21,23},{22,14}... | collective-permute-start | bytes 2359304 | tf_op jit(solution)/shard_map/ppermute | solution.py:50
  118.5 51.4 %collective-permute-start.12 = (bf16[4,384,256]{2,1,0:T(8,128)(2,1)}, bf16[4,384,256]{2,1,0:T(8,128)(2,1)S(1)}, u32[]{:S(2)}, u32[]{:S(2)}) collective-permute-start(bf16[4,384,256]{2,1,0:T(8,128)(2,1)} %collective-permute-done.11), channel_id=1, source_target_pairs={{2,0},{9,1},{4,2},{11,3},{6,4},{13,5},{0,6},{23,7},{10,8},{17,9},{... | collective-permute-start | bytes 2359304 | tf_op jit(solution)/shard_map/ppermute | solution.py:52
  136.7 36.0 %collective-permute-start.8 = (bf16[4,384,256]{2,1,0:T(8,128)(2,1)}, bf16[4,384,256]{2,1,0:T(8,128)(2,1)}, u32[]{:S(2)}, u32[]{:S(2)}) collective-permute-start(bf16[4,384,256]{2,1,0:T(8,128)(2,1)} %collective-permute-done.7), channel_id=1, source_target_pairs={{8,10},{3,11},{10,12},{5,13},{12,14},{7,15},{22,16},{1,17},{16,18}... | collective-permute-start | bytes 2359304 | tf_op jit(solution)/shard_map/ppermute | solution.py:52
  138.3 36.4 %collective-permute-start.3 = (bf16[4,384,256]{2,1,0:T(8,128)(2,1)}, bf16[4,384,256]{2,1,0:T(8,128)(2,1)}, u32[]{:S(2)}, u32[]{:S(2)}) collective-permute-start(bf16[4,384,256]{2,1,0:T(8,128)(2,1)} %collective-permute-done.2), channel_id=1, source_target_pairs={{8,14},{7,15},{18,16},{1,17},{20,18},{3,19},{22,20},{5,21},{16,22}... | collective-permute-start | bytes 2359304 | tf_op jit(solution)/shard_map/ppermute | solution.py:52
  139.9 14.0 %collective-permute-start.17 = (bf16[3,384,256]{2,1,0:T(8,128)(2,1)}, bf16[3,384,256]{2,1,0:T(8,128)(2,1)}, u32[]{:S(2)}, u32[]{:S(2)}) collective-permute-start(bf16[3,384,256]{2,1,0:T(8,128)(2,1)} %copy-done.19), channel_id=1, source_target_pairs={{4,4},{5,1},{6,6},{7,3},{8,0},{9,13},{10,2},{11,15},{12,12},{13,9}... | collective-permute-start | bytes 1769480 | tf_op jit(solution)/shard_map/ppermute | solution.py:50
  141.5 52.5 %copy-start.8 = (bf16[1,384,256]{2,1,0:T(8,128)(2,1)S(1)}, bf16[1,384,256]{2,1,0:T(8,128)(2,1)}, u32[]{:S(2)}) copy-start(bf16[1,384,256]{2,1,0:T(8,128)(2,1)} %copy-done.7) | copy-start | bytes 589828
  141.6 52.5 %copy-start.10 = (bf16[1,384,256]{2,1,0:T(8,128)(2,1)S(1)}, bf16[1,384,256]{2,1,0:T(8,128)(2,1)}, u32[]{:S(2)}) copy-start(bf16[1,384,256]{2,1,0:T(8,128)(2,1)} %copy-done.9) | copy-start | bytes 589828
  141.6 52.6 %copy-start.12 = (bf16[1,384,256]{2,1,0:T(8,128)(2,1)S(1)}, bf16[1,384,256]{2,1,0:T(8,128)(2,1)}, u32[]{:S(2)}) copy-start(bf16[1,384,256]{2,1,0:T(8,128)(2,1)} %copy-done.11) | copy-start | bytes 589828
  141.6 52.6 %copy-start.14 = (bf16[1,384,256]{2,1,0:T(8,128)(2,1)S(1)}, bf16[1,384,256]{2,1,0:T(8,128)(2,1)}, u32[]{:S(2)}) copy-start(bf16[1,384,256]{2,1,0:T(8,128)(2,1)} %copy-done.13) | copy-start | bytes 589828
  153.8 46.8 %collective-permute-start.14 = (bf16[2,384,256]{2,1,0:T(8,128)(2,1)}, bf16[2,384,256]{2,1,0:T(8,128)(2,1)S(1)}, u32[]{:S(2)}, u32[]{:S(2)}) collective-permute-start(bf16[2,384,256]{2,1,0:T(8,128)(2,1)} %collective-permute-done.13), channel_id=1, source_target_pairs={{0,6},{7,7},{10,8},{1,9},{12,10},{3,11},{14,12},{5,13},{8,14},{15,... | collective-permute-start | bytes 1179656 | tf_op jit(solution)/shard_map/ppermute | solution.py:52
  155.2 45.5 %collective-permute-start.20 = (bf16[2,384,256]{2,1,0:T(8,128)(2,1)}, bf16[2,384,256]{2,1,0:T(8,128)(2,1)S(1)}, u32[]{:S(2)}, u32[]{:S(2)}) collective-permute-start(bf16[2,384,256]{2,1,0:T(8,128)(2,1)} %collective-permute-done.19), channel_id=1, source_target_pairs={{6,0},{1,1},{0,2},{11,3},{2,4},{13,5},{4,6},{15,7},{14,8},{9,9},{8... | collective-permute-start | bytes 1179656 | tf_op jit(solution)/shard_map/ppermute | solution.py:52
  169.9 30.8 %collective-permute-start.16 = (bf16[3,384,256]{2,1,0:T(8,128)(2,1)}, bf16[3,384,256]{2,1,0:T(8,128)(2,1)S(1)}, u32[]{:S(2)}, u32[]{:S(2)}) collective-permute-start(bf16[3,384,256]{2,1,0:T(8,128)(2,1)} %collective-permute-done.15), channel_id=1, source_target_pairs={{0,4},{5,5},{2,6},{7,7},{12,8},{1,9},{14,10},{3,11},{8,12},{13,13}... | collective-permute-start | bytes 1769480 | tf_op jit(solution)/shard_map/ppermute | solution.py:52
  172.7 28.0 %collective-permute-start.18 = (bf16[3,384,256]{2,1,0:T(8,128)(2,1)}, bf16[3,384,256]{2,1,0:T(8,128)(2,1)S(1)}, u32[]{:S(2)}, u32[]{:S(2)}) collective-permute-start(bf16[3,384,256]{2,1,0:T(8,128)(2,1)} %collective-permute-done.17), channel_id=1, source_target_pairs={{4,0},{1,1},{6,2},{3,3},{0,4},{13,5},{2,6},{15,7},{12,8},{9,9},{14... | collective-permute-start | bytes 1769480 | tf_op jit(solution)/shard_map/ppermute | solution.py:52
  174.7 19.4 %collective-permute-start.5 = (bf16[4,384,256]{2,1,0:T(8,128)(2,1)}, bf16[4,384,256]{2,1,0:T(8,128)(2,1)S(1)}, u32[]{:S(2)}, u32[]{:S(2)}) collective-permute-start(bf16[4,384,256]{2,1,0:T(8,128)(2,1)} %collective-permute-done.4), channel_id=1, source_target_pairs={{6,0},{9,1},{0,2},{19,3},{2,4},{21,5},{4,6},{23,7},{14,8},{17,9},{... | collective-permute-start | bytes 2359304 | tf_op jit(solution)/shard_map/ppermute | solution.py:52
  192.8 1.3 copy-start.5
  194.1 6.6 %copy-start.17 = (f32[256]{0:T(256)S(1)}, f32[256]{0:T(256)}, u32[]{:S(2)}) copy-start(f32[256]{0:T(256)} %param.17) | copy-start | bytes 3076
  194.1 6.6 %copy-start.18 = (f32[256]{0:T(256)S(1)}, f32[256]{0:T(256)}, u32[]{:S(2)}) copy-start(f32[256]{0:T(256)} %param.18) | copy-start | bytes 3076
  200.7 1.5 copy-start.3
where the time goes:
time: 260 us; the launch traced here: 258 us
  starting transfers between devices  87.6 us (34%)
  Pallas kernels  71.7 us (28%)
  blocking collectives  44.1 us (17%)
  waiting for transfers between devices  38.2 us (15%)
  local copies, waits for them, and re-layouts  14.8 us (6%)
    pallas_call x4, Pallas kernels, row_taps(): pl.pallas_call(functools.partial(taps_body, plan, row_count), grid=(row_c...  46.1 us
    ppermute x8, starting transfers between devices, passed_along(): array = lax.ppermute(array, ('band', 'sample'), second)  45 us
    all_to_all x1, blocking collectives, shards(): lax.all_to_all(outgoing, ('band', 'sample'), split_axis=0, concat_axis=0,...  44.1 us
    ppermute x12, waiting for transfers between devices, passed_along(): array = lax.ppermute(array, ('band', 'sample'), first)  32.6 us
    ppermute x12, starting transfers between devices, passed_along(): array = lax.ppermute(array, ('band', 'sample'), first)  31.5 us
    pallas_call x1, Pallas kernels, own_rows(): pl.pallas_call(own_body, grid=(row_count,), in_specs=[pl.BlockSpec((1, wi...  15.2 us
    ppermute x5, starting transfers between devices, total_over_devices(): lax.ppermute(values, axis, [(i, i ^ step) for i in range(size)])  10.5 us
    pallas_call x2, Pallas kernels, join(): pl.pallas_call(functools.partial(join_body, plan, remainders, tail is not...  10.4 us
  transfers between devices with their start and end apart: 26, of which 8 were waited for; matrix products, arithmetic and copies ran while one was open for 0% of the time, Pallas kernels for 26%

commit v1 on v0

--- a/solution.py
+++ b/solution.py
@@ -10,6 +10,7 @@
 dilation_list = (12, 24, 36)
 pad = 48
 vmem_limit = 48 * 2**20
+small_cost = pl.CostEstimate(flops=1024, bytes_accessed=1024, transcendentals=0)
 levels = 4
 
 
@@ -151,11 +152,7 @@
         out_shape=out_shapes,
         scratch_shapes=[pltpu.VMEM((width + 2 * pad, channels), jnp.bfloat16)],
         compiler_params=pltpu.CompilerParams(vmem_limit_bytes=vmem_limit),
-        cost_estimate=pl.CostEstimate(
-            flops=len(plan) * 6 * row_count * width * channels * depth,
-            bytes_accessed=2 * (row_count * width * channels + len(plan) * 3 * channels * depth),
-            transcendentals=0,
-        ),
+        cost_estimate=small_cost,
     )(features, before, after, *([w_atrous] * len(plan)))
 
 
@@ -217,12 +214,7 @@
         ],
         scratch_shapes=[pltpu.VMEM((width + 2 * pad, channels), jnp.bfloat16)],
         compiler_params=pltpu.CompilerParams(vmem_limit_bytes=vmem_limit),
-        cost_estimate=pl.CostEstimate(
-            flops=20 * row_count * width * channels * depth,
-            bytes_accessed=2 * (row_count * width * channels + 10 * channels * depth)
-            + 16 * row_count * width * depth,
-            transcendentals=0,
-        ),
+        cost_estimate=small_cost,
     )(features, before, after, *([w_atrous] * 3), w_point, w_project, gain, shift_term)
 
 
@@ -304,11 +296,7 @@
         out_specs=block,
         out_shape=jax.ShapeDtypeStruct((row_count, width, depth), out_type),
         compiler_params=pltpu.CompilerParams(vmem_limit_bytes=vmem_limit),
-        cost_estimate=pl.CostEstimate(
-            flops=len(plan) * 2 * row_count * width * depth * depth,
-            bytes_accessed=row_count * width * depth * (8 + 8 * len(plan)),
-            transcendentals=0,
-        ),
+        cost_estimate=small_cost,
     )(*operands)
 
 
@@ -331,7 +319,7 @@
     before, after = neighbours_columns(features)
 
     arrived = {}
-    for calls in (((2, 0),), ((2, 2),), ((1, 0), (1, 2)), ((0, 0), (0, 2))):
+    for calls in (((2, 0),), ((2, 2),), ((1, 0),), ((1, 2),), ((0, 0),), ((0, 2),)):
         pieces = list(row_taps(features, before, after, w_atrous, calls))
         for branch, row_tap in calls:
             band_step, remainder = split_of((row_tap - 1) * dilation_list[branch], row_count)

time: 260 us -> 226 us (0.87)
  starting transfers between devices: 87.6 us -> 74.2 us
  waiting for transfers between devices: 38.2 us -> 25.9 us
  Pallas kernels: 71.7 us -> 60.3 us
    ppermute x12, waiting for transfers between devices: 32.6 us -> 17.9 us  [passed_along(): array = lax.ppermute(array, ('band', 'sample'), first)]
    ppermute x8, starting transfers between devices: 45 us -> 31.8 us  [passed_along(): array = lax.ppermute(array, ('band', 'sample'), second)]
    pallas_call x4 -> x6, Pallas kernels: 46.1 us -> 34.1 us  [row_taps(): pl.pallas_call(functools.partial(taps_body, plan, row_count), grid=(row_c...]
    unnamed x43 -> x53, local copies, waits for them, and re-layouts: 5.6 us -> 6.76 us
  transfers between devices with their start and end apart: 26 -> 26, of which waited for: 8 -> 7; matrix products, arithmetic and copies ran while one was open for 0% -> 3% of each run, Pallas kernels for 26% -> 18%
where the time goes in v1:
time: 226 us; the launch traced here: 224 us
  starting transfers between devices  74.2 us (33%)
  Pallas kernels  60.3 us (27%)
  blocking collectives  41.6 us (18%)
  waiting for transfers between devices  25.9 us (11%)
  local copies, waits for them, and re-layouts  17.3 us (8%)
  other arithmetic  3.13 us (1%)
    all_to_all x1, blocking collectives, shards(): lax.all_to_all(outgoing, ('band', 'sample'), split_axis=0, concat_axis=0,...  41.6 us
    pallas_call x6, Pallas kernels, row_taps(): pl.pallas_call(functools.partial(taps_body, plan, row_count), grid=(row_c...  34.1 us
    ppermute x8, starting transfers between devices, passed_along(): array = lax.ppermute(array, ('band', 'sample'), second)  31.8 us
    ppermute x12, starting transfers between devices, passed_along(): array = lax.ppermute(array, ('band', 'sample'), first)  29.2 us
    ppermute x12, waiting for transfers between devices, passed_along(): array = lax.ppermute(array, ('band', 'sample'), first)  17.9 us
    pallas_call x1, Pallas kernels, own_rows(): pl.pallas_call(own_body, grid=(row_count,), in_specs=[pl.BlockSpec((1, wi...  15.2 us
    ppermute x5, starting transfers between devices, total_over_devices(): lax.ppermute(values, axis, [(i, i ^ step) for i in range(size)])  12.7 us
    pallas_call x2, Pallas kernels, join(): pl.pallas_call(functools.partial(join_body, plan, remainders, tail is not...  11 us
  transfers between devices with their start and end apart: 26, of which 7 were waited for; matrix products, arithmetic and copies ran while one was open for 3% of the time, Pallas kernels for 18%

profile of v1, /device:TPU:0, one launch (start us, length us, event | category | flops | bytes accessed | tf_op | source)
XLA Modules:
  0.0 224.5 jit_solution(10257368078590506158)
XLA Ops:
  0.0 1.4 fusion.11
  2.0 2.2 collective-permute-done
  4.3 5.4 %shard_map.104 = (bf16[1,384,256]{2,1,0:T(8,128)(2,1)S(1)}, bf16[4,384,256]{2,1,0:T(8,128)(2,1)S(1)}) custom-call(bf16[5,384,1024]{2,1,0:T(8,128)(2,1)S(1)} %copy-done.1, bf16[5,48,1024]{2,1,0:T(8,128)(2,1)S(1)} %get-tuple-element.36.before_ref, bf16[5,48,1024]{2,1,0:T(8,128)(2,1)S(1)} %get-tuple-element.35.after_ref, bf16[3,3,3,1024,256]{4,3,2,1,0:T(8,128)(2,1)} %refs_0_.13), custom_call_target="tpu_custom_call" | custom-call | flops 1024 | bytes 1024 | tf_op jit(solution)/shard_map/pallas_call | solution.py:147
  9.7 5.5 %shard_map.101 = (bf16[1,384,256]{2,1,0:T(8,128)(2,1)S(1)}, bf16[4,384,256]{2,1,0:T(8,128)(2,1)S(1)}) custom-call(bf16[5,384,1024]{2,1,0:T(8,128)(2,1)S(1)} %copy-done.1, bf16[5,48,1024]{2,1,0:T(8,128)(2,1)S(1)} %get-tuple-element.36.before_ref, bf16[5,48,1024]{2,1,0:T(8,128)(2,1)S(1)} %get-tuple-element.35.after_ref, bf16[3,3,3,1024,256]{4,3,2,1,0:T(8,128)(2,1)} %refs_0_.13), custom_call_target="tpu_custom_call" | custom-call | flops 1024 | bytes 1024 | tf_op jit(solution)/shard_map/pallas_call | solution.py:147
  15.2 5.5 %shard_map.106 = (bf16[2,384,256]{2,1,0:T(8,128)(2,1)S(1)}, bf16[3,384,256]{2,1,0:T(8,128)(2,1)S(1)}) custom-call(bf16[5,384,1024]{2,1,0:T(8,128)(2,1)S(1)} %copy-done.1, bf16[5,48,1024]{2,1,0:T(8,128)(2,1)S(1)} %get-tuple-element.36.before_ref, bf16[5,48,1024]{2,1,0:T(8,128)(2,1)S(1)} %get-tuple-element.35.after_ref, bf16[3,3,3,1024,256]{4,3,2,1,0:T(8,128)(2,1)} %refs_0_.13), custom_call_target="tpu_custom_call" | custom-call | flops 1024 | bytes 1024 | tf_op jit(solution)/shard_map/pallas_call | solution.py:147
  20.7 1.3 collective-permute-start.11
  22.0 6.7 %collective-permute-start.1 = (bf16[1,384,256]{2,1,0:T(8,128)(2,1)S(1)}, bf16[1,384,256]{2,1,0:T(8,128)(2,1)S(1)}, u32[]{:S(2)}, u32[]{:S(2)}) collective-permute-start(bf16[1,384,256]{2,1,0:T(8,128)(2,1)S(1)} %get-tuple-element.21), channel_id=1, source_target_pairs={{0,16},{1,17},{2,18},{3,19},{4,20},{5,21},{6,22},{7,23},{8,24},{9,... | collective-permute-start | bytes 589832 | tf_op jit(solution)/shard_map/ppermute | solution.py:51
  28.8 1.3 collective-permute-start.10
  31.4 3.3 %collective-permute-start.21 = (f32[1024]{0:T(1024)S(1)}, f32[1024]{0:T(1024)S(1)}, u32[]{:S(2)}, u32[]{:S(2)}) collective-permute-start(f32[1024]{0:T(1024)S(1)} %convert_reduce_fusion), channel_id=1, source_target_pairs={{0,1},{1,0},{2,3},{3,2},{4,5},{5,4},{6,7},{7,6},{8,9},{9,8},{10,11... | collective-permute-start | bytes 12296 | tf_op jit(solution)/shard_map/ppermute | solution.py:65
  34.7 0.8 collective-permute-done.21
  35.5 3.1 %collective-permute-start.22 = (f32[1024]{0:T(1024)S(1)}, f32[1024]{0:T(1024)S(1)}, u32[]{:S(2)}, u32[]{:S(2)}) collective-permute-start(f32[1024]{0:T(1024)S(1)} %add.42), channel_id=1, source_target_pairs={{0,2},{2,0},{4,6},{6,4},{8,10},{10,8},{12,14},{14,12},{16,18},{18,... | collective-permute-start | bytes 12296 | tf_op jit(solution)/shard_map/ppermute | solution.py:65
  38.6 1.7 collective-permute-done.22
  40.3 1.9 collective-permute-start.23
  42.3 1.7 collective-permute-done.23
  43.9 2.0 collective-permute-start.24
  45.9 1.6 collective-permute-done.24
  47.5 2.3 %collective-permute-start.25 = (f32[1024]{0:T(1024)S(1)}, f32[1024]{0:T(1024)S(1)}, u32[]{:S(2)}, u32[]{:S(2)}) collective-permute-start(f32[1024]{0:T(1024)S(1)} %add.45), channel_id=1, source_target_pairs={{0,16},{2,18},{4,20},{6,22},{8,24},{10,26},{12,28},{14,30},{16,0},... | collective-permute-start | bytes 12296 | tf_op jit(solution)/shard_map/ppermute | solution.py:65
  49.9 5.5 %shard_map.102 = (bf16[4,384,256]{2,1,0:T(8,128)(2,1)S(1)}, bf16[1,384,256]{2,1,0:T(8,128)(2,1)S(1)}) custom-call(bf16[5,384,1024]{2,1,0:T(8,128)(2,1)S(1)} %copy-done.1, bf16[5,48,1024]{2,1,0:T(8,128)(2,1)S(1)} %get-tuple-element.36.before_ref, bf16[5,48,1024]{2,1,0:T(8,128)(2,1)S(1)} %get-tuple-element.35.after_ref, bf16[3,3,3,1024,256]{4,3,2,1,0:T(8,128)(2,1)} %refs_0_.13), custom_call_target="tpu_custom_call" | custom-call | flops 1024 | bytes 1024 | tf_op jit(solution)/shard_map/pallas_call | solution.py:147
  55.3 6.1 %shard_map.103 = (bf16[4,384,256]{2,1,0:T(8,128)(2,1)}, bf16[1,384,256]{2,1,0:T(8,128)(2,1)S(1)}) custom-call(bf16[5,384,1024]{2,1,0:T(8,128)(2,1)S(1)} %copy-done.1, bf16[5,48,1024]{2,1,0:T(8,128)(2,1)S(1)} %get-tuple-element.36.before_ref, bf16[5,48,1024]{2,1,0:T(8,128)(2,1)S(1)} %get-tuple-element.35.after_ref, bf16[3,3,3,1024,256]{4,3,2,1,0:T(8,128)(2,1)} %refs_0_.13), custom_call_target="tpu_custom_call" | custom-call | flops 1024 | bytes 1024 | tf_op jit(solution)/shard_map/pallas_call | solution.py:147
  61.5 1.3 collective-permute-start.6
  62.8 2.1 collective-permute-start.9
  64.9 6.2 %shard_map.107 = (bf16[3,384,256]{2,1,0:T(8,128)(2,1)}, bf16[2,384,256]{2,1,0:T(8,128)(2,1)S(1)}) custom-call(bf16[5,384,1024]{2,1,0:T(8,128)(2,1)S(1)} %copy-done.1, bf16[5,48,1024]{2,1,0:T(8,128)(2,1)S(1)} %get-tuple-element.36.before_ref, bf16[5,48,1024]{2,1,0:T(8,128)(2,1)S(1)} %get-tuple-element.35.after_ref, bf16[3,3,3,1024,256]{4,3,2,1,0:T(8,128)(2,1)} %refs_0_.13), custom_call_target="tpu_custom_call" | custom-call | flops 1024 | bytes 1024 | tf_op jit(solution)/shard_map/pallas_call | solution.py:147
  71.8 1.3 collective-permute-start.19
  74.4 6.9 %collective-permute-start.2 = (bf16[4,384,256]{2,1,0:T(8,128)(2,1)S(1)}, bf16[4,384,256]{2,1,0:T(8,128)(2,1)}, u32[]{:S(2)}, u32[]{:S(2)}) collective-permute-start(bf16[4,384,256]{2,1,0:T(8,128)(2,1)S(1)} %get-tuple-element.22), channel_id=1, source_target_pairs={{0,8},{1,7},{2,18},{3,1},{4,20},{5,3},{6,22},{7,5},{8,16},{9,15},{... | collective-permute-start | bytes 2359304 | tf_op jit(solution)/shard_map/ppermute | solution.py:51
  82.0 1.3 collective-permute-start.4
  84.0 4.4 %collective-permute-start.7 = (bf16[4,384,256]{2,1,0:T(8,128)(2,1)}, bf16[4,384,256]{2,1,0:T(8,128)(2,1)}, u32[]{:S(2)}, u32[]{:S(2)}) collective-permute-start(bf16[4,384,256]{2,1,0:T(8,128)(2,1)} %get-tuple-element.25), channel_id=1, source_target_pairs={{0,8},{1,3},{2,10},{3,5},{4,12},{5,7},{6,22},{7,1},{8,16},{9,11},{... | collective-permute-start | bytes 2359304 | tf_op jit(solution)/shard_map/ppermute | solution.py:51
  88.4 4.5 %collective-permute-start.12 = (bf16[4,384,256]{2,1,0:T(8,128)(2,1)}, bf16[4,384,256]{2,1,0:T(8,128)(2,1)S(1)}, u32[]{:S(2)}, u32[]{:S(2)}) collective-permute-start(bf16[4,384,256]{2,1,0:T(8,128)(2,1)} %collective-permute-done.11), channel_id=1, source_target_pairs={{2,0},{9,1},{4,2},{11,3},{6,4},{13,5},{0,6},{23,7},{10,8},{17,9},{... | collective-permute-start | bytes 2359304 | tf_op jit(solution)/shard_map/ppermute | solution.py:53
  92.9 1.3 collective-permute-start.17
  94.2 1.6 collective-permute-start.3
  95.8 17.2 %collective-permute-done.4 = bf16[4,384,256]{2,1,0:T(8,128)(2,1)} collective-permute-done((bf16[4,384,256]{2,1,0:T(8,128)(2,1)S(1)}, bf16[4,384,256]{2,1,0:T(8,128)(2,1)}, u32[]{:S(2)}, u32[]{:S(2)}) %collective-permute-start.4) | collective-permute-done | bytes 786464 | tf_op jit(solution)/shard_map/ppermute | solution.py:51
  113.0 13.4 %collective-permute-start.5 = (bf16[4,384,256]{2,1,0:T(8,128)(2,1)}, bf16[4,384,256]{2,1,0:T(8,128)(2,1)}, u32[]{:S(2)}, u32[]{:S(2)}) collective-permute-start(bf16[4,384,256]{2,1,0:T(8,128)(2,1)} %collective-permute-done.4), channel_id=1, source_target_pairs={{6,0},{9,1},{0,2},{19,3},{2,4},{21,5},{4,6},{23,7},{14,8},{17,9},{... | collective-permute-start | bytes 2359304 | tf_op jit(solution)/shard_map/ppermute | solution.py:53
  126.5 0.8 reshape.59
  127.3 1.6 collective-permute-start.8
  129.4 0.7 copy.11
  130.2 2.0 collective-permute-start.16
  132.2 1.9 collective-permute-start.18
  134.7 4.9 %collective-permute-start.14 = (bf16[2,384,256]{2,1,0:T(8,128)(2,1)}, bf16[2,384,256]{2,1,0:T(8,128)(2,1)}, u32[]{:S(2)}, u32[]{:S(2)}) collective-permute-start(bf16[2,384,256]{2,1,0:T(8,128)(2,1)} %copy-done.24), channel_id=1, source_target_pairs={{0,6},{7,7},{10,8},{1,9},{12,10},{3,11},{14,12},{5,13},{8,14},{15,... | collective-permute-start | bytes 1179656 | tf_op jit(solution)/shard_map/ppermute | solution.py:53
  139.7 1.9 collective-permute-start.20
  142.9 1.6 fusion.4.refs_5_
  144.5 1.0 copy-done.5
  145.5 15.2 %shard_map.100 = (f32[3,5,384,256]{3,2,1,0:T(8,128)}, f32[5,384,256]{2,1,0:T(8,128)S(1)}) custom-call(bf16[5,384,1024]{2,1,0:T(8,128)(2,1)} %x_ref.13, bf16[5,48,1024]{2,1,0:T(8,128)(2,1)S(1)} %get-tuple-element.36.before_ref, bf16[5,48,1024]{2,1,0:T(8,128)(2,1)S(1)} %get-tuple-element.35.after_ref, bf16[3,3,3,1024,256]{4,3,2,1,0:T(8,128)(2,1)} %refs_0_.13, ...), custom_call_target="tpu_custom_call" | custom-call | flops 1024 | bytes 1024 | tf_op jit(solution)/shard_map/pallas_call | solution.py:186
  160.7 1.3 copy-done.4
  162.1 6.7 %shard_map.105.base_ref = f32[5,384,256]{2,1,0:T(8,128)} custom-call(f32[5,384,256]{2,1,0:T(8,128)} %copy-done.4, bf16[1280,256]{1,0:T(8,128)(2,1)S(1)} %copy-done.3, f32[5,256]{1,0:T(8,128)S(1)} %copy-done.14, f32[5,256]{1,0:T(8,128)S(1)} %copy-done.15, f32[3,5,384,256]{3,2,1,0:T(8,128)} %get-tuple-element.20.refs_0_.refs_5_, ...), custom_call_target="tpu_custom_call" | custom-call | flops 1024 | bytes 1024 | tf_op jit(solution)/shard_map/pallas_call | solution.py:292
  168.9 1.5 copy-done.2
  170.5 4.3 %shard_map.108 = bf16[5,384,256]{2,1,0:T(8,128)(2,1)S(1)} custom-call(f32[5,384,256]{2,1,0:T(8,128)S(1)} %copy-done.2, bf16[1280,256]{1,0:T(8,128)(2,1)S(1)} %copy-done.3, f32[5,256]{1,0:T(8,128)S(1)} %copy-done.14, f32[5,256]{1,0:T(8,128)S(1)} %copy-done.15, f32[3,5,384,256]{3,2,1,0:T(8,128)} %get-tuple-element.20.refs_0_.refs_5_, ...), custom_call_target="tpu_custom_call" | custom-call | flops 1024 | bytes 1024 | tf_op jit(solution)/shard_map/pallas_call | solution.py:292
  174.8 6.4 %gather_fusion = bf16[1920,256]{1,0:T(8,128)(2,1)S(1)} fusion(bf16[1920,256]{1,0:T(8,128)(2,1)S(1)} %bitcast.15, s32[2048]{0:T(1024)S(1)} %copy-done.19), kind=kCustom, calls=%fused_computation | custom fusion | bytes 1973760 | tf_op jit(solution)/shard_map/jit(_take)/gather | solution.py:349
  181.8 41.6 %all_to_all.5 = bf16[32,60,256]{2,1,0:T(8,128)(2,1)S(1)} all-to-all(bf16[32,60,256]{2,1,0:T(8,128)(2,1)S(1)} %broadcast_select_fusion), channel_id=1, replica_groups=mesh['band'=16,'sample'=2] {'band','sample'}, dimensions={0} | all-to-all | bytes 1966080 | tf_op jit(solution)/shard_map/all_to_all | solution.py:351
  223.3 1.1 reshape.63
  (86 shorter events, 8.7 us)
Async XLA Ops:
  0.0 142.9 %copy-start = (bf16[1024,256]{1,0:T(8,128)(2,1)S(1)}, bf16[1024,256]{1,0:T(8,128)(2,1)}, u32[]{:S(2)}) copy-start(bf16[1024,256]{1,0:T(8,128)(2,1)} %param.13) | copy-start | bytes 1572868
  0.0 4.3 %copy-start.1 = (bf16[5,384,1024]{2,1,0:T(8,128)(2,1)S(1)}, bf16[5,384,1024]{2,1,0:T(8,128)(2,1)}, u32[]{:S(2)}) copy-start(bf16[5,384,1024]{2,1,0:T(8,128)(2,1)} %x_ref.13) | copy-start | bytes 11796484
  1.5 2.7 %collective-permute-start = (bf16[5,96,1024]{2,1,0:T(8,128)(2,1)S(1)}, bf16[5,96,1024]{2,1,0:T(8,128)(2,1)S(1)}, u32[]{:S(2)}, u32[]{:S(2)}) collective-permute-start(bf16[5,96,1024]{2,1,0:T(8,128)(2,1)S(1)} %pad_maximum_fusion), channel_id=1, source_target_pairs={{0,1},{1,0},{2,3},{3,2},{4,5},{5,4},{6,7},{7,6},{8,9},{9,8},{10,11... | collective-permute-start | bytes 2949128 | tf_op jit(solution)/shard_map/ppermute | solution.py:29
  20.7 67.7 %collective-permute-start.11 = (bf16[4,384,256]{2,1,0:T(8,128)(2,1)S(1)}, bf16[4,384,256]{2,1,0:T(8,128)(2,1)}, u32[]{:S(2)}, u32[]{:S(2)}) collective-permute-start(bf16[4,384,256]{2,1,0:T(8,128)(2,1)S(1)} %get-tuple-element.28), channel_id=1, source_target_pairs={{10,2},{11,9},{12,4},{13,11},{14,6},{15,13},{16,0},{17,23},{18,10}... | collective-permute-start | bytes 2359304 | tf_op jit(solution)/shard_map/ppermute | solution.py:51
  22.0 40.8 %collective-permute-start.1 = (bf16[1,384,256]{2,1,0:T(8,128)(2,1)S(1)}, bf16[1,384,256]{2,1,0:T(8,128)(2,1)S(1)}, u32[]{:S(2)}, u32[]{:S(2)}) collective-permute-start(bf16[1,384,256]{2,1,0:T(8,128)(2,1)S(1)} %get-tuple-element.21), channel_id=1, source_target_pairs={{0,16},{1,17},{2,18},{3,19},{4,20},{5,21},{6,22},{7,23},{8,24},{9,... | collective-permute-start | bytes 589832 | tf_op jit(solution)/shard_map/ppermute | solution.py:51
  28.8 42.3 %collective-permute-start.10 = (bf16[1,384,256]{2,1,0:T(8,128)(2,1)S(1)}, bf16[1,384,256]{2,1,0:T(8,128)(2,1)S(1)}, u32[]{:S(2)}, u32[]{:S(2)}) collective-permute-start(bf16[1,384,256]{2,1,0:T(8,128)(2,1)S(1)} %get-tuple-element.27), channel_id=1, source_target_pairs={{8,0},{9,1},{10,2},{11,3},{12,4},{13,5},{14,6},{15,7},{16,8},{17,9... | collective-permute-start | bytes 589832 | tf_op jit(solution)/shard_map/ppermute | solution.py:51
  30.1 53.2 %collective-permute-start.13 = (bf16[2,384,256]{2,1,0:T(8,128)(2,1)S(1)}, bf16[2,384,256]{2,1,0:T(8,128)(2,1)S(1)}, u32[]{:S(2)}, u32[]{:S(2)}) collective-permute-start(bf16[2,384,256]{2,1,0:T(8,128)(2,1)S(1)} %get-tuple-element.29), channel_id=1, source_target_pairs={{0,0},{1,7},{2,10},{3,1},{4,12},{5,3},{6,14},{7,5},{8,8},{9,15},{1... | collective-permute-start | bytes 1179656 | tf_op jit(solution)/shard_map/ppermute | solution.py:51
  31.4 4.1 %collective-permute-start.21 = (f32[1024]{0:T(1024)S(1)}, f32[1024]{0:T(1024)S(1)}, u32[]{:S(2)}, u32[]{:S(2)}) collective-permute-start(f32[1024]{0:T(1024)S(1)} %convert_reduce_fusion), channel_id=1, source_target_pairs={{0,1},{1,0},{2,3},{3,2},{4,5},{5,4},{6,7},{7,6},{8,9},{9,8},{10,11... | collective-permute-start | bytes 12296 | tf_op jit(solution)/shard_map/ppermute | solution.py:65
  35.5 4.8 %collective-permute-start.22 = (f32[1024]{0:T(1024)S(1)}, f32[1024]{0:T(1024)S(1)}, u32[]{:S(2)}, u32[]{:S(2)}) collective-permute-start(f32[1024]{0:T(1024)S(1)} %add.42), channel_id=1, source_target_pairs={{0,2},{2,0},{4,6},{6,4},{8,10},{10,8},{12,14},{14,12},{16,18},{18,... | collective-permute-start | bytes 12296 | tf_op jit(solution)/shard_map/ppermute | solution.py:65
  40.3 3.6 %collective-permute-start.23 = (f32[1024]{0:T(1024)S(1)}, f32[1024]{0:T(1024)S(1)}, u32[]{:S(2)}, u32[]{:S(2)}) collective-permute-start(f32[1024]{0:T(1024)S(1)} %add.43), channel_id=1, source_target_pairs={{0,4},{2,6},{4,0},{6,2},{8,12},{10,14},{12,8},{14,10},{16,20},{18,... | collective-permute-start | bytes 12296 | tf_op jit(solution)/shard_map/ppermute | solution.py:65
  43.9 3.6 %collective-permute-start.24 = (f32[1024]{0:T(1024)S(1)}, f32[1024]{0:T(1024)S(1)}, u32[]{:S(2)}, u32[]{:S(2)}) collective-permute-start(f32[1024]{0:T(1024)S(1)} %add.44), channel_id=1, source_target_pairs={{0,8},{2,10},{4,12},{6,14},{8,0},{10,2},{12,4},{14,6},{16,24},{18,... | collective-permute-start | bytes 12296 | tf_op jit(solution)/shard_map/ppermute | solution.py:65
  47.5 13.9 %copy-start.21 = (f32[1024]{0:T(1024)}, f32[1024]{0:T(1024)S(1)}, u32[]{:S(2)}) copy-start(f32[1024]{0:T(1024)S(1)} %add.45) | copy-start | bytes 12292
  47.5 13.9 %collective-permute-start.25 = (f32[1024]{0:T(1024)S(1)}, f32[1024]{0:T(1024)S(1)}, u32[]{:S(2)}, u32[]{:S(2)}) collective-permute-start(f32[1024]{0:T(1024)S(1)} %add.45), channel_id=1, source_target_pairs={{0,16},{2,18},{4,20},{6,22},{8,24},{10,26},{12,28},{14,30},{16,0},... | collective-permute-start | bytes 12296 | tf_op jit(solution)/shard_map/ppermute | solution.py:65
  61.5 51.5 %copy-start.22 = (f32[1024]{0:T(1024)}, f32[1024]{0:T(1024)S(1)}, u32[]{:S(2)}) copy-start(f32[1024]{0:T(1024)S(1)} %collective-permute-done.25) | copy-start | bytes 12292
  61.5 12.2 %collective-permute-start.6 = (bf16[1,384,256]{2,1,0:T(8,128)(2,1)S(1)}, bf16[1,384,256]{2,1,0:T(8,128)(2,1)S(1)}, u32[]{:S(2)}, u32[]{:S(2)}) collective-permute-start(bf16[1,384,256]{2,1,0:T(8,128)(2,1)S(1)} %get-tuple-element.24), channel_id=1, source_target_pairs={{16,0},{17,1},{18,2},{19,3},{20,4},{21,5},{22,6},{23,7},{24,8},{25... | collective-permute-start | bytes 589832 | tf_op jit(solution)/shard_map/ppermute | solution.py:51
  62.8 8.3 %copy-start.6 = (bf16[1,384,256]{2,1,0:T(8,128)(2,1)}, bf16[1,384,256]{2,1,0:T(8,128)(2,1)S(1)}, u32[]{:S(2)}) copy-start(bf16[1,384,256]{2,1,0:T(8,128)(2,1)S(1)} %collective-permute-done.1.refs_1_) | copy-start | bytes 589828
  62.8 80.1 %copy-start.3 = (bf16[1280,256]{1,0:T(8,128)(2,1)S(1)}, bf16[1280,256]{1,0:T(8,128)(2,1)}, u32[]{:S(2)}) copy-start(bf16[1280,256]{1,0:T(8,128)(2,1)} %w_project.3) | copy-start | bytes 1966084
  62.8 80.1 %copy-start.14 = (f32[5,256]{1,0:T(8,128)S(1)}, f32[5,256]{1,0:T(8,128)}, u32[]{:S(2)}) copy-start(f32[5,256]{1,0:T(8,128)} %gain.3) | copy-start | bytes 15364
  62.8 80.1 %copy-start.15 = (f32[5,256]{1,0:T(8,128)S(1)}, f32[5,256]{1,0:T(8,128)}, u32[]{:S(2)}) copy-start(f32[5,256]{1,0:T(8,128)} %shift_term.3) | copy-start | bytes 15364
  62.8 18.4 %collective-permute-start.9 = (bf16[1,384,256]{2,1,0:T(8,128)(2,1)S(1)}, bf16[1,384,256]{2,1,0:T(8,128)(2,1)S(1)}, u32[]{:S(2)}, u32[]{:S(2)}) collective-permute-start(bf16[1,384,256]{2,1,0:T(8,128)(2,1)S(1)} %get-tuple-element.26), channel_id=1, source_target_pairs={{0,8},{1,9},{2,10},{3,11},{4,12},{5,13},{6,14},{7,15},{8,16},{9,17... | collective-permute-start | bytes 589832 | tf_op jit(solution)/shard_map/ppermute | solution.py:51
  71.8 12.2 %collective-permute-start.19 = (bf16[2,384,256]{2,1,0:T(8,128)(2,1)S(1)}, bf16[2,384,256]{2,1,0:T(8,128)(2,1)S(1)}, u32[]{:S(2)}, u32[]{:S(2)}) collective-permute-start(bf16[2,384,256]{2,1,0:T(8,128)(2,1)S(1)} %get-tuple-element.32), channel_id=1, source_target_pairs={{6,6},{7,1},{8,0},{9,11},{10,2},{11,13},{12,4},{13,15},{14,14},{15... | collective-permute-start | bytes 1179656 | tf_op jit(solution)/shard_map/ppermute | solution.py:51
  74.4 19.8 %collective-permute-start.2 = (bf16[4,384,256]{2,1,0:T(8,128)(2,1)S(1)}, bf16[4,384,256]{2,1,0:T(8,128)(2,1)}, u32[]{:S(2)}, u32[]{:S(2)}) collective-permute-start(bf16[4,384,256]{2,1,0:T(8,128)(2,1)S(1)} %get-tuple-element.22), channel_id=1, source_target_pairs={{0,8},{1,7},{2,18},{3,1},{4,20},{5,3},{6,22},{7,5},{8,16},{9,15},{... | collective-permute-start | bytes 2359304 | tf_op jit(solution)/shard_map/ppermute | solution.py:51
  82.0 31.0 %collective-permute-start.4 = (bf16[4,384,256]{2,1,0:T(8,128)(2,1)S(1)}, bf16[4,384,256]{2,1,0:T(8,128)(2,1)}, u32[]{:S(2)}, u32[]{:S(2)}) collective-permute-start(bf16[4,384,256]{2,1,0:T(8,128)(2,1)S(1)} %get-tuple-element.23), channel_id=1, source_target_pairs={{14,6},{15,9},{16,0},{17,19},{18,2},{19,21},{20,4},{21,23},{22,14}... | collective-permute-start | bytes 2359304 | tf_op jit(solution)/shard_map/ppermute | solution.py:51
  83.3 29.7 %copy-start.24 = (bf16[2,384,256]{2,1,0:T(8,128)(2,1)}, bf16[2,384,256]{2,1,0:T(8,128)(2,1)S(1)}, u32[]{:S(2)}) copy-start(bf16[2,384,256]{2,1,0:T(8,128)(2,1)S(1)} %collective-permute-done.13) | copy-start | bytes 1179652
  83.3 9.6 %collective-permute-start.15 = (bf16[3,384,256]{2,1,0:T(8,128)(2,1)S(1)}, bf16[3,384,256]{2,1,0:T(8,128)(2,1)S(1)}, u32[]{:S(2)}, u32[]{:S(2)}) collective-permute-start(bf16[3,384,256]{2,1,0:T(8,128)(2,1)S(1)} %get-tuple-element.30), channel_id=1, source_target_pairs={{0,0},{1,5},{2,2},{3,7},{4,12},{5,1},{6,14},{7,3},{8,8},{9,13},{10... | collective-permute-start | bytes 1769480 | tf_op jit(solution)/shard_map/ppermute | solution.py:51
  84.0 29.0 %copy-start.25 = (bf16[2,384,256]{2,1,0:T(8,128)(2,1)}, bf16[2,384,256]{2,1,0:T(8,128)(2,1)S(1)}, u32[]{:S(2)}) copy-start(bf16[2,384,256]{2,1,0:T(8,128)(2,1)S(1)} %collective-permute-done.19) | copy-start | bytes 1179652
  84.0 43.3 %collective-permute-start.7 = (bf16[4,384,256]{2,1,0:T(8,128)(2,1)}, bf16[4,384,256]{2,1,0:T(8,128)(2,1)}, u32[]{:S(2)}, u32[]{:S(2)}) collective-permute-start(bf16[4,384,256]{2,1,0:T(8,128)(2,1)} %get-tuple-element.25), channel_id=1, source_target_pairs={{0,8},{1,3},{2,10},{3,5},{4,12},{5,7},{6,22},{7,1},{8,16},{9,11},{... | collective-permute-start | bytes 2359304 | tf_op jit(solution)/shard_map/ppermute | solution.py:51
  88.4 43.8 %collective-permute-start.12 = (bf16[4,384,256]{2,1,0:T(8,128)(2,1)}, bf16[4,384,256]{2,1,0:T(8,128)(2,1)S(1)}, u32[]{:S(2)}, u32[]{:S(2)}) collective-permute-start(bf16[4,384,256]{2,1,0:T(8,128)(2,1)} %collective-permute-done.11), channel_id=1, source_target_pairs={{2,0},{9,1},{4,2},{11,3},{6,4},{13,5},{0,6},{23,7},{10,8},{17,9},{... | collective-permute-start | bytes 2359304 | tf_op jit(solution)/shard_map/ppermute | solution.py:53
  92.9 20.1 %copy-start.23 = (bf16[3,384,256]{2,1,0:T(8,128)(2,1)}, bf16[3,384,256]{2,1,0:T(8,128)(2,1)S(1)}, u32[]{:S(2)}) copy-start(bf16[3,384,256]{2,1,0:T(8,128)(2,1)S(1)} %collective-permute-done.15) | copy-start | bytes 1769476
  92.9 37.3 %collective-permute-start.17 = (bf16[3,384,256]{2,1,0:T(8,128)(2,1)}, bf16[3,384,256]{2,1,0:T(8,128)(2,1)}, u32[]{:S(2)}, u32[]{:S(2)}) collective-permute-start(bf16[3,384,256]{2,1,0:T(8,128)(2,1)} %get-tuple-element.31), channel_id=1, source_target_pairs={{4,4},{5,1},{6,6},{7,3},{8,0},{9,13},{10,2},{11,15},{12,12},{13,9}... | collective-permute-start | bytes 1769480 | tf_op jit(solution)/shard_map/ppermute | solution.py:51
  94.2 40.5 %collective-permute-start.3 = (bf16[4,384,256]{2,1,0:T(8,128)(2,1)}, bf16[4,384,256]{2,1,0:T(8,128)(2,1)}, u32[]{:S(2)}, u32[]{:S(2)}) collective-permute-start(bf16[4,384,256]{2,1,0:T(8,128)(2,1)} %collective-permute-done.2), channel_id=1, source_target_pairs={{8,14},{7,15},{18,16},{1,17},{20,18},{3,19},{22,20},{5,21},{16,22}... | collective-permute-start | bytes 2359304 | tf_op jit(solution)/shard_map/ppermute | solution.py:53
  113.0 26.7 %collective-permute-start.5 = (bf16[4,384,256]{2,1,0:T(8,128)(2,1)}, bf16[4,384,256]{2,1,0:T(8,128)(2,1)}, u32[]{:S(2)}, u32[]{:S(2)}) collective-permute-start(bf16[4,384,256]{2,1,0:T(8,128)(2,1)} %collective-permute-done.4), channel_id=1, source_target_pairs={{6,0},{9,1},{0,2},{19,3},{2,4},{21,5},{4,6},{23,7},{14,8},{17,9},{... | collective-permute-start | bytes 2359304 | tf_op jit(solution)/shard_map/ppermute | solution.py:53
  127.3 34.8 %collective-permute-start.8 = (bf16[4,384,256]{2,1,0:T(8,128)(2,1)}, bf16[4,384,256]{2,1,0:T(8,128)(2,1)}, u32[]{:S(2)}, u32[]{:S(2)}) collective-permute-start(bf16[4,384,256]{2,1,0:T(8,128)(2,1)} %collective-permute-done.7), channel_id=1, source_target_pairs={{8,10},{3,11},{10,12},{5,13},{12,14},{7,15},{22,16},{1,17},{16,18}... | collective-permute-start | bytes 2359304 | tf_op jit(solution)/shard_map/ppermute | solution.py:53
  130.2 38.7 %collective-permute-start.16 = (bf16[3,384,256]{2,1,0:T(8,128)(2,1)}, bf16[3,384,256]{2,1,0:T(8,128)(2,1)S(1)}, u32[]{:S(2)}, u32[]{:S(2)}) collective-permute-start(bf16[3,384,256]{2,1,0:T(8,128)(2,1)} %copy-done.23), channel_id=1, source_target_pairs={{0,4},{5,5},{2,6},{7,7},{12,8},{1,9},{14,10},{3,11},{8,12},{13,13}... | collective-permute-start | bytes 1769480 | tf_op jit(solution)/shard_map/ppermute | solution.py:53
  132.2 36.7 %collective-permute-start.18 = (bf16[3,384,256]{2,1,0:T(8,128)(2,1)}, bf16[3,384,256]{2,1,0:T(8,128)(2,1)}, u32[]{:S(2)}, u32[]{:S(2)}) collective-permute-start(bf16[3,384,256]{2,1,0:T(8,128)(2,1)} %collective-permute-done.17), channel_id=1, source_target_pairs={{4,0},{1,1},{6,2},{3,3},{0,4},{13,5},{2,6},{15,7},{12,8},{9,9},{14... | collective-permute-start | bytes 1769480 | tf_op jit(solution)/shard_map/ppermute | solution.py:53
  134.7 34.1 %collective-permute-start.14 = (bf16[2,384,256]{2,1,0:T(8,128)(2,1)}, bf16[2,384,256]{2,1,0:T(8,128)(2,1)}, u32[]{:S(2)}, u32[]{:S(2)}) collective-permute-start(bf16[2,384,256]{2,1,0:T(8,128)(2,1)} %copy-done.24), channel_id=1, source_target_pairs={{0,6},{7,7},{10,8},{1,9},{12,10},{3,11},{14,12},{5,13},{8,14},{15,... | collective-permute-start | bytes 1179656 | tf_op jit(solution)/shard_map/ppermute | solution.py:53
  139.7 29.2 %collective-permute-start.20 = (bf16[2,384,256]{2,1,0:T(8,128)(2,1)}, bf16[2,384,256]{2,1,0:T(8,128)(2,1)}, u32[]{:S(2)}, u32[]{:S(2)}) collective-permute-start(bf16[2,384,256]{2,1,0:T(8,128)(2,1)} %copy-done.25), channel_id=1, source_target_pairs={{6,0},{1,1},{0,2},{11,3},{2,4},{13,5},{4,6},{15,7},{14,8},{9,9},{8... | collective-permute-start | bytes 1179656 | tf_op jit(solution)/shard_map/ppermute | solution.py:53
  145.5 16.6 %copy-start.7 = (bf16[1,384,256]{2,1,0:T(8,128)(2,1)S(1)}, bf16[1,384,256]{2,1,0:T(8,128)(2,1)}, u32[]{:S(2)}) copy-start(bf16[1,384,256]{2,1,0:T(8,128)(2,1)} %copy-done.6) | copy-start | bytes 589828
  145.5 16.6 %copy-start.9 = (bf16[1,384,256]{2,1,0:T(8,128)(2,1)S(1)}, bf16[1,384,256]{2,1,0:T(8,128)(2,1)}, u32[]{:S(2)}) copy-start(bf16[1,384,256]{2,1,0:T(8,128)(2,1)} %copy-done.8) | copy-start | bytes 589828
  145.5 16.6 %copy-start.11 = (bf16[1,384,256]{2,1,0:T(8,128)(2,1)S(1)}, bf16[1,384,256]{2,1,0:T(8,128)(2,1)}, u32[]{:S(2)}) copy-start(bf16[1,384,256]{2,1,0:T(8,128)(2,1)} %copy-done.10) | copy-start | bytes 589828
  145.5 16.6 %copy-start.13 = (bf16[1,384,256]{2,1,0:T(8,128)(2,1)S(1)}, bf16[1,384,256]{2,1,0:T(8,128)(2,1)}, u32[]{:S(2)}) copy-start(bf16[1,384,256]{2,1,0:T(8,128)(2,1)} %copy-done.12) | copy-start | bytes 589828
  160.7 1.3 copy-start.4
  162.1 6.8 %copy-start.16 = (f32[1,256]{1,0:T(1,128)S(1)}, f32[1,256]{1,0:T(1,128)}, u32[]{:S(2)}) copy-start(f32[1,256]{1,0:T(1,128)} %fusion.4.refs_5_) | copy-start | bytes 3076
  162.1 6.8 %copy-start.17 = (f32[256]{0:T(256)S(1)}, f32[256]{0:T(256)}, u32[]{:S(2)}) copy-start(f32[256]{0:T(256)} %param.17) | copy-start | bytes 3076
  162.1 6.8 %copy-start.18 = (f32[256]{0:T(256)S(1)}, f32[256]{0:T(256)}, u32[]{:S(2)}) copy-start(f32[256]{0:T(256)} %param.18) | copy-start | bytes 3076
  168.9 1.5 copy-start.2
  170.5 4.3 %copy-start.19 = (s32[2048]{0:T(1024)S(1)}, s32[2048]{0:T(1024)}, u32[]{:S(2)}) copy-start(s32[2048]{0:T(1024)} %pad_clamp_fusion) | copy-start | bytes 24580
  174.8 6.6 %copy-start.20 = (pred[32,60]{1,0:T(8,128)(4,1)S(1)}, pred[32,60]{1,0:T(8,128)(4,1)}, u32[]{:S(2)}) copy-start(pred[32,60]{1,0:T(8,128)(4,1)} %compare_and_fusion) | copy-start | bytes 5764
  (4 other events, 3.1 us)

commit v2 on v1

--- a/solution.py
+++ b/solution.py
@@ -9,8 +9,10 @@
 
 dilation_list = (12, 24, 36)
 pad = 48
-vmem_limit = 48 * 2**20
+vmem_limit = 24 * 2**20
+wide_limit = 56 * 2**20
 small_cost = pl.CostEstimate(flops=1024, bytes_accessed=1024, transcendentals=0)
+routes = {5: "within", 2: "split"}
 levels = 4
 
 
@@ -35,6 +37,9 @@
     band_count = lax.axis_size("band")
     half_count = lax.axis_size("sample")
     level = max(band_count // levels, 1)
+    route = routes.get(abs(by), "direct")
+    if by % level == 0:
+        route = "direct"
     first, second = [], []
     for band in range(band_count):
         goal = band + by
@@ -43,28 +48,37 @@
         along = goal // level * level + band % level
         within = band // level * level + goal % level
         for half in range(half_count):
-            middle = along if half % 2 == 0 or by % level == 0 else within
+            if route == "direct":
+                middle = goal
+            elif route == "within" or half % 2:
+                middle = within
+            else:
+                middle = along
             first.append((band * half_count + half, middle * half_count + half))
             second.append((middle * half_count + half, goal * half_count + half))
     if not first:
-        return jnp.zeros_like(array)
+        return jnp.zeros_like(array), array
     array = lax.ppermute(array, ("band", "sample"), first)
-    if by % level != 0:
+    part_way = array
+    if route != "direct":
         array = lax.ppermute(array, ("band", "sample"), second)
-    return array
+    return array, part_way
 
 
 def total_over_devices(values):
+    steps = []
     for axis in ("sample", "band"):
         size = lax.axis_size(axis)
         if size & (size - 1):
             values = lax.psum(values, axis)
+            steps.append(values)
             continue
         step = 1
         while step < size:
             values = values + lax.ppermute(values, axis, [(i, i ^ step) for i in range(size)])
+            steps.append(values)
             step *= 2
-    return values
+    return values, steps
 
 
 def split_of(offset, row_count):
@@ -72,9 +86,9 @@
     return band_step, offset - band_step * row_count
 
 
-def taps_body(plan, row_count, x_ref, before_ref, after_ref, *refs):
+def taps_body(plan, row_count, token_count, x_ref, before_ref, after_ref, *refs):
     weights = refs[: len(plan)]
-    outs = refs[len(plan) : -1]
+    outs = refs[len(plan) + token_count : -1]
     wide = refs[-1]
     width = x_ref.shape[1]
     row = pl.program_id(0)
@@ -112,7 +126,7 @@
             near[0] = summed
 
 
-def row_taps(features, before, after, w_atrous, plan):
+def row_taps(features, before, after, w_atrous, plan, tokens=()):
     row_count, width, channels = features.shape
     depth = w_atrous.shape[-1]
     in_specs = [
@@ -145,77 +159,92 @@
             )
             out_shapes.append(jax.ShapeDtypeStruct((remainder, width, depth), jnp.bfloat16))
     return pl.pallas_call(
-        functools.partial(taps_body, plan, row_count),
+        functools.partial(taps_body, plan, row_count, len(tokens)),
         grid=(row_count,),
-        in_specs=in_specs,
+        in_specs=in_specs + [pl.BlockSpec(memory_space=pl.ANY)] * len(tokens),
         out_specs=out_specs,
         out_shape=out_shapes,
         scratch_shapes=[pltpu.VMEM((width + 2 * pad, channels), jnp.bfloat16)],
         compiler_params=pltpu.CompilerParams(vmem_limit_bytes=vmem_limit),
         cost_estimate=small_cost,
-    )(features, before, after, *([w_atrous] * len(plan)))
-
-
-def own_body(x_ref, before_ref, after_ref, *refs):
-    w_atrous = refs[:3]
-    w_point, w_project, gain, shift_term, centre_ref, base_ref, wide = refs[3:]
+    )(features, before, after, *([w_atrous] * len(plan)), *tokens)
+
+
+def own_body(plan, with_point, token_count, x_ref, before_ref, after_ref, *refs):
+    weights = refs[: len(plan)]
+    place = len(plan)
+    if with_point:
+        w_point, w_project, gain, shift_term = refs[place : place + 4]
+        place += 4
+    place += token_count
+    centres = refs[place : place + len(plan)]
+    extra_ref, wide = refs[place + len(plan) :]
     width = x_ref.shape[1]
     wide[0:pad] = before_ref[0]
     wide[pad : pad + width] = x_ref[0]
     wide[pad + width :] = after_ref[0]
-    for branch, dilation in enumerate(dilation_list):
+    for branch, w_ref, centre_ref in zip(plan, weights, centres):
+        dilation = dilation_list[branch]
         summed = None
         for column_tap in range(3):
             start = pad + (column_tap - 1) * dilation
             term = jnp.dot(
                 wide[start : start + width],
-                w_atrous[branch][0, 0, column_tap],
+                w_ref[0, 0, column_tap],
                 preferred_element_type=jnp.float32,
             )
             summed = term if summed is None else summed + term
-        centre_ref[branch, 0] = summed
-    point = jnp.dot(x_ref[0], w_point[...], preferred_element_type=jnp.float32)
-    point = activate(point, gain[0:1], shift_term[0:1])
-    base_ref[0] = jnp.dot(point, w_project[...], preferred_element_type=jnp.float32)
-
-
-def own_rows(features, before, after, w_atrous, w_point, w_project, gain, shift_term):
+        centre_ref[0] = summed
+    if with_point:
+        point = jnp.dot(x_ref[0], w_point[...], preferred_element_type=jnp.float32)
+        point = activate(point, gain[0:1], shift_term[0:1])
+        extra_ref[0] = jnp.dot(point, w_project[...], preferred_element_type=jnp.float32)
+
+
+def own_rows(features, before, after, w_atrous, plan, point_operands=None, tokens=()):
     row_count, width, channels = features.shape
     depth = w_atrous.shape[-1]
     whole = lambda array: pl.BlockSpec(array.shape, lambda r: (0,) * array.ndim)
-    return pl.pallas_call(
-        own_body,
-        grid=(row_count,),
-        in_specs=[
-            pl.BlockSpec((1, width, channels), lambda r: (r, 0, 0)),
-            pl.BlockSpec((1, pad, channels), lambda r: (r, 0, 0)),
-            pl.BlockSpec((1, pad, channels), lambda r: (r, 0, 0)),
-        ]
-        + [
+    operands = [features, before, after] + [w_atrous] * len(plan)
+    in_specs = [
+        pl.BlockSpec((1, width, channels), lambda r: (r, 0, 0)),
+        pl.BlockSpec((1, pad, channels), lambda r: (r, 0, 0)),
+        pl.BlockSpec((1, pad, channels), lambda r: (r, 0, 0)),
+    ]
+    for branch in plan:
+        in_specs.append(
             pl.BlockSpec(
                 (1, 1, 3, channels, depth),
                 functools.partial(lambda branch, r: (branch, 1, 0, 0, 0), branch),
             )
-            for branch in range(3)
-        ]
-        + [
+        )
+    row_block = pl.BlockSpec((1, width, depth), lambda r: (r, 0, 0))
+    row_type = jax.ShapeDtypeStruct((row_count, width, depth), jnp.float32)
+    if point_operands is not None:
+        w_point, w_project, gain, shift_term = point_operands
+        operands += [w_point, w_project, gain, shift_term]
+        in_specs += [
             whole(w_point),
             pl.BlockSpec((depth, depth), lambda r: (0, 0)),
             whole(gain),
             whole(shift_term),
-        ],
-        out_specs=[
-            pl.BlockSpec((3, 1, width, depth), lambda r: (0, r, 0, 0)),
-            pl.BlockSpec((1, width, depth), lambda r: (r, 0, 0)),
-        ],
-        out_shape=[
-            jax.ShapeDtypeStruct((3, row_count, width, depth), jnp.float32),
-            jax.ShapeDtypeStruct((row_count, width, depth), jnp.float32),
-        ],
+        ]
+        extra_spec, extra_type = row_block, row_type
+    else:
+        extra_spec = pl.BlockSpec((1, channels), lambda r: (0, 0))
+        extra_type = jax.ShapeDtypeStruct((1, channels), jnp.float32)
+    operands += list(tokens)
+    in_specs += [pl.BlockSpec(memory_space=pl.ANY)] * len(tokens)
+    return pl.pallas_call(
+        functools.partial(own_body, plan, point_operands is not None, len(tokens)),
+        grid=(row_count,),
+        in_specs=in_specs,
+        out_specs=[row_block] * len(plan) + [extra_spec],
+        out_shape=[row_type] * len(plan) + [extra_type],
         scratch_shapes=[pltpu.VMEM((width + 2 * pad, channels), jnp.bfloat16)],
-        compiler_params=pltpu.CompilerParams(vmem_limit_bytes=vmem_limit),
+        compiler_params=pltpu.CompilerParams(vmem_limit_bytes=wide_limit),
         cost_estimate=small_cost,
-    )(features, before, after, *([w_atrous] * 3), w_point, w_project, gain, shift_term)
+    )(*operands)
 
 
 def join_body(plan, remainders, last, base_ref, w_project, gain, shift_term, *refs):
@@ -223,7 +252,7 @@
     total = base_ref[0]
     place = 0
     for branch in plan:
-        summed = refs[place][0, 0]
+        summed = refs[place][0]
         place += 1
         for row_tap in (0, 2):
             remainder = remainders[branch, row_tap]
@@ -257,13 +286,8 @@
     in_specs = [block, whole(w_project), whole(gain), whole(shift_term)]
     remainders = {}
     for branch in plan:
-        operands.append(centre)
-        in_specs.append(
-            pl.BlockSpec(
-                (1, 1, width, depth),
-                functools.partial(lambda branch, r: (branch, r, 0, 0), branch),
-            )
-        )
+        operands.append(centre[branch])
+        in_specs.append(block)
         for row_tap in (0, 2):
             _, remainder = split_of((row_tap - 1) * dilation_list[branch], row_count)
             remainders[branch, row_tap] = remainder
@@ -295,7 +319,7 @@
         in_specs=in_specs,
         out_specs=block,
         out_shape=jax.ShapeDtypeStruct((row_count, width, depth), out_type),
-        compiler_params=pltpu.CompilerParams(vmem_limit_bytes=vmem_limit),
+        compiler_params=pltpu.CompilerParams(vmem_limit_bytes=wide_limit),
         cost_estimate=small_cost,
     )(*operands)
 
@@ -318,17 +342,31 @@
     device_count = band_count * half_count
     before, after = neighbours_columns(features)
 
-    arrived = {}
-    for calls in (((2, 0),), ((2, 2),), ((1, 0),), ((1, 2),), ((0, 0),), ((0, 2),)):
-        pieces = list(row_taps(features, before, after, w_atrous, calls))
-        for branch, row_tap in calls:
-            band_step, remainder = split_of((row_tap - 1) * dilation_list[branch], row_count)
-            near = passed_along(pieces.pop(0), -band_step)
-            far = passed_along(pieces.pop(0), -band_step - 1) if remainder else None
-            arrived[branch, row_tap] = (near, far)
-
-    local_totals = jnp.sum(features, axis=(0, 1), dtype=jnp.float32)
-    totals = total_over_devices(local_totals)
+    arrived, part_way = {}, {}
+
+    def send(branch, row_tap, tokens=()):
+        near, *far = row_taps(features, before, after, w_atrous, ((branch, row_tap),), tokens)
+        band_step, remainder = split_of((row_tap - 1) * dilation_list[branch], row_count)
+        near, near_way = passed_along(near, -band_step)
+        far, far_way = passed_along(far[0], -band_step - 1) if far else (None, near_way)
+        arrived[branch, row_tap] = (near, far)
+        ways = (near_way, far_way) if near_way.shape[0] < far_way.shape[0] else (far_way, near_way)
+        part_way[branch, row_tap] = ways
+
+    totals, steps = total_over_devices(jnp.sum(features, axis=(0, 1), dtype=jnp.float32))
+    order = ((2, 0), (2, 2), (1, 0), (1, 2), (0, 0), (0, 2))
+    for place, (branch, row_tap) in enumerate(order):
+        send(branch, row_tap, steps[place - 1 : place] if place else ())
+    centre = {}
+    centre[2], centre[1], centre[0], base = own_rows(
+        features,
+        before,
+        after,
+        w_atrous,
+        (2, 1, 0),
+        (w_point, w_project, branch_gain, branch_bias),
+        [part_way[2, 0][1]],
+    )
     pooled = totals / (row_count * band_count * width_local * half_count)
     pool_input = pooled.astype(jnp.bfloat16)
     pool_value = jnp.dot(pool_input[None, :], w_pool, preferred_element_type=jnp.float32)
@@ -336,9 +374,6 @@
     depth = w_project.shape[-1]
     pool_projected = jnp.dot(pool_branch, w_project[4 * depth :], preferred_element_type=jnp.float32)
 
-    centre, base = own_rows(
-        features, before, after, w_atrous, w_point, w_project, branch_gain, branch_bias
-    )
     base = join((2, 1), base, centre, arrived, w_project, branch_gain, branch_bias)
     tail = (pool_projected, project_gain[None, :], project_bias[None, :])
     projected = join((0,), base, centre, arrived, w_project, branch_gain, branch_bias, tail)

time: 226 us -> 213 us (0.942)
  starting transfers between devices: 74.2 us -> 91.8 us
  waiting for transfers between devices: 25.9 us -> 13.9 us
  blocking collectives: 41.6 us -> 31 us
  Pallas kernels: 60.3 us -> 54.2 us
    ppermute x12, starting transfers between devices: 29.2 us -> 57.9 us  [passed_along(): array = lax.ppermute(array, ('band', 'sample'), first)]
    all_to_all x1, blocking collectives: 41.6 us -> 31 us  [shards(): lax.all_to_all(outgoing, ('band', 'sample'), split_axis=0, concat_axis=0,...]
    ppermute x12, waiting for transfers between devices: 17.9 us -> 8.35 us  [passed_along(): array = lax.ppermute(array, ('band', 'sample'), first)]
    ppermute x8 -> x4, starting transfers between devices: 31.8 us -> 22.9 us  [passed_along(): array = lax.ppermute(array, ('band', 'sample'), second)]
    pallas_call x7, Pallas kernels: 49.3 us -> 40.6 us  [the longest x6 25.2 us: row_taps(): pl.pallas_call(functools.partial(taps_body, plan, row_count, len(tokens))...]
    pallas_call x2, Pallas kernels: 11 us -> 13.6 us  [join(): pl.pallas_call(functools.partial(join_body, plan, remainders, tail is not...]
    unnamed x53 -> x37, local copies, waits for them, and re-layouts: 6.76 us -> 8.43 us
  transfers between devices with their start and end apart: 26 -> 22, of which waited for: 7 -> 5; matrix products, arithmetic and copies ran while one was open for 3% -> 1% of each run, Pallas kernels for 18% -> 23%
where the time goes in v2:
time: 213 us; the launch traced here: 212 us
  starting transfers between devices  91.8 us (43%)
  Pallas kernels  54.2 us (25%)
  blocking collectives  31 us (15%)
  local copies, waits for them, and re-layouts  17.5 us (8%)
  waiting for transfers between devices  13.9 us (7%)
    ppermute x12, starting transfers between devices, passed_along(): array = lax.ppermute(array, ('band', 'sample'), first)  57.9 us
    all_to_all x1, blocking collectives, shards(): lax.all_to_all(outgoing, ('band', 'sample'), split_axis=0, concat_axis=0,...  31 us
    pallas_call x6, Pallas kernels, row_taps(): pl.pallas_call(functools.partial(taps_body, plan, row_count, len(tokens))...  25.2 us
    ppermute x4, starting transfers between devices, passed_along(): array = lax.ppermute(array, ('band', 'sample'), second)  22.9 us
    pallas_call x1, Pallas kernels, own_rows(): pl.pallas_call(functools.partial(own_body, plan, point_operands is not No...  15.4 us
    pallas_call x2, Pallas kernels, join(): pl.pallas_call(functools.partial(join_body, plan, remainders, tail is not...  13.6 us
    ppermute x5, starting transfers between devices, total_over_devices(): lax.ppermute(values, axis, [(i, i ^ step) for i in range(size)])  10.5 us
    unnamed x37, local copies, waits for them, and re-layouts  8.43 us
  transfers between devices with their start and end apart: 22, of which 5 were waited for; matrix products, arithmetic and copies ran while one was open for 1% of the time, Pallas kernels for 23%

profile of v2, /device:TPU:0, one launch (start us, length us, event | category | flops | bytes accessed | tf_op | source)
XLA Modules:
  0.0 212.0 jit_solution(4266003169751296253)
XLA Ops:
  0.0 1.4 fusion.11
  1.5 0.5 collective-permute-start
  2.0 0.5 copy-done.2
  2.5 0.7 convert_reduce_fusion
  3.2 0.5 collective-permute-start.3
  3.7 0.8 collective-permute-done.3
  4.5 2.8 %collective-permute-start.6 = (f32[1024]{0:T(1024)S(1)}, f32[1024]{0:T(1024)S(1)}, u32[]{:S(2)}, u32[]{:S(2)}) collective-permute-start(f32[1024]{0:T(1024)S(1)} %add.42.refs_1_), channel_id=1, source_target_pairs={{0,2},{2,0},{4,6},{6,4},{8,10},{10,8},{12,14},{14,12},{16,18},{18,... | collective-permute-start | bytes 12296 | tf_op jit(solution)/shard_map/ppermute | solution.py:78
  7.3 1.6 collective-permute-done.6
  8.9 2.1 collective-permute-start.10
  11.0 1.6 collective-permute-done.10
  12.6 2.1 collective-permute-start.14
  14.6 1.6 collective-permute-done.14
  16.2 3.0 %collective-permute-start.18 = (f32[1024]{0:T(1024)S(1)}, f32[1024]{0:T(1024)S(1)}, u32[]{:S(2)}, u32[]{:S(2)}) collective-permute-start(f32[1024]{0:T(1024)S(1)} %add.45.refs_1_), channel_id=1, source_target_pairs={{0,16},{2,18},{4,20},{6,22},{8,24},{10,26},{12,28},{14,30},{16,0},... | collective-permute-start | bytes 12296 | tf_op jit(solution)/shard_map/ppermute | solution.py:78
  19.4 5.4 %copy-done.1 = bf16[3,3,3,1024,256]{4,3,2,1,0:T(8,128)(2,1)S(1)} copy-done((bf16[3,3,3,1024,256]{4,3,2,1,0:T(8,128)(2,1)S(1)}, bf16[3,3,3,1024,256]{4,3,2,1,0:T(8,128)(2,1)}, u32[]{:S(2)}) %copy-start.1) | copy-done | bytes 14155800
  24.7 4.0 %shard_map.104 = (bf16[1,384,256]{2,1,0:T(8,128)(2,1)S(1)}, bf16[4,384,256]{2,1,0:T(8,128)(2,1)S(1)}) custom-call(bf16[5,384,1024]{2,1,0:T(8,128)(2,1)S(1)} %copy-done.2, bf16[5,48,1024]{2,1,0:T(8,128)(2,1)S(1)} %get-tuple-element.42.before_ref, bf16[5,48,1024]{2,1,0:T(8,128)(2,1)S(1)} %get-tuple-element.41.after_ref, ...), custom_call_target="tpu_custom_call" | custom-call | flops 1024 | bytes 1024 | tf_op jit(solution)/shard_map/pallas_call | solution.py:161
  28.7 1.6 collective-permute-start.12
  30.3 4.1 %shard_map.107 = (bf16[3,384,256]{2,1,0:T(8,128)(2,1)S(1)}, bf16[2,384,256]{2,1,0:T(8,128)(2,1)S(1)}) custom-call(bf16[5,384,1024]{2,1,0:T(8,128)(2,1)S(1)} %copy-done.2, bf16[5,48,1024]{2,1,0:T(8,128)(2,1)S(1)} %get-tuple-element.42.before_ref, bf16[5,48,1024]{2,1,0:T(8,128)(2,1)S(1)} %get-tuple-element.41.after_ref, ...), custom_call_target="tpu_custom_call" | custom-call | flops 1024 | bytes 1024 | tf_op jit(solution)/shard_map/pallas_call | solution.py:161
  34.5 1.3 collective-permute-start.19
  35.8 1.3 collective-permute-start.11
  37.1 4.0 %shard_map.103 = (bf16[4,384,256]{2,1,0:T(8,128)(2,1)S(1)}, bf16[1,384,256]{2,1,0:T(8,128)(2,1)S(1)}) custom-call(bf16[5,384,1024]{2,1,0:T(8,128)(2,1)S(1)} %copy-done.2, bf16[5,48,1024]{2,1,0:T(8,128)(2,1)S(1)} %get-tuple-element.42.before_ref, bf16[5,48,1024]{2,1,0:T(8,128)(2,1)S(1)} %get-tuple-element.41.after_ref, ...), custom_call_target="tpu_custom_call" | custom-call | flops 1024 | bytes 1024 | tf_op jit(solution)/shard_map/pallas_call | solution.py:161
  41.1 5.2 %collective-permute-start.9 = (bf16[1,384,256]{2,1,0:T(8,128)(2,1)S(1)}, bf16[1,384,256]{2,1,0:T(8,128)(2,1)S(1)}, u32[]{:S(2)}, u32[]{:S(2)}) collective-permute-start(bf16[1,384,256]{2,1,0:T(8,128)(2,1)S(1)} %get-tuple-element.29), channel_id=1, source_target_pairs={{0,8},{1,9},{2,10},{3,11},{4,12},{5,13},{6,14},{7,15},{8,16},{9,17... | collective-permute-start | bytes 589832 | tf_op jit(solution)/shard_map/ppermute | solution.py:61
  46.3 4.1 %shard_map.102 = (bf16[4,384,256]{2,1,0:T(8,128)(2,1)S(1)}, bf16[1,384,256]{2,1,0:T(8,128)(2,1)S(1)}) custom-call(bf16[5,384,1024]{2,1,0:T(8,128)(2,1)S(1)} %copy-done.2, bf16[5,48,1024]{2,1,0:T(8,128)(2,1)S(1)} %get-tuple-element.42.before_ref, bf16[5,48,1024]{2,1,0:T(8,128)(2,1)S(1)} %get-tuple-element.41.after_ref, ...), custom_call_target="tpu_custom_call" | custom-call | flops 1024 | bytes 1024 | tf_op jit(solution)/shard_map/pallas_call | solution.py:161
  50.4 1.3 collective-permute-start.5
  51.7 3.9 %collective-permute-start.7 = (bf16[4,384,256]{2,1,0:T(8,128)(2,1)S(1)}, bf16[4,384,256]{2,1,0:T(8,128)(2,1)}, u32[]{:S(2)}, u32[]{:S(2)}) collective-permute-start(bf16[4,384,256]{2,1,0:T(8,128)(2,1)S(1)} %get-tuple-element.28), channel_id=1, source_target_pairs={{0,2},{1,3},{2,4},{3,5},{4,6},{5,7},{6,0},{7,1},{8,10},{9,11},{10,... | collective-permute-start | bytes 2359304 | tf_op jit(solution)/shard_map/ppermute | solution.py:61
  55.6 4.1 %shard_map.100 = (bf16[1,384,256]{2,1,0:T(8,128)(2,1)S(1)}, bf16[4,384,256]{2,1,0:T(8,128)(2,1)S(1)}) custom-call(bf16[5,384,1024]{2,1,0:T(8,128)(2,1)S(1)} %copy-done.2, bf16[5,48,1024]{2,1,0:T(8,128)(2,1)S(1)} %get-tuple-element.42.before_ref, bf16[5,48,1024]{2,1,0:T(8,128)(2,1)S(1)} %get-tuple-element.41.after_ref, bf16[3,3,3,1024,256]{4,3,2,1,0:T(8,128)(2,1)S(1)} %copy-done.1), custom_call_target="tpu_custom_call" | custom-call | flops 1024 | bytes 1024 | tf_op jit(solution)/shard_map/pallas_call | solution.py:161
  59.7 6.3 %collective-permute-start.2 = (bf16[1,384,256]{2,1,0:T(8,128)(2,1)S(1)}, bf16[1,384,256]{2,1,0:T(8,128)(2,1)S(1)}, u32[]{:S(2)}, u32[]{:S(2)}) collective-permute-start(bf16[1,384,256]{2,1,0:T(8,128)(2,1)S(1)} %get-tuple-element.24), channel_id=1, source_target_pairs={{0,16},{1,17},{2,18},{3,19},{4,20},{5,21},{6,22},{7,23},{8,24},{9,... | collective-permute-start | bytes 589832 | tf_op jit(solution)/shard_map/ppermute | solution.py:61
  66.1 0.7 copy-done.12
  66.8 2.9 %collective-permute-start.1 = (bf16[4,384,256]{2,1,0:T(8,128)(2,1)S(1)}, bf16[4,384,256]{2,1,0:T(8,128)(2,1)S(1)}, u32[]{:S(2)}, u32[]{:S(2)}) collective-permute-start(bf16[4,384,256]{2,1,0:T(8,128)(2,1)S(1)} %get-tuple-element.21), channel_id=1, source_target_pairs={{0,14},{1,15},{2,16},{3,17},{4,18},{5,19},{6,20},{7,21},{8,22},{9,... | collective-permute-start | bytes 2359304 | tf_op jit(solution)/shard_map/ppermute | solution.py:61
  69.7 4.9 %shard_map.106 = (bf16[2,384,256]{2,1,0:T(8,128)(2,1)S(1)}, bf16[3,384,256]{2,1,0:T(8,128)(2,1)}) custom-call(bf16[5,384,1024]{2,1,0:T(8,128)(2,1)S(1)} %copy-done.2, bf16[5,48,1024]{2,1,0:T(8,128)(2,1)S(1)} %get-tuple-element.42.before_ref, bf16[5,48,1024]{2,1,0:T(8,128)(2,1)S(1)} %get-tuple-element.41.after_ref, ...), custom_call_target="tpu_custom_call" | custom-call | flops 1024 | bytes 1024 | tf_op jit(solution)/shard_map/pallas_call | solution.py:161
  74.5 0.8 copy-done.5
  75.3 6.0 %collective-permute-start.16 = (bf16[3,384,256]{2,1,0:T(8,128)(2,1)}, bf16[3,384,256]{2,1,0:T(8,128)(2,1)}, u32[]{:S(2)}, u32[]{:S(2)}) collective-permute-start(bf16[3,384,256]{2,1,0:T(8,128)(2,1)} %get-tuple-element.34), channel_id=1, source_target_pairs={{0,0},{1,5},{2,2},{3,7},{4,12},{5,1},{6,14},{7,3},{8,8},{9,13},{10... | collective-permute-start | bytes 1769480 | tf_op jit(solution)/shard_map/ppermute | solution.py:61
  81.3 1.3 collective-permute-start.4
  82.6 1.3 collective-permute-start.13
  83.9 6.8 %collective-permute-start.8 = (bf16[4,384,256]{2,1,0:T(8,128)(2,1)}, bf16[4,384,256]{2,1,0:T(8,128)(2,1)}, u32[]{:S(2)}, u32[]{:S(2)}) collective-permute-start(bf16[4,384,256]{2,1,0:T(8,128)(2,1)} %collective-permute-done.7), channel_id=1, source_target_pairs={{2,10},{3,11},{4,12},{5,13},{6,14},{7,15},{0,16},{1,17},{10,18},{1... | collective-permute-start | bytes 2359304 | tf_op jit(solution)/shard_map/ppermute | solution.py:64
  90.8 12.9 %collective-permute-start.20 = (bf16[3,384,256]{2,1,0:T(8,128)(2,1)}, bf16[3,384,256]{2,1,0:T(8,128)(2,1)}, u32[]{:S(2)}, u32[]{:S(2)}) collective-permute-start(bf16[3,384,256]{2,1,0:T(8,128)(2,1)} %copy-done.17), channel_id=1, source_target_pairs={{4,0},{1,1},{6,2},{3,3},{0,4},{13,5},{2,6},{15,7},{12,8},{9,9},{14... | collective-permute-start | bytes 1769480 | tf_op jit(solution)/shard_map/ppermute | solution.py:64
  103.7 2.0 collective-permute-start.17
  105.7 8.3 %collective-permute-done.4.refs_3_ = bf16[4,384,256]{2,1,0:T(8,128)(2,1)} collective-permute-done((bf16[4,384,256]{2,1,0:T(8,128)(2,1)S(1)}, bf16[4,384,256]{2,1,0:T(8,128)(2,1)}, u32[]{:S(2)}, u32[]{:S(2)}) %collective-permute-start.4) | collective-permute-done | bytes 786464 | tf_op jit(solution)/shard_map/ppermute | solution.py:61
  114.0 1.3 collective-permute-start.21
  115.3 25.7 %collective-permute-start.15 = (bf16[2,384,256]{2,1,0:T(8,128)(2,1)}, bf16[2,384,256]{2,1,0:T(8,128)(2,1)S(1)}, u32[]{:S(2)}, u32[]{:S(2)}) collective-permute-start(bf16[2,384,256]{2,1,0:T(8,128)(2,1)} %copy-done.5), channel_id=1, source_target_pairs={{0,6},{1,7},{2,8},{3,9},{4,10},{5,11},{6,12},{7,13},{8,14},{9,15},... | collective-permute-start | bytes 1179656 | tf_op jit(solution)/shard_map/ppermute | solution.py:61
  141.1 1.8 fusion.4.refs_5_
  142.8 15.4 %shard_map.101 = (f32[5,384,256]{2,1,0:T(8,128)}, f32[5,384,256]{2,1,0:T(8,128)}, f32[5,384,256]{2,1,0:T(8,128)}, f32[5,384,256]{2,1,0:T(8,128)}) custom-call(bf16[5,384,1024]{2,1,0:T(8,128)(2,1)} %x_ref.13, bf16[5,48,1024]{2,1,0:T(8,128)(2,1)} %copy-done.4, bf16[5,48,1024]{2,1,0:T(8,128)(2,1)} %copy-done.3, bf16[3,3,3,1024,256]{4,3,2,1,0:T(8,128)(2,1)} %refs_0_.13, ...), custom_call_target="tpu_custom_call" | custom-call | flops 1024 | bytes 1024 | tf_op jit(solution)/shard_map/pallas_call | solution.py:238
  158.3 7.6 %shard_map.105.base_ref = f32[5,384,256]{2,1,0:T(8,128)} custom-call(f32[5,384,256]{2,1,0:T(8,128)} %get-tuple-element.22.base_ref, bf16[1280,256]{1,0:T(8,128)(2,1)} %w_project.3, f32[5,256]{1,0:T(8,128)} %gain.3, f32[5,256]{1,0:T(8,128)} %shift_term.3, f32[5,384,256]{2,1,0:T(8,128)} %get-tuple-element.23.refs_0_, bf16[1,384,256]{2,1,0:T(8,128)(2,1)} %copy-done.13, ...), custom_call_target="tpu_custom_call" | custom-call | flops 1024 | bytes 1024 | tf_op jit(solution)/shard_map/pallas_call | solution.py:316
  166.0 0.7 copy-done.8
  167.1 6.0 %shard_map.108 = bf16[5,384,256]{2,1,0:T(8,128)(2,1)} custom-call(f32[5,384,256]{2,1,0:T(8,128)} %shard_map.105.base_ref, bf16[1280,256]{1,0:T(8,128)(2,1)} %w_project.3, f32[5,256]{1,0:T(8,128)} %gain.3, f32[5,256]{1,0:T(8,128)} %shift_term.3, f32[5,384,256]{2,1,0:T(8,128)} %get-tuple-element.32.refs_0_, bf16[2,384,256]{2,1,0:T(8,128)(2,1)} %copy-done.9, ...), custom_call_target="tpu_custom_call" | custom-call | flops 1024 | bytes 1024 | tf_op jit(solution)/shard_map/pallas_call | solution.py:316
  173.0 6.2 %gather_fusion = bf16[1920,256]{1,0:T(8,128)(2,1)S(1)} fusion(bf16[1920,256]{1,0:T(8,128)(2,1)} %bitcast.15, s32[2048]{0:T(1024)S(1)} %pad_clamp_fusion), kind=kCustom, calls=%fused_computation | custom fusion | bytes 1973760 | tf_op jit(solution)/shard_map/jit(_take)/gather | solution.py:384
  179.4 0.4 broadcast_select_fusion
  179.8 31.0 %all_to_all.5 = bf16[32,60,256]{2,1,0:T(8,128)(2,1)S(1)} all-to-all(bf16[32,60,256]{2,1,0:T(8,128)(2,1)S(1)} %broadcast_select_fusion), channel_id=1, replica_groups=mesh['band'=16,'sample'=2] {'band','sample'}, dimensions={0} | all-to-all | bytes 1966080 | tf_op jit(solution)/shard_map/all_to_all | solution.py:386
  210.9 1.1 reshape.63
  (62 shorter events, 0.9 us)
Async XLA Ops:
  0.0 141.0 %copy-start = (bf16[1024,256]{1,0:T(8,128)(2,1)S(1)}, bf16[1024,256]{1,0:T(8,128)(2,1)}, u32[]{:S(2)}) copy-start(bf16[1024,256]{1,0:T(8,128)(2,1)} %param.13) | copy-start | bytes 1572868
  0.0 2.5 %copy-start.2 = (bf16[5,384,1024]{2,1,0:T(8,128)(2,1)S(1)}, bf16[5,384,1024]{2,1,0:T(8,128)(2,1)}, u32[]{:S(2)}) copy-start(bf16[5,384,1024]{2,1,0:T(8,128)(2,1)} %x_ref.13) | copy-start | bytes 11796484
  1.5 17.8 %collective-permute-start = (bf16[5,96,1024]{2,1,0:T(8,128)(2,1)S(1)}, bf16[5,96,1024]{2,1,0:T(8,128)(2,1)S(1)}, u32[]{:S(2)}, u32[]{:S(2)}) collective-permute-start(bf16[5,96,1024]{2,1,0:T(8,128)(2,1)S(1)} %pad_maximum_fusion), channel_id=1, source_target_pairs={{0,1},{1,0},{2,3},{3,2},{4,5},{5,4},{6,7},{7,6},{8,9},{9,8},{10,11... | collective-permute-start | bytes 2949128 | tf_op jit(solution)/shard_map/ppermute | solution.py:31
  3.2 1.3 collective-permute-start.3
  4.5 4.4 %collective-permute-start.6 = (f32[1024]{0:T(1024)S(1)}, f32[1024]{0:T(1024)S(1)}, u32[]{:S(2)}, u32[]{:S(2)}) collective-permute-start(f32[1024]{0:T(1024)S(1)} %add.42.refs_1_), channel_id=1, source_target_pairs={{0,2},{2,0},{4,6},{6,4},{8,10},{10,8},{12,14},{14,12},{16,18},{18,... | collective-permute-start | bytes 12296 | tf_op jit(solution)/shard_map/ppermute | solution.py:78
  8.9 3.6 %collective-permute-start.10 = (f32[1024]{0:T(1024)S(1)}, f32[1024]{0:T(1024)S(1)}, u32[]{:S(2)}, u32[]{:S(2)}) collective-permute-start(f32[1024]{0:T(1024)S(1)} %add.43.refs_1_), channel_id=1, source_target_pairs={{0,4},{2,6},{4,0},{6,2},{8,12},{10,14},{12,8},{14,10},{16,20},{18,... | collective-permute-start | bytes 12296 | tf_op jit(solution)/shard_map/ppermute | solution.py:78
  12.6 3.7 %collective-permute-start.14 = (f32[1024]{0:T(1024)S(1)}, f32[1024]{0:T(1024)S(1)}, u32[]{:S(2)}, u32[]{:S(2)}) collective-permute-start(f32[1024]{0:T(1024)S(1)} %add.44.refs_1_), channel_id=1, source_target_pairs={{0,8},{2,10},{4,12},{6,14},{8,0},{10,2},{12,4},{14,6},{16,24},{18,... | collective-permute-start | bytes 12296 | tf_op jit(solution)/shard_map/ppermute | solution.py:78
  16.2 14.1 %collective-permute-start.18 = (f32[1024]{0:T(1024)S(1)}, f32[1024]{0:T(1024)S(1)}, u32[]{:S(2)}, u32[]{:S(2)}) collective-permute-start(f32[1024]{0:T(1024)S(1)} %add.45.refs_1_), channel_id=1, source_target_pairs={{0,16},{2,18},{4,20},{6,22},{8,24},{10,26},{12,28},{14,30},{16,0},... | collective-permute-start | bytes 12296 | tf_op jit(solution)/shard_map/ppermute | solution.py:78
  19.3 50.3 %copy-start.3 = (bf16[5,48,1024]{2,1,0:T(8,128)(2,1)}, bf16[5,48,1024]{2,1,0:T(8,128)(2,1)S(1)}, u32[]{:S(2)}) copy-start(bf16[5,48,1024]{2,1,0:T(8,128)(2,1)S(1)} %get-tuple-element.41.after_ref) | copy-start | bytes 1474564
  19.3 50.3 %copy-start.4 = (bf16[5,48,1024]{2,1,0:T(8,128)(2,1)}, bf16[5,48,1024]{2,1,0:T(8,128)(2,1)S(1)}, u32[]{:S(2)}) copy-start(bf16[5,48,1024]{2,1,0:T(8,128)(2,1)S(1)} %get-tuple-element.42.before_ref) | copy-start | bytes 1474564
  19.4 5.4 %copy-start.1 = (bf16[3,3,3,1024,256]{4,3,2,1,0:T(8,128)(2,1)S(1)}, bf16[3,3,3,1024,256]{4,3,2,1,0:T(8,128)(2,1)}, u32[]{:S(2)}) copy-start(bf16[3,3,3,1024,256]{4,3,2,1,0:T(8,128)(2,1)} %refs_0_.13) | copy-start | bytes 42467332
  28.7 53.8 %collective-permute-start.12 = (bf16[4,384,256]{2,1,0:T(8,128)(2,1)S(1)}, bf16[4,384,256]{2,1,0:T(8,128)(2,1)}, u32[]{:S(2)}, u32[]{:S(2)}) collective-permute-start(bf16[4,384,256]{2,1,0:T(8,128)(2,1)S(1)} %get-tuple-element.31), channel_id=1, source_target_pairs={{10,8},{11,9},{12,10},{13,11},{14,12},{15,13},{16,22},{17,23},{18,... | collective-permute-start | bytes 2359304 | tf_op jit(solution)/shard_map/ppermute | solution.py:61
  34.5 46.8 %collective-permute-start.19 = (bf16[3,384,256]{2,1,0:T(8,128)(2,1)S(1)}, bf16[3,384,256]{2,1,0:T(8,128)(2,1)S(1)}, u32[]{:S(2)}, u32[]{:S(2)}) collective-permute-start(bf16[3,384,256]{2,1,0:T(8,128)(2,1)S(1)} %get-tuple-element.35), channel_id=1, source_target_pairs={{4,4},{5,1},{6,6},{7,3},{8,0},{9,13},{10,2},{11,15},{12,12},{13,9}... | collective-permute-start | bytes 1769480 | tf_op jit(solution)/shard_map/ppermute | solution.py:61
  35.8 15.9 %collective-permute-start.11 = (bf16[1,384,256]{2,1,0:T(8,128)(2,1)S(1)}, bf16[1,384,256]{2,1,0:T(8,128)(2,1)S(1)}, u32[]{:S(2)}, u32[]{:S(2)}) collective-permute-start(bf16[1,384,256]{2,1,0:T(8,128)(2,1)S(1)} %get-tuple-element.30), channel_id=1, source_target_pairs={{8,0},{9,1},{10,2},{11,3},{12,4},{13,5},{14,6},{15,7},{16,8},{17,9... | collective-permute-start | bytes 589832 | tf_op jit(solution)/shard_map/ppermute | solution.py:61
  41.1 18.6 %collective-permute-start.9 = (bf16[1,384,256]{2,1,0:T(8,128)(2,1)S(1)}, bf16[1,384,256]{2,1,0:T(8,128)(2,1)S(1)}, u32[]{:S(2)}, u32[]{:S(2)}) collective-permute-start(bf16[1,384,256]{2,1,0:T(8,128)(2,1)S(1)} %get-tuple-element.29), channel_id=1, source_target_pairs={{0,8},{1,9},{2,10},{3,11},{4,12},{5,13},{6,14},{7,15},{8,16},{9,17... | collective-permute-start | bytes 589832 | tf_op jit(solution)/shard_map/ppermute | solution.py:61
  50.4 15.7 %collective-permute-start.5 = (bf16[1,384,256]{2,1,0:T(8,128)(2,1)S(1)}, bf16[1,384,256]{2,1,0:T(8,128)(2,1)S(1)}, u32[]{:S(2)}, u32[]{:S(2)}) collective-permute-start(bf16[1,384,256]{2,1,0:T(8,128)(2,1)S(1)} %get-tuple-element.26), channel_id=1, source_target_pairs={{16,0},{17,1},{18,2},{19,3},{20,4},{21,5},{22,6},{23,7},{24,8},{25... | collective-permute-start | bytes 589832 | tf_op jit(solution)/shard_map/ppermute | solution.py:61
  51.7 8.0 %copy-start.10 = (bf16[1,384,256]{2,1,0:T(8,128)(2,1)}, bf16[1,384,256]{2,1,0:T(8,128)(2,1)S(1)}, u32[]{:S(2)}) copy-start(bf16[1,384,256]{2,1,0:T(8,128)(2,1)S(1)} %collective-permute-done.11.refs_8_) | copy-start | bytes 589828
  51.7 32.2 %collective-permute-start.7 = (bf16[4,384,256]{2,1,0:T(8,128)(2,1)S(1)}, bf16[4,384,256]{2,1,0:T(8,128)(2,1)}, u32[]{:S(2)}, u32[]{:S(2)}) collective-permute-start(bf16[4,384,256]{2,1,0:T(8,128)(2,1)S(1)} %get-tuple-element.28), channel_id=1, source_target_pairs={{0,2},{1,3},{2,4},{3,5},{4,6},{5,7},{6,0},{7,1},{8,10},{9,11},{10,... | collective-permute-start | bytes 2359304 | tf_op jit(solution)/shard_map/ppermute | solution.py:61
  59.7 6.4 %copy-start.11 = (bf16[1,384,256]{2,1,0:T(8,128)(2,1)}, bf16[1,384,256]{2,1,0:T(8,128)(2,1)S(1)}, u32[]{:S(2)}) copy-start(bf16[1,384,256]{2,1,0:T(8,128)(2,1)S(1)} %collective-permute-done.9.refs_7_) | copy-start | bytes 589828
  59.7 15.6 %collective-permute-start.2 = (bf16[1,384,256]{2,1,0:T(8,128)(2,1)S(1)}, bf16[1,384,256]{2,1,0:T(8,128)(2,1)S(1)}, u32[]{:S(2)}, u32[]{:S(2)}) collective-permute-start(bf16[1,384,256]{2,1,0:T(8,128)(2,1)S(1)} %get-tuple-element.24), channel_id=1, source_target_pairs={{0,16},{1,17},{2,18},{3,19},{4,20},{5,21},{6,22},{7,23},{8,24},{9,... | collective-permute-start | bytes 589832 | tf_op jit(solution)/shard_map/ppermute | solution.py:61
  66.1 0.7 copy-start.12
  66.8 23.9 %copy-start.16 = (s32[5,384]{1,0:T(8,128)S(1)}, s32[5,384]{1,0:T(8,128)}, u32[]{:S(2)}) copy-start(s32[5,384]{1,0:T(8,128)} %param.19) | copy-start | bytes 23044
  66.8 74.3 %copy-start.14 = (f32[5,256]{1,0:T(8,128)S(1)}, f32[5,256]{1,0:T(8,128)}, u32[]{:S(2)}) copy-start(f32[5,256]{1,0:T(8,128)} %gain.3) | copy-start | bytes 15364
  66.8 74.3 %copy-start.15 = (f32[5,256]{1,0:T(8,128)S(1)}, f32[5,256]{1,0:T(8,128)}, u32[]{:S(2)}) copy-start(f32[5,256]{1,0:T(8,128)} %shift_term.3) | copy-start | bytes 15364
  66.8 36.9 %collective-permute-start.1 = (bf16[4,384,256]{2,1,0:T(8,128)(2,1)S(1)}, bf16[4,384,256]{2,1,0:T(8,128)(2,1)S(1)}, u32[]{:S(2)}, u32[]{:S(2)}) collective-permute-start(bf16[4,384,256]{2,1,0:T(8,128)(2,1)S(1)} %get-tuple-element.21), channel_id=1, source_target_pairs={{0,14},{1,15},{2,16},{3,17},{4,18},{5,19},{6,20},{7,21},{8,22},{9,... | collective-permute-start | bytes 2359304 | tf_op jit(solution)/shard_map/ppermute | solution.py:61
  74.5 0.8 copy-start.5
  75.3 83.0 %copy-start.13 = (bf16[1,384,256]{2,1,0:T(8,128)(2,1)}, bf16[1,384,256]{2,1,0:T(8,128)(2,1)S(1)}, u32[]{:S(2)}) copy-start(bf16[1,384,256]{2,1,0:T(8,128)(2,1)S(1)} %collective-permute-done.2.refs_1_) | copy-start | bytes 589828
  75.3 15.5 %collective-permute-start.16 = (bf16[3,384,256]{2,1,0:T(8,128)(2,1)}, bf16[3,384,256]{2,1,0:T(8,128)(2,1)}, u32[]{:S(2)}, u32[]{:S(2)}) collective-permute-start(bf16[3,384,256]{2,1,0:T(8,128)(2,1)} %get-tuple-element.34), channel_id=1, source_target_pairs={{0,0},{1,5},{2,2},{3,7},{4,12},{5,1},{6,14},{7,3},{8,8},{9,13},{10... | collective-permute-start | bytes 1769480 | tf_op jit(solution)/shard_map/ppermute | solution.py:61
  81.3 2.6 %copy-start.17 = (bf16[3,384,256]{2,1,0:T(8,128)(2,1)}, bf16[3,384,256]{2,1,0:T(8,128)(2,1)S(1)}, u32[]{:S(2)}) copy-start(bf16[3,384,256]{2,1,0:T(8,128)(2,1)S(1)} %collective-permute-done.19) | copy-start | bytes 1769476
  81.3 32.7 %collective-permute-start.4 = (bf16[4,384,256]{2,1,0:T(8,128)(2,1)S(1)}, bf16[4,384,256]{2,1,0:T(8,128)(2,1)}, u32[]{:S(2)}, u32[]{:S(2)}) collective-permute-start(bf16[4,384,256]{2,1,0:T(8,128)(2,1)S(1)} %get-tuple-element.25), channel_id=1, source_target_pairs={{14,0},{15,1},{16,2},{17,3},{18,4},{19,5},{20,6},{21,7},{22,8},{23... | collective-permute-start | bytes 2359304 | tf_op jit(solution)/shard_map/ppermute | solution.py:61
  82.6 32.7 %collective-permute-start.13 = (bf16[4,384,256]{2,1,0:T(8,128)(2,1)}, bf16[4,384,256]{2,1,0:T(8,128)(2,1)}, u32[]{:S(2)}, u32[]{:S(2)}) collective-permute-start(bf16[4,384,256]{2,1,0:T(8,128)(2,1)} %collective-permute-done.12), channel_id=1, source_target_pairs={{8,0},{9,1},{10,2},{11,3},{12,4},{13,5},{22,6},{23,7},{16,8},{17,9... | collective-permute-start | bytes 2359304 | tf_op jit(solution)/shard_map/ppermute | solution.py:64
  83.9 74.4 %collective-permute-start.8 = (bf16[4,384,256]{2,1,0:T(8,128)(2,1)}, bf16[4,384,256]{2,1,0:T(8,128)(2,1)}, u32[]{:S(2)}, u32[]{:S(2)}) collective-permute-start(bf16[4,384,256]{2,1,0:T(8,128)(2,1)} %collective-permute-done.7), channel_id=1, source_target_pairs={{2,10},{3,11},{4,12},{5,13},{6,14},{7,15},{0,16},{1,17},{10,18},{1... | collective-permute-start | bytes 2359304 | tf_op jit(solution)/shard_map/ppermute | solution.py:64
  90.8 75.2 %collective-permute-start.20 = (bf16[3,384,256]{2,1,0:T(8,128)(2,1)}, bf16[3,384,256]{2,1,0:T(8,128)(2,1)}, u32[]{:S(2)}, u32[]{:S(2)}) collective-permute-start(bf16[3,384,256]{2,1,0:T(8,128)(2,1)} %copy-done.17), channel_id=1, source_target_pairs={{4,0},{1,1},{6,2},{3,3},{0,4},{13,5},{2,6},{15,7},{12,8},{9,9},{14... | collective-permute-start | bytes 1769480 | tf_op jit(solution)/shard_map/ppermute | solution.py:64
  103.7 39.2 %copy-start.6 = (bf16[4,384,256]{2,1,0:T(8,128)(2,1)}, bf16[4,384,256]{2,1,0:T(8,128)(2,1)S(1)}, u32[]{:S(2)}) copy-start(bf16[4,384,256]{2,1,0:T(8,128)(2,1)S(1)} %collective-permute-done.1.refs_7_.refs_2_) | copy-start | bytes 2359300
  103.7 62.3 %collective-permute-start.17 = (bf16[3,384,256]{2,1,0:T(8,128)(2,1)}, bf16[3,384,256]{2,1,0:T(8,128)(2,1)S(1)}, u32[]{:S(2)}, u32[]{:S(2)}) collective-permute-start(bf16[3,384,256]{2,1,0:T(8,128)(2,1)} %collective-permute-done.16), channel_id=1, source_target_pairs={{0,4},{5,5},{2,6},{7,7},{12,8},{1,9},{14,10},{3,11},{8,12},{13,13}... | collective-permute-start | bytes 1769480 | tf_op jit(solution)/shard_map/ppermute | solution.py:64
  114.0 52.0 %collective-permute-start.21 = (bf16[2,384,256]{2,1,0:T(8,128)(2,1)S(1)}, bf16[2,384,256]{2,1,0:T(8,128)(2,1)S(1)}, u32[]{:S(2)}, u32[]{:S(2)}) collective-permute-start(bf16[2,384,256]{2,1,0:T(8,128)(2,1)S(1)} %get-tuple-element.36), channel_id=1, source_target_pairs={{6,0},{7,1},{8,2},{9,3},{10,4},{11,5},{12,6},{13,7},{14,8},{15,9},... | collective-permute-start | bytes 1179656 | tf_op jit(solution)/shard_map/ppermute | solution.py:61
  115.3 50.7 %collective-permute-start.15 = (bf16[2,384,256]{2,1,0:T(8,128)(2,1)}, bf16[2,384,256]{2,1,0:T(8,128)(2,1)S(1)}, u32[]{:S(2)}, u32[]{:S(2)}) collective-permute-start(bf16[2,384,256]{2,1,0:T(8,128)(2,1)} %copy-done.5), channel_id=1, source_target_pairs={{0,6},{1,7},{2,8},{3,9},{4,10},{5,11},{6,12},{7,13},{8,14},{9,15},... | collective-permute-start | bytes 1179656 | tf_op jit(solution)/shard_map/ppermute | solution.py:61
  165.9 0.8 copy-start.8
  165.9 0.9 copy-start.9
  166.0 1.1 copy-start.7

commit v3 on v2

--- a/solution.py
+++ b/solution.py
@@ -13,6 +13,7 @@
 wide_limit = 56 * 2**20
 small_cost = pl.CostEstimate(flops=1024, bytes_accessed=1024, transcendentals=0)
 routes = {5: "within", 2: "split"}
+own_place = 4
 levels = 4
 
 
@@ -33,7 +34,7 @@
     return lax.ppermute(last, "sample", up), lax.ppermute(leading, "sample", down)
 
 
-def passed_along(array, by):
+def passed_along(array, by, hold=None):
     band_count = lax.axis_size("band")
     half_count = lax.axis_size("sample")
     level = max(band_count // levels, 1)
@@ -61,6 +62,8 @@
     array = lax.ppermute(array, ("band", "sample"), first)
     part_way = array
     if route != "direct":
+        if hold is not None:
+            array, _ = lax.optimization_barrier((array, hold))
         array = lax.ppermute(array, ("band", "sample"), second)
     return array, part_way
 
@@ -344,29 +347,31 @@
 
     arrived, part_way = {}, {}
 
-    def send(branch, row_tap, tokens=()):
+    def send(branch, row_tap, tokens=(), hold=None):
         near, *far = row_taps(features, before, after, w_atrous, ((branch, row_tap),), tokens)
         band_step, remainder = split_of((row_tap - 1) * dilation_list[branch], row_count)
-        near, near_way = passed_along(near, -band_step)
-        far, far_way = passed_along(far[0], -band_step - 1) if far else (None, near_way)
+        near, near_way = passed_along(near, -band_step, hold)
+        far, far_way = passed_along(far[0], -band_step - 1, hold) if far else (None, near_way)
         arrived[branch, row_tap] = (near, far)
         ways = (near_way, far_way) if near_way.shape[0] < far_way.shape[0] else (far_way, near_way)
         part_way[branch, row_tap] = ways
 
     totals, steps = total_over_devices(jnp.sum(features, axis=(0, 1), dtype=jnp.float32))
     order = ((2, 0), (2, 2), (1, 0), (1, 2), (0, 0), (0, 2))
+    centre, base = {}, None
     for place, (branch, row_tap) in enumerate(order):
-        send(branch, row_tap, steps[place - 1 : place] if place else ())
-    centre = {}
-    centre[2], centre[1], centre[0], base = own_rows(
-        features,
-        before,
-        after,
-        w_atrous,
-        (2, 1, 0),
-        (w_point, w_project, branch_gain, branch_bias),
-        [part_way[2, 0][1]],
-    )
+        if place == own_place:
+            centre[2], centre[1], centre[0], base = own_rows(
+                features,
+                before,
+                after,
+                w_atrous,
+                (2, 1, 0),
+                (w_point, w_project, branch_gain, branch_bias),
+                [part_way[2, 0][1]],
+            )
+        send(branch, row_tap, steps[place - 1 : place] if place else (), base)
+
     pooled = totals / (row_count * band_count * width_local * half_count)
     pool_input = pooled.astype(jnp.bfloat16)
     pool_value = jnp.dot(pool_input[None, :], w_pool, preferred_element_type=jnp.float32)

time: 213 us -> 202 us (0.948)
  starting transfers between devices: 91.8 us -> 71.4 us
  blocking collectives: 31 us -> 40.7 us
  waiting for transfers between devices: 13.9 us -> 16.9 us
  local copies, waits for them, and re-layouts: 17.5 us -> 15 us
    all_to_all x1, blocking collectives: 31 us -> 40.7 us  [shards(): lax.all_to_all(outgoing, ('band', 'sample'), split_axis=0, concat_axis=0,...]
    ppermute x12, starting transfers between devices: 57.9 us -> 50.8 us  [passed_along(): array = lax.ppermute(array, ('band', 'sample'), first)]
    ppermute x4, starting transfers between devices: 22.9 us -> 16.1 us  [passed_along(): array = lax.ppermute(array, ('band', 'sample'), second)]
    ppermute x5, starting transfers between devices: 10.5 us -> 4.01 us  [total_over_devices(): lax.ppermute(values, axis, [(i, i ^ step) for i in range(size)])]
    ppermute x5, waiting for transfers between devices: 5.58 us -> 9.37 us  [total_over_devices(): lax.ppermute(values, axis, [(i, i ^ step) for i in range(size)])]
    unnamed x37 -> x31, local copies, waits for them, and re-layouts: 8.43 us -> 5.89 us
    ppermute x12, waiting for transfers between devices: 8.35 us -> 6 us  [passed_along(): array = lax.ppermute(array, ('band', 'sample'), first)]
  transfers between devices with their start and end apart: 22 -> 22, of which waited for: 5 -> 8; matrix products, arithmetic and copies ran while one was open for 1% -> 1% of each run, Pallas kernels for 23% -> 22%
where the time goes in v3:
time: 202 us; the launch traced here: 201 us
  starting transfers between devices  71.4 us (35%)
  Pallas kernels  53.4 us (26%)
  blocking collectives  40.7 us (20%)
  waiting for transfers between devices  16.9 us (8%)
  local copies, waits for them, and re-layouts  15 us (7%)
    ppermute x12, starting transfers between devices, passed_along(): array = lax.ppermute(array, ('band', 'sample'), first)  50.8 us
    all_to_all x1, blocking collectives, shards(): lax.all_to_all(outgoing, ('band', 'sample'), split_axis=0, concat_axis=0,...  40.7 us
    pallas_call x6, Pallas kernels, row_taps(): pl.pallas_call(functools.partial(taps_body, plan, row_count, len(tokens))...  24.3 us
    ppermute x4, starting transfers between devices, passed_along(): array = lax.ppermute(array, ('band', 'sample'), second)  16.1 us
    pallas_call x1, Pallas kernels, own_rows(): pl.pallas_call(functools.partial(own_body, plan, point_operands is not No...  15.5 us
    pallas_call x2, Pallas kernels, join(): pl.pallas_call(functools.partial(join_body, plan, remainders, tail is not...  13.6 us
    ppermute x5, waiting for transfers between devices, total_over_devices(): lax.ppermute(values, axis, [(i, i ^ step) for i in range(size)])  9.37 us
    gather x2, local copies, waits for them, and re-layouts, shards(): outgoing = jnp.take(projected.reshape(pixels, depth), slots, axis=0)  6.35 us
  transfers between devices with their start and end apart: 22, of which 8 were waited for; matrix products, arithmetic and copies ran while one was open for 1% of the time, Pallas kernels for 22%

profile of v3, /device:TPU:0, one launch (start us, length us, event | category | flops | bytes accessed | tf_op | source)
XLA Modules:
  0.0 201.0 jit_solution(15012985064108125283)
XLA Ops:
  0.0 1.4 fusion.11
  1.5 0.5 collective-permute-start
  2.0 0.5 copy-done.2
  2.5 0.7 convert_reduce_fusion
  3.2 0.5 collective-permute-start.3
  3.7 0.8 collective-permute-done.3
  4.5 2.8 %collective-permute-start.6 = (f32[1024]{0:T(1024)S(1)}, f32[1024]{0:T(1024)S(1)}, u32[]{:S(2)}, u32[]{:S(2)}) collective-permute-start(f32[1024]{0:T(1024)S(1)} %add.42.refs_1_), channel_id=1, source_target_pairs={{0,2},{2,0},{4,6},{6,4},{8,10},{10,8},{12,14},{14,12},{16,18},{18,... | collective-permute-start | bytes 12296 | tf_op jit(solution)/shard_map/ppermute | solution.py:81
  7.3 1.6 collective-permute-done.6
  9.1 5.4 %copy-done.1 = bf16[3,3,3,1024,256]{4,3,2,1,0:T(8,128)(2,1)S(1)} copy-done((bf16[3,3,3,1024,256]{4,3,2,1,0:T(8,128)(2,1)S(1)}, bf16[3,3,3,1024,256]{4,3,2,1,0:T(8,128)(2,1)}, u32[]{:S(2)}) %copy-start.1) | copy-done | bytes 14155800
  14.4 4.0 %shard_map.103 = (bf16[4,384,256]{2,1,0:T(8,128)(2,1)S(1)}, bf16[1,384,256]{2,1,0:T(8,128)(2,1)S(1)}) custom-call(bf16[5,384,1024]{2,1,0:T(8,128)(2,1)S(1)} %copy-done.2, bf16[5,48,1024]{2,1,0:T(8,128)(2,1)S(1)} %get-tuple-element.46.before_ref, bf16[5,48,1024]{2,1,0:T(8,128)(2,1)S(1)} %get-tuple-element.45.after_ref, ...), custom_call_target="tpu_custom_call" | custom-call | flops 1024 | bytes 1024 | tf_op jit(solution)/shard_map/pallas_call | solution.py:164
  18.4 3.9 %collective-permute-start.7 = (bf16[4,384,256]{2,1,0:T(8,128)(2,1)S(1)}, bf16[4,384,256]{2,1,0:T(8,128)(2,1)}, u32[]{:S(2)}, u32[]{:S(2)}) collective-permute-start(bf16[4,384,256]{2,1,0:T(8,128)(2,1)S(1)} %get-tuple-element.30), channel_id=1, source_target_pairs={{0,2},{1,3},{2,4},{3,5},{4,6},{5,7},{6,0},{7,1},{8,10},{9,11},{10,... | collective-permute-start | bytes 2359304 | tf_op jit(solution)/shard_map/ppermute | solution.py:62
  22.4 4.1 %shard_map.100 = (bf16[1,384,256]{2,1,0:T(8,128)(2,1)S(1)}, bf16[4,384,256]{2,1,0:T(8,128)(2,1)S(1)}) custom-call(bf16[5,384,1024]{2,1,0:T(8,128)(2,1)S(1)} %copy-done.2, bf16[5,48,1024]{2,1,0:T(8,128)(2,1)S(1)} %get-tuple-element.46.before_ref, bf16[5,48,1024]{2,1,0:T(8,128)(2,1)S(1)} %get-tuple-element.45.after_ref, bf16[3,3,3,1024,256]{4,3,2,1,0:T(8,128)(2,1)S(1)} %copy-done.1), custom_call_target="tpu_custom_call" | custom-call | flops 1024 | bytes 1024 | tf_op jit(solution)/shard_map/pallas_call | solution.py:164
  26.4 5.4 %collective-permute-start.2 = (bf16[1,384,256]{2,1,0:T(8,128)(2,1)S(1)}, bf16[1,384,256]{2,1,0:T(8,128)(2,1)S(1)}, u32[]{:S(2)}, u32[]{:S(2)}) collective-permute-start(bf16[1,384,256]{2,1,0:T(8,128)(2,1)S(1)} %get-tuple-element.26), channel_id=1, source_target_pairs={{0,16},{1,17},{2,18},{3,19},{4,20},{5,21},{6,22},{7,23},{8,24},{9,... | collective-permute-start | bytes 589832 | tf_op jit(solution)/shard_map/ppermute | solution.py:62
  31.9 0.7 collective-permute-start.10
  32.5 3.4 %collective-permute-done.10 = f32[1024]{0:T(1024)S(1)} collective-permute-done((f32[1024]{0:T(1024)S(1)}, f32[1024]{0:T(1024)S(1)}, u32[]{:S(2)}, u32[]{:S(2)}) %collective-permute-start.10) | collective-permute-done | bytes 4128 | tf_op jit(solution)/shard_map/ppermute | solution.py:81
  35.9 3.6 %collective-permute-done.14 = f32[1024]{0:T(1024)S(1)} collective-permute-done((f32[1024]{0:T(1024)S(1)}, f32[1024]{0:T(1024)S(1)}, u32[]{:S(2)}, u32[]{:S(2)}) %collective-permute-start.14) | collective-permute-done | bytes 4128 | tf_op jit(solution)/shard_map/ppermute | solution.py:81
  39.5 4.1 %shard_map.106 = (bf16[2,384,256]{2,1,0:T(8,128)(2,1)S(1)}, bf16[3,384,256]{2,1,0:T(8,128)(2,1)S(1)}) custom-call(bf16[5,384,1024]{2,1,0:T(8,128)(2,1)S(1)} %copy-done.2, bf16[5,48,1024]{2,1,0:T(8,128)(2,1)S(1)} %get-tuple-element.46.before_ref, bf16[5,48,1024]{2,1,0:T(8,128)(2,1)S(1)} %get-tuple-element.45.after_ref, ...), custom_call_target="tpu_custom_call" | custom-call | flops 1024 | bytes 1024 | tf_op jit(solution)/shard_map/pallas_call | solution.py:164
  43.6 1.5 collective-permute-start.16
  45.1 4.1 %shard_map.102 = (bf16[4,384,256]{2,1,0:T(8,128)(2,1)S(1)}, bf16[1,384,256]{2,1,0:T(8,128)(2,1)S(1)}) custom-call(bf16[5,384,1024]{2,1,0:T(8,128)(2,1)S(1)} %copy-done.2, bf16[5,48,1024]{2,1,0:T(8,128)(2,1)S(1)} %get-tuple-element.46.before_ref, bf16[5,48,1024]{2,1,0:T(8,128)(2,1)S(1)} %get-tuple-element.45.after_ref, ...), custom_call_target="tpu_custom_call" | custom-call | flops 1024 | bytes 1024 | tf_op jit(solution)/shard_map/pallas_call | solution.py:164
  49.2 4.0 %shard_map.104 = (bf16[1,384,256]{2,1,0:T(8,128)(2,1)S(1)}, bf16[4,384,256]{2,1,0:T(8,128)(2,1)S(1)}) custom-call(bf16[5,384,1024]{2,1,0:T(8,128)(2,1)S(1)} %copy-done.2, bf16[5,48,1024]{2,1,0:T(8,128)(2,1)S(1)} %get-tuple-element.46.before_ref, bf16[5,48,1024]{2,1,0:T(8,128)(2,1)S(1)} %get-tuple-element.45.after_ref, ...), custom_call_target="tpu_custom_call" | custom-call | flops 1024 | bytes 1024 | tf_op jit(solution)/shard_map/pallas_call | solution.py:164
  53.2 2.8 %collective-permute-start.1 = (bf16[4,384,256]{2,1,0:T(8,128)(2,1)S(1)}, bf16[4,384,256]{2,1,0:T(8,128)(2,1)S(1)}, u32[]{:S(2)}, u32[]{:S(2)}) collective-permute-start(bf16[4,384,256]{2,1,0:T(8,128)(2,1)S(1)} %get-tuple-element.23), channel_id=1, source_target_pairs={{0,14},{1,15},{2,16},{3,17},{4,18},{5,19},{6,20},{7,21},{8,22},{9,... | collective-permute-start | bytes 2359304 | tf_op jit(solution)/shard_map/ppermute | solution.py:62
  56.1 1.3 collective-permute-start.5
  57.4 1.5 collective-permute-start.12
  59.0 4.1 %shard_map.107 = (bf16[3,384,256]{2,1,0:T(8,128)(2,1)S(1)}, bf16[2,384,256]{2,1,0:T(8,128)(2,1)S(1)}) custom-call(bf16[5,384,1024]{2,1,0:T(8,128)(2,1)S(1)} %copy-done.2, bf16[5,48,1024]{2,1,0:T(8,128)(2,1)S(1)} %get-tuple-element.46.before_ref, bf16[5,48,1024]{2,1,0:T(8,128)(2,1)S(1)} %get-tuple-element.45.after_ref, ...), custom_call_target="tpu_custom_call" | custom-call | flops 1024 | bytes 1024 | tf_op jit(solution)/shard_map/pallas_call | solution.py:164
  63.1 2.3 %collective-permute-done.5.refs_4_ = bf16[1,384,256]{2,1,0:T(8,128)(2,1)S(1)} collective-permute-done((bf16[1,384,256]{2,1,0:T(8,128)(2,1)S(1)}, bf16[1,384,256]{2,1,0:T(8,128)(2,1)S(1)}, u32[]{:S(2)}, u32[]{:S(2)}) %collective-permute-start.5) | collective-permute-done | bytes 196640 | tf_op jit(solution)/shard_map/ppermute | solution.py:62
  65.4 1.3 collective-permute-start.19
  66.7 1.3 collective-permute-start.4
  68.0 10.8 %collective-permute-start.8 = (bf16[4,384,256]{2,1,0:T(8,128)(2,1)}, bf16[4,384,256]{2,1,0:T(8,128)(2,1)}, u32[]{:S(2)}, u32[]{:S(2)}) collective-permute-start(bf16[4,384,256]{2,1,0:T(8,128)(2,1)} %collective-permute-done.7), channel_id=1, source_target_pairs={{2,10},{3,11},{4,12},{5,13},{6,14},{7,15},{0,16},{1,17},{10,18},{1... | collective-permute-start | bytes 2359304 | tf_op jit(solution)/shard_map/ppermute | solution.py:67
  78.8 0.5 collective-permute-done.19
  79.2 26.2 %collective-permute-start.9 = (bf16[1,384,256]{2,1,0:T(8,128)(2,1)S(1)}, bf16[1,384,256]{2,1,0:T(8,128)(2,1)S(1)}, u32[]{:S(2)}, u32[]{:S(2)}) collective-permute-start(bf16[1,384,256]{2,1,0:T(8,128)(2,1)S(1)} %get-tuple-element.31), channel_id=1, source_target_pairs={{0,8},{1,9},{2,10},{3,11},{4,12},{5,13},{6,14},{7,15},{8,16},{9,17... | collective-permute-start | bytes 589832 | tf_op jit(solution)/shard_map/ppermute | solution.py:62
  105.4 1.3 collective-permute-start.11
  106.8 1.3 collective-permute-start.13
  108.1 0.1 reshape.59
  108.2 15.5 %shard_map.101 = (f32[5,384,256]{2,1,0:T(8,128)}, f32[5,384,256]{2,1,0:T(8,128)}, f32[5,384,256]{2,1,0:T(8,128)}, f32[5,384,256]{2,1,0:T(8,128)}) custom-call(bf16[5,384,1024]{2,1,0:T(8,128)(2,1)} %x_ref.13, bf16[5,48,1024]{2,1,0:T(8,128)(2,1)} %copy-done.4, bf16[5,48,1024]{2,1,0:T(8,128)(2,1)} %copy-done.3, bf16[3,3,3,1024,256]{4,3,2,1,0:T(8,128)(2,1)} %refs_0_.13, ...), custom_call_target="tpu_custom_call" | custom-call | flops 1024 | bytes 1024 | tf_op jit(solution)/shard_map/pallas_call | solution.py:241
  123.7 2.1 %collective-permute-start.17 = (bf16[3,384,256]{2,1,0:T(8,128)(2,1)}, bf16[3,384,256]{2,1,0:T(8,128)(2,1)}, u32[]{:S(2)}, u32[]{:S(2)}) collective-permute-start(bf16[3,384,256]{2,1,0:T(8,128)(2,1)} %collective-permute-done.16), channel_id=1, source_target_pairs={{0,4},{5,5},{2,6},{7,7},{12,8},{1,9},{14,10},{3,11},{8,12},{13,13}... | collective-permute-start | bytes 1769480 | tf_op jit(solution)/shard_map/ppermute | solution.py:67
  125.9 1.9 collective-permute-start.20
  127.8 2.9 %collective-permute-start.15 = (bf16[2,384,256]{2,1,0:T(8,128)(2,1)S(1)}, bf16[2,384,256]{2,1,0:T(8,128)(2,1)S(1)}, u32[]{:S(2)}, u32[]{:S(2)}) collective-permute-start(bf16[2,384,256]{2,1,0:T(8,128)(2,1)S(1)} %get-tuple-element.35), channel_id=1, source_target_pairs={{0,6},{1,7},{2,8},{3,9},{4,10},{5,11},{6,12},{7,13},{8,14},{9,15},... | collective-permute-start | bytes 1179656 | tf_op jit(solution)/shard_map/ppermute | solution.py:62
  130.8 1.3 collective-permute-start.21
  132.1 1.8 fusion.4.refs_5_
  134.0 7.6 %shard_map.105.base_ref = f32[5,384,256]{2,1,0:T(8,128)} custom-call(f32[5,384,256]{2,1,0:T(8,128)} %get-tuple-element.24.base_ref, bf16[1280,256]{1,0:T(8,128)(2,1)} %w_project.3, f32[5,256]{1,0:T(8,128)} %gain.3, f32[5,256]{1,0:T(8,128)} %shift_term.3, f32[5,384,256]{2,1,0:T(8,128)} %get-tuple-element.25.refs_0_, bf16[1,384,256]{2,1,0:T(8,128)(2,1)} %copy-done.9, ...), custom_call_target="tpu_custom_call" | custom-call | flops 1024 | bytes 1024 | tf_op jit(solution)/shard_map/pallas_call | solution.py:319
  141.6 3.2 %collective-permute-done.15.refs_1_ = bf16[2,384,256]{2,1,0:T(8,128)(2,1)S(1)} collective-permute-done((bf16[2,384,256]{2,1,0:T(8,128)(2,1)S(1)}, bf16[2,384,256]{2,1,0:T(8,128)(2,1)S(1)}, u32[]{:S(2)}, u32[]{:S(2)}) %collective-permute-start.15) | collective-permute-done | bytes 393248 | tf_op jit(solution)/shard_map/ppermute | solution.py:62
  144.8 1.6 collective-permute-done.20.refs_3_
  146.4 6.0 %shard_map.108 = bf16[5,384,256]{2,1,0:T(8,128)(2,1)} custom-call(f32[5,384,256]{2,1,0:T(8,128)} %shard_map.105.base_ref, bf16[1280,256]{1,0:T(8,128)(2,1)} %w_project.3, f32[5,256]{1,0:T(8,128)} %gain.3, f32[5,256]{1,0:T(8,128)} %shift_term.3, f32[5,384,256]{2,1,0:T(8,128)} %get-tuple-element.34.refs_0_, bf16[2,384,256]{2,1,0:T(8,128)(2,1)} %copy-done.7, ...), custom_call_target="tpu_custom_call" | custom-call | flops 1024 | bytes 1024 | tf_op jit(solution)/shard_map/pallas_call | solution.py:319
  152.4 6.2 %gather_fusion = bf16[1920,256]{1,0:T(8,128)(2,1)S(1)} fusion(bf16[1920,256]{1,0:T(8,128)(2,1)} %bitcast.15, s32[2048]{0:T(1024)S(1)} %pad_clamp_fusion), kind=kCustom, calls=%fused_computation | custom fusion | bytes 1973760 | tf_op jit(solution)/shard_map/jit(_take)/gather | solution.py:389
  158.5 0.2 gather.7
  158.7 0.4 broadcast_select_fusion
  159.2 40.7 %all_to_all.5 = bf16[32,60,256]{2,1,0:T(8,128)(2,1)S(1)} all-to-all(bf16[32,60,256]{2,1,0:T(8,128)(2,1)S(1)} %broadcast_select_fusion), channel_id=1, replica_groups=mesh['band'=16,'sample'=2] {'band','sample'}, dimensions={0} | all-to-all | bytes 1966080 | tf_op jit(solution)/shard_map/all_to_all | solution.py:391
  199.9 1.1 reshape.63
  (56 shorter events, 0.4 us)
Async XLA Ops:
  0.0 132.1 %copy-start = (bf16[1024,256]{1,0:T(8,128)(2,1)S(1)}, bf16[1024,256]{1,0:T(8,128)(2,1)}, u32[]{:S(2)}) copy-start(bf16[1024,256]{1,0:T(8,128)(2,1)} %param.13) | copy-start | bytes 1572868
  0.0 2.5 %copy-start.2 = (bf16[5,384,1024]{2,1,0:T(8,128)(2,1)S(1)}, bf16[5,384,1024]{2,1,0:T(8,128)(2,1)}, u32[]{:S(2)}) copy-start(bf16[5,384,1024]{2,1,0:T(8,128)(2,1)} %x_ref.13) | copy-start | bytes 11796484
  1.5 7.4 %collective-permute-start = (bf16[5,96,1024]{2,1,0:T(8,128)(2,1)S(1)}, bf16[5,96,1024]{2,1,0:T(8,128)(2,1)S(1)}, u32[]{:S(2)}, u32[]{:S(2)}) collective-permute-start(bf16[5,96,1024]{2,1,0:T(8,128)(2,1)S(1)} %pad_maximum_fusion), channel_id=1, source_target_pairs={{0,1},{1,0},{2,3},{3,2},{4,5},{5,4},{6,7},{7,6},{8,9},{9,8},{10,11... | collective-permute-start | bytes 2949128 | tf_op jit(solution)/shard_map/ppermute | solution.py:32
  3.2 1.3 collective-permute-start.3
  4.5 4.4 %collective-permute-start.6 = (f32[1024]{0:T(1024)S(1)}, f32[1024]{0:T(1024)S(1)}, u32[]{:S(2)}, u32[]{:S(2)}) collective-permute-start(f32[1024]{0:T(1024)S(1)} %add.42.refs_1_), channel_id=1, source_target_pairs={{0,2},{2,0},{4,6},{6,4},{8,10},{10,8},{12,14},{14,12},{16,18},{18,... | collective-permute-start | bytes 12296 | tf_op jit(solution)/shard_map/ppermute | solution.py:81
  9.0 49.9 %copy-start.3 = (bf16[5,48,1024]{2,1,0:T(8,128)(2,1)}, bf16[5,48,1024]{2,1,0:T(8,128)(2,1)S(1)}, u32[]{:S(2)}) copy-start(bf16[5,48,1024]{2,1,0:T(8,128)(2,1)S(1)} %get-tuple-element.45.after_ref) | copy-start | bytes 1474564
  9.0 49.9 %copy-start.4 = (bf16[5,48,1024]{2,1,0:T(8,128)(2,1)}, bf16[5,48,1024]{2,1,0:T(8,128)(2,1)S(1)}, u32[]{:S(2)}) copy-start(bf16[5,48,1024]{2,1,0:T(8,128)(2,1)S(1)} %get-tuple-element.46.before_ref) | copy-start | bytes 1474564
  9.0 5.4 %copy-start.1 = (bf16[3,3,3,1024,256]{4,3,2,1,0:T(8,128)(2,1)S(1)}, bf16[3,3,3,1024,256]{4,3,2,1,0:T(8,128)(2,1)}, u32[]{:S(2)}) copy-start(bf16[3,3,3,1024,256]{4,3,2,1,0:T(8,128)(2,1)} %refs_0_.13) | copy-start | bytes 42467332
  18.4 49.6 %collective-permute-start.7 = (bf16[4,384,256]{2,1,0:T(8,128)(2,1)S(1)}, bf16[4,384,256]{2,1,0:T(8,128)(2,1)}, u32[]{:S(2)}, u32[]{:S(2)}) collective-permute-start(bf16[4,384,256]{2,1,0:T(8,128)(2,1)S(1)} %get-tuple-element.30), channel_id=1, source_target_pairs={{0,2},{1,3},{2,4},{3,5},{4,6},{5,7},{6,0},{7,1},{8,10},{9,11},{10,... | collective-permute-start | bytes 2359304 | tf_op jit(solution)/shard_map/ppermute | solution.py:62
  26.4 30.9 %collective-permute-start.2 = (bf16[1,384,256]{2,1,0:T(8,128)(2,1)S(1)}, bf16[1,384,256]{2,1,0:T(8,128)(2,1)S(1)}, u32[]{:S(2)}, u32[]{:S(2)}) collective-permute-start(bf16[1,384,256]{2,1,0:T(8,128)(2,1)S(1)} %get-tuple-element.26), channel_id=1, source_target_pairs={{0,16},{1,17},{2,18},{3,19},{4,20},{5,21},{6,22},{7,23},{8,24},{9,... | collective-permute-start | bytes 589832 | tf_op jit(solution)/shard_map/ppermute | solution.py:62
  31.9 4.0 %collective-permute-start.10 = (f32[1024]{0:T(1024)S(1)}, f32[1024]{0:T(1024)S(1)}, u32[]{:S(2)}, u32[]{:S(2)}) collective-permute-start(f32[1024]{0:T(1024)S(1)} %add.43.refs_1_), channel_id=1, source_target_pairs={{0,4},{2,6},{4,0},{6,2},{8,12},{10,14},{12,8},{14,10},{16,20},{18,... | collective-permute-start | bytes 12296 | tf_op jit(solution)/shard_map/ppermute | solution.py:81
  35.9 3.6 %collective-permute-start.14 = (f32[1024]{0:T(1024)S(1)}, f32[1024]{0:T(1024)S(1)}, u32[]{:S(2)}, u32[]{:S(2)}) collective-permute-start(f32[1024]{0:T(1024)S(1)} %add.44.refs_1_), channel_id=1, source_target_pairs={{0,8},{2,10},{4,12},{6,14},{8,0},{10,2},{12,4},{14,6},{16,24},{18,... | collective-permute-start | bytes 12296 | tf_op jit(solution)/shard_map/ppermute | solution.py:81
  43.6 23.1 %collective-permute-start.16 = (bf16[3,384,256]{2,1,0:T(8,128)(2,1)S(1)}, bf16[3,384,256]{2,1,0:T(8,128)(2,1)}, u32[]{:S(2)}, u32[]{:S(2)}) collective-permute-start(bf16[3,384,256]{2,1,0:T(8,128)(2,1)S(1)} %get-tuple-element.36), channel_id=1, source_target_pairs={{0,0},{1,5},{2,2},{3,7},{4,12},{5,1},{6,14},{7,3},{8,8},{9,13},{10... | collective-permute-start | bytes 1769480 | tf_op jit(solution)/shard_map/ppermute | solution.py:62
  45.1 10.9 %collective-permute-start.18 = (f32[1024]{0:T(1024)S(1)}, f32[1024]{0:T(1024)S(1)}, u32[]{:S(2)}, u32[]{:S(2)}) collective-permute-start(f32[1024]{0:T(1024)S(1)} %add.45.refs_1_), channel_id=1, source_target_pairs={{0,16},{2,18},{4,20},{6,22},{8,24},{10,26},{12,28},{14,30},{16,0},... | collective-permute-start | bytes 12296 | tf_op jit(solution)/shard_map/ppermute | solution.py:81
  53.2 52.2 %collective-permute-start.1 = (bf16[4,384,256]{2,1,0:T(8,128)(2,1)S(1)}, bf16[4,384,256]{2,1,0:T(8,128)(2,1)S(1)}, u32[]{:S(2)}, u32[]{:S(2)}) collective-permute-start(bf16[4,384,256]{2,1,0:T(8,128)(2,1)S(1)} %get-tuple-element.23), channel_id=1, source_target_pairs={{0,14},{1,15},{2,16},{3,17},{4,18},{5,19},{6,20},{7,21},{8,22},{9,... | collective-permute-start | bytes 2359304 | tf_op jit(solution)/shard_map/ppermute | solution.py:62
  56.1 9.3 %collective-permute-start.5 = (bf16[1,384,256]{2,1,0:T(8,128)(2,1)S(1)}, bf16[1,384,256]{2,1,0:T(8,128)(2,1)S(1)}, u32[]{:S(2)}, u32[]{:S(2)}) collective-permute-start(bf16[1,384,256]{2,1,0:T(8,128)(2,1)S(1)} %get-tuple-element.28), channel_id=1, source_target_pairs={{16,0},{17,1},{18,2},{19,3},{20,4},{21,5},{22,6},{23,7},{24,8},{25... | collective-permute-start | bytes 589832 | tf_op jit(solution)/shard_map/ppermute | solution.py:62
  57.4 1.6 copy-start.9
  57.4 49.3 %collective-permute-start.12 = (bf16[4,384,256]{2,1,0:T(8,128)(2,1)S(1)}, bf16[4,384,256]{2,1,0:T(8,128)(2,1)}, u32[]{:S(2)}, u32[]{:S(2)}) collective-permute-start(bf16[4,384,256]{2,1,0:T(8,128)(2,1)S(1)} %get-tuple-element.33), channel_id=1, source_target_pairs={{10,8},{11,9},{12,10},{13,11},{14,12},{15,13},{16,22},{17,23},{18,... | collective-permute-start | bytes 2359304 | tf_op jit(solution)/shard_map/ppermute | solution.py:62
  59.0 49.1 %copy-start.14 = (s32[5,384]{1,0:T(8,128)S(1)}, s32[5,384]{1,0:T(8,128)}, u32[]{:S(2)}) copy-start(s32[5,384]{1,0:T(8,128)} %param.19) | copy-start | bytes 23044
  65.4 41.3 %copy-start.10 = (bf16[1,384,256]{2,1,0:T(8,128)(2,1)}, bf16[1,384,256]{2,1,0:T(8,128)(2,1)S(1)}, u32[]{:S(2)}) copy-start(bf16[1,384,256]{2,1,0:T(8,128)(2,1)S(1)} %collective-permute-done.5.refs_4_) | copy-start | bytes 589828
  65.4 13.8 %collective-permute-start.19 = (bf16[3,384,256]{2,1,0:T(8,128)(2,1)S(1)}, bf16[3,384,256]{2,1,0:T(8,128)(2,1)}, u32[]{:S(2)}, u32[]{:S(2)}) collective-permute-start(bf16[3,384,256]{2,1,0:T(8,128)(2,1)S(1)} %get-tuple-element.38), channel_id=1, source_target_pairs={{4,4},{5,1},{6,6},{7,3},{8,0},{9,13},{10,2},{11,15},{12,12},{13,9}... | collective-permute-start | bytes 1769480 | tf_op jit(solution)/shard_map/ppermute | solution.py:62
  66.7 61.1 %collective-permute-start.4 = (bf16[4,384,256]{2,1,0:T(8,128)(2,1)S(1)}, bf16[4,384,256]{2,1,0:T(8,128)(2,1)S(1)}, u32[]{:S(2)}, u32[]{:S(2)}) collective-permute-start(bf16[4,384,256]{2,1,0:T(8,128)(2,1)S(1)} %get-tuple-element.27), channel_id=1, source_target_pairs={{14,0},{15,1},{16,2},{17,3},{18,4},{19,5},{20,6},{21,7},{22,8},{23... | collective-permute-start | bytes 2359304 | tf_op jit(solution)/shard_map/ppermute | solution.py:62
  68.0 62.7 %collective-permute-start.8 = (bf16[4,384,256]{2,1,0:T(8,128)(2,1)}, bf16[4,384,256]{2,1,0:T(8,128)(2,1)}, u32[]{:S(2)}, u32[]{:S(2)}) collective-permute-start(bf16[4,384,256]{2,1,0:T(8,128)(2,1)} %collective-permute-done.7), channel_id=1, source_target_pairs={{2,10},{3,11},{4,12},{5,13},{6,14},{7,15},{0,16},{1,17},{10,18},{1... | collective-permute-start | bytes 2359304 | tf_op jit(solution)/shard_map/ppermute | solution.py:67
  79.2 44.5 %collective-permute-start.9 = (bf16[1,384,256]{2,1,0:T(8,128)(2,1)S(1)}, bf16[1,384,256]{2,1,0:T(8,128)(2,1)S(1)}, u32[]{:S(2)}, u32[]{:S(2)}) collective-permute-start(bf16[1,384,256]{2,1,0:T(8,128)(2,1)S(1)} %get-tuple-element.31), channel_id=1, source_target_pairs={{0,8},{1,9},{2,10},{3,11},{4,12},{5,13},{6,14},{7,15},{8,16},{9,17... | collective-permute-start | bytes 589832 | tf_op jit(solution)/shard_map/ppermute | solution.py:62
  105.4 1.3 copy-start.5
  105.4 20.4 %collective-permute-start.11 = (bf16[1,384,256]{2,1,0:T(8,128)(2,1)S(1)}, bf16[1,384,256]{2,1,0:T(8,128)(2,1)}, u32[]{:S(2)}, u32[]{:S(2)}) collective-permute-start(bf16[1,384,256]{2,1,0:T(8,128)(2,1)S(1)} %get-tuple-element.32), channel_id=1, source_target_pairs={{8,0},{9,1},{10,2},{11,3},{12,4},{13,5},{14,6},{15,7},{16,8},{17,9... | collective-permute-start | bytes 589832 | tf_op jit(solution)/shard_map/ppermute | solution.py:62
  106.8 27.2 %collective-permute-start.13 = (bf16[4,384,256]{2,1,0:T(8,128)(2,1)}, bf16[4,384,256]{2,1,0:T(8,128)(2,1)}, u32[]{:S(2)}, u32[]{:S(2)}) collective-permute-start(bf16[4,384,256]{2,1,0:T(8,128)(2,1)} %collective-permute-done.12), channel_id=1, source_target_pairs={{8,0},{9,1},{10,2},{11,3},{12,4},{13,5},{22,6},{23,7},{16,8},{17,9... | collective-permute-start | bytes 2359304 | tf_op jit(solution)/shard_map/ppermute | solution.py:67
  108.2 23.9 %copy-start.12 = (f32[5,256]{1,0:T(8,128)S(1)}, f32[5,256]{1,0:T(8,128)}, u32[]{:S(2)}) copy-start(f32[5,256]{1,0:T(8,128)} %gain.3) | copy-start | bytes 15364
  108.2 23.9 %copy-start.13 = (f32[5,256]{1,0:T(8,128)S(1)}, f32[5,256]{1,0:T(8,128)}, u32[]{:S(2)}) copy-start(f32[5,256]{1,0:T(8,128)} %shift_term.3) | copy-start | bytes 15364
  123.7 4.1 %copy-start.11 = (bf16[1,384,256]{2,1,0:T(8,128)(2,1)}, bf16[1,384,256]{2,1,0:T(8,128)(2,1)S(1)}, u32[]{:S(2)}) copy-start(bf16[1,384,256]{2,1,0:T(8,128)(2,1)S(1)} %collective-permute-done.9.refs_7_) | copy-start | bytes 589828
  123.7 21.1 %collective-permute-start.17 = (bf16[3,384,256]{2,1,0:T(8,128)(2,1)}, bf16[3,384,256]{2,1,0:T(8,128)(2,1)}, u32[]{:S(2)}, u32[]{:S(2)}) collective-permute-start(bf16[3,384,256]{2,1,0:T(8,128)(2,1)} %collective-permute-done.16), channel_id=1, source_target_pairs={{0,4},{5,5},{2,6},{7,7},{12,8},{1,9},{14,10},{3,11},{8,12},{13,13}... | collective-permute-start | bytes 1769480 | tf_op jit(solution)/shard_map/ppermute | solution.py:67
  125.9 20.5 %collective-permute-start.20 = (bf16[3,384,256]{2,1,0:T(8,128)(2,1)}, bf16[3,384,256]{2,1,0:T(8,128)(2,1)}, u32[]{:S(2)}, u32[]{:S(2)}) collective-permute-start(bf16[3,384,256]{2,1,0:T(8,128)(2,1)} %collective-permute-done.19), channel_id=1, source_target_pairs={{4,0},{1,1},{6,2},{3,3},{0,4},{13,5},{2,6},{15,7},{12,8},{9,9},{14... | collective-permute-start | bytes 1769480 | tf_op jit(solution)/shard_map/ppermute | solution.py:67
  127.8 6.2 %copy-start.6 = (bf16[4,384,256]{2,1,0:T(8,128)(2,1)}, bf16[4,384,256]{2,1,0:T(8,128)(2,1)S(1)}, u32[]{:S(2)}) copy-start(bf16[4,384,256]{2,1,0:T(8,128)(2,1)S(1)} %collective-permute-done.4.refs_3_) | copy-start | bytes 2359300
  127.8 17.0 %collective-permute-start.15 = (bf16[2,384,256]{2,1,0:T(8,128)(2,1)S(1)}, bf16[2,384,256]{2,1,0:T(8,128)(2,1)S(1)}, u32[]{:S(2)}, u32[]{:S(2)}) collective-permute-start(bf16[2,384,256]{2,1,0:T(8,128)(2,1)S(1)} %get-tuple-element.35), channel_id=1, source_target_pairs={{0,6},{1,7},{2,8},{3,9},{4,10},{5,11},{6,12},{7,13},{8,14},{9,15},... | collective-permute-start | bytes 1179656 | tf_op jit(solution)/shard_map/ppermute | solution.py:62
  130.8 14.0 %collective-permute-start.21 = (bf16[2,384,256]{2,1,0:T(8,128)(2,1)S(1)}, bf16[2,384,256]{2,1,0:T(8,128)(2,1)S(1)}, u32[]{:S(2)}, u32[]{:S(2)}) collective-permute-start(bf16[2,384,256]{2,1,0:T(8,128)(2,1)S(1)} %get-tuple-element.40), channel_id=1, source_target_pairs={{6,0},{7,1},{8,2},{9,3},{10,4},{11,5},{12,6},{13,7},{14,8},{15,9},... | collective-permute-start | bytes 1179656 | tf_op jit(solution)/shard_map/ppermute | solution.py:62
  144.8 1.6 copy-start.7
  144.8 1.6 copy-start.8

commit v4 on v3

--- a/solution.py
+++ b/solution.py
@@ -275,8 +275,21 @@
             preferred_element_type=jnp.float32,
         )
     if last:
-        pooled, project_gain, project_bias, out = refs[place:]
-        out[0] = activate(total + pooled[...], project_gain[...], project_bias[...])
+        pooled, project_gain, project_bias, slots, out, cells = refs[place:]
+        width = total.shape[0]
+        pixels = cells.shape[0]
+        cells[pl.ds(pl.multiple_of(row * width, width), width)] = activate(
+            total + pooled[...], project_gain[...], project_bias[...]
+        )
+
+        @pl.when(row == pl.num_programs(0) - 1)
+        def _():
+            for start in range(0, pixels, width):
+                place_of = lax.broadcasted_iota(jnp.int32, (width, pixels), 1)
+                picked = jnp.where(slots[start : start + width] == place_of, 1.0, 0.0)
+                out[start : start + width] = jnp.dot(
+                    picked.astype(jnp.bfloat16), cells[...], preferred_element_type=jnp.float32
+                ).astype(jnp.bfloat16)
     else:
         refs[place][0] = total
 
@@ -311,17 +324,21 @@
                         functools.partial(lambda n, r: (jnp.maximum(r - n, 0), 0, 0), near_count),
                     )
                 )
-    out_type = jnp.float32
+    out_spec, scratch = block, []
+    out_type = jax.ShapeDtypeStruct((row_count, width, depth), jnp.float32)
     if tail is not None:
         operands += list(tail)
         in_specs += [whole(array) for array in tail]
-        out_type = jnp.bfloat16
+        out_type = jax.ShapeDtypeStruct((row_count * width, depth), jnp.bfloat16)
+        out_spec = pl.BlockSpec((row_count * width, depth), lambda r: (0, 0))
+        scratch = [pltpu.VMEM((row_count * width, depth), jnp.bfloat16)]
     return pl.pallas_call(
         functools.partial(join_body, plan, remainders, tail is not None),
         grid=(row_count,),
         in_specs=in_specs,
-        out_specs=block,
-        out_shape=jax.ShapeDtypeStruct((row_count, width, depth), out_type),
+        out_specs=out_spec,
+        out_shape=out_type,
+        scratch_shapes=scratch,
         compiler_params=pltpu.CompilerParams(vmem_limit_bytes=wide_limit),
         cost_estimate=small_cost,
     )(*operands)
@@ -380,13 +397,11 @@
     pool_projected = jnp.dot(pool_branch, w_project[4 * depth :], preferred_element_type=jnp.float32)
 
     base = join((2, 1), base, centre, arrived, w_project, branch_gain, branch_bias)
-    tail = (pool_projected, project_gain[None, :], project_bias[None, :])
-    projected = join((0,), base, centre, arrived, w_project, branch_gain, branch_bias, tail)
-
     pixels = row_count * width_local
     per_peer = pixels // device_count
-    slots = pixel_order.reshape(pixels)
-    outgoing = jnp.take(projected.reshape(pixels, depth), slots, axis=0)
+    slots = pixel_order.reshape(pixels, 1)
+    tail = (pool_projected, project_gain[None, :], project_bias[None, :], slots)
+    outgoing = join((0,), base, centre, arrived, w_project, branch_gain, branch_bias, tail)
     outgoing = outgoing.reshape(device_count, per_peer, depth)
     owned = lax.all_to_all(outgoing, ("band", "sample"), split_axis=0, concat_axis=0, tiled=True)
     return owned.reshape(device_count * per_peer, depth)

time: 202 us -> 202 us (level)
  starting transfers between devices: 71.4 us -> 82.1 us
  blocking collectives: 40.7 us -> 32.8 us
  local copies, waits for them, and re-layouts: 15 us -> 12.1 us
  Pallas kernels: 53.4 us -> 56.2 us
    all_to_all x1, blocking collectives: 40.7 us -> 32.8 us  [shards(): lax.all_to_all(outgoing, ('band', 'sample'), split_axis=0, concat_axis=0,...]
    ppermute x12, starting transfers between devices: 50.8 us -> 58.3 us  [passed_along(): array = lax.ppermute(array, ('band', 'sample'), first)]
    gather x2 -> x0, local copies, waits for them, and re-layouts: 6.35 us -> none  [shards(): outgoing = jnp.take(projected.reshape(pixels, depth), slots, axis=0)]
    ppermute x4, starting transfers between devices: 16.1 us -> 19.2 us  [passed_along(): array = lax.ppermute(array, ('band', 'sample'), second)]
    pallas_call x2, Pallas kernels: 13.6 us -> 16.3 us  [join(): pl.pallas_call(functools.partial(join_body, plan, remainders, tail is not...]
    unnamed x31 -> x36, local copies, waits for them, and re-layouts: 5.89 us -> 8.25 us
  transfers between devices with their start and end apart: 22 -> 22, of which waited for: 8 -> 6; matrix products, arithmetic and copies ran while one was open for 1% -> 2% of each run, Pallas kernels for 22% -> 22%
where the time goes in v4:
time: 202 us; the launch traced here: 201 us
  starting transfers between devices  82.1 us (41%)
  Pallas kernels  56.2 us (28%)
  blocking collectives  32.8 us (16%)
  waiting for transfers between devices  15 us (7%)
  local copies, waits for them, and re-layouts  12.1 us (6%)
    ppermute x12, starting transfers between devices, passed_along(): array = lax.ppermute(array, ('band', 'sample'), first)  58.3 us
    all_to_all x1, blocking collectives, shards(): lax.all_to_all(outgoing, ('band', 'sample'), split_axis=0, concat_axis=0,...  32.8 us
    pallas_call x6, Pallas kernels, row_taps(): pl.pallas_call(functools.partial(taps_body, plan, row_count, len(tokens))...  24.5 us
    ppermute x4, starting transfers between devices, passed_along(): array = lax.ppermute(array, ('band', 'sample'), second)  19.2 us
    pallas_call x2, Pallas kernels, join(): pl.pallas_call(functools.partial(join_body, plan, remainders, tail is not...  16.3 us
    pallas_call x1, Pallas kernels, own_rows(): pl.pallas_call(functools.partial(own_body, plan, point_operands is not No...  15.4 us
    ppermute x5, waiting for transfers between devices, total_over_devices(): lax.ppermute(values, axis, [(i, i ^ step) for i in range(size)])  9.33 us
    unnamed x36, local copies, waits for them, and re-layouts  8.25 us
  transfers between devices with their start and end apart: 22, of which 6 were waited for; matrix products, arithmetic and copies ran while one was open for 2% of the time, Pallas kernels for 22%

profile of v4, /device:TPU:0, one launch (start us, length us, event | category | flops | bytes accessed | tf_op | source)
XLA Modules:
  0.0 201.2 jit_solution(249027970434657223)
XLA Ops:
  0.0 1.4 fusion.10
  1.4 0.1 pad_maximum_fusion
  1.5 0.5 collective-permute-start
  2.0 0.5 copy-done.2
  2.5 0.7 convert_reduce_fusion
  3.2 0.5 collective-permute-start.3
  3.7 0.8 collective-permute-done.3
  4.5 2.8 %collective-permute-start.6 = (f32[1024]{0:T(1024)S(1)}, f32[1024]{0:T(1024)S(1)}, u32[]{:S(2)}, u32[]{:S(2)}) collective-permute-start(f32[1024]{0:T(1024)S(1)} %add.18.refs_1_), channel_id=1, source_target_pairs={{0,2},{2,0},{4,6},{6,4},{8,10},{10,8},{12,14},{14,12},{16,18},{18,... | collective-permute-start | bytes 12296 | tf_op jit(solution)/shard_map/ppermute | solution.py:81
  7.3 1.6 collective-permute-done.6
  8.9 0.1 fusion.11
  9.0 5.4 %copy-done.1 = bf16[3,3,3,1024,256]{4,3,2,1,0:T(8,128)(2,1)S(1)} copy-done((bf16[3,3,3,1024,256]{4,3,2,1,0:T(8,128)(2,1)S(1)}, bf16[3,3,3,1024,256]{4,3,2,1,0:T(8,128)(2,1)}, u32[]{:S(2)}) %copy-start.1) | copy-done | bytes 14155800
  14.4 4.0 %shard_map.103 = (bf16[4,384,256]{2,1,0:T(8,128)(2,1)S(1)}, bf16[1,384,256]{2,1,0:T(8,128)(2,1)S(1)}) custom-call(bf16[5,384,1024]{2,1,0:T(8,128)(2,1)S(1)} %copy-done.2, bf16[5,48,1024]{2,1,0:T(8,128)(2,1)S(1)} %get-tuple-element.46.before_ref, bf16[5,48,1024]{2,1,0:T(8,128)(2,1)S(1)} %get-tuple-element.45.after_ref, ...), custom_call_target="tpu_custom_call" | custom-call | flops 1024 | bytes 1024 | tf_op jit(solution)/shard_map/pallas_call | solution.py:164
  18.4 3.9 %collective-permute-start.7 = (bf16[4,384,256]{2,1,0:T(8,128)(2,1)S(1)}, bf16[4,384,256]{2,1,0:T(8,128)(2,1)}, u32[]{:S(2)}, u32[]{:S(2)}) collective-permute-start(bf16[4,384,256]{2,1,0:T(8,128)(2,1)S(1)} %get-tuple-element.30), channel_id=1, source_target_pairs={{0,2},{1,3},{2,4},{3,5},{4,6},{5,7},{6,0},{7,1},{8,10},{9,11},{10,... | collective-permute-start | bytes 2359304 | tf_op jit(solution)/shard_map/ppermute | solution.py:62
  22.3 4.1 %shard_map.100 = (bf16[1,384,256]{2,1,0:T(8,128)(2,1)S(1)}, bf16[4,384,256]{2,1,0:T(8,128)(2,1)S(1)}) custom-call(bf16[5,384,1024]{2,1,0:T(8,128)(2,1)S(1)} %copy-done.2, bf16[5,48,1024]{2,1,0:T(8,128)(2,1)S(1)} %get-tuple-element.46.before_ref, bf16[5,48,1024]{2,1,0:T(8,128)(2,1)S(1)} %get-tuple-element.45.after_ref, bf16[3,3,3,1024,256]{4,3,2,1,0:T(8,128)(2,1)S(1)} %copy-done.1), custom_call_target="tpu_custom_call" | custom-call | flops 1024 | bytes 1024 | tf_op jit(solution)/shard_map/pallas_call | solution.py:164
  26.4 5.4 %collective-permute-start.2 = (bf16[1,384,256]{2,1,0:T(8,128)(2,1)S(1)}, bf16[1,384,256]{2,1,0:T(8,128)(2,1)S(1)}, u32[]{:S(2)}, u32[]{:S(2)}) collective-permute-start(bf16[1,384,256]{2,1,0:T(8,128)(2,1)S(1)} %get-tuple-element.26), channel_id=1, source_target_pairs={{0,16},{1,17},{2,18},{3,19},{4,20},{5,21},{6,22},{7,23},{8,24},{9,... | collective-permute-start | bytes 589832 | tf_op jit(solution)/shard_map/ppermute | solution.py:62
  31.8 0.7 collective-permute-start.10
  32.5 3.3 %collective-permute-done.10 = f32[1024]{0:T(1024)S(1)} collective-permute-done((f32[1024]{0:T(1024)S(1)}, f32[1024]{0:T(1024)S(1)}, u32[]{:S(2)}, u32[]{:S(2)}) %collective-permute-start.10) | collective-permute-done | bytes 4128 | tf_op jit(solution)/shard_map/ppermute | solution.py:81
  35.9 3.6 %collective-permute-done.14 = f32[1024]{0:T(1024)S(1)} collective-permute-done((f32[1024]{0:T(1024)S(1)}, f32[1024]{0:T(1024)S(1)}, u32[]{:S(2)}, u32[]{:S(2)}) %collective-permute-start.14) | collective-permute-done | bytes 4128 | tf_op jit(solution)/shard_map/ppermute | solution.py:81
  39.5 4.2 %shard_map.106 = (bf16[2,384,256]{2,1,0:T(8,128)(2,1)S(1)}, bf16[3,384,256]{2,1,0:T(8,128)(2,1)S(1)}) custom-call(bf16[5,384,1024]{2,1,0:T(8,128)(2,1)S(1)} %copy-done.2, bf16[5,48,1024]{2,1,0:T(8,128)(2,1)S(1)} %get-tuple-element.46.before_ref, bf16[5,48,1024]{2,1,0:T(8,128)(2,1)S(1)} %get-tuple-element.45.after_ref, ...), custom_call_target="tpu_custom_call" | custom-call | flops 1024 | bytes 1024 | tf_op jit(solution)/shard_map/pallas_call | solution.py:164
  43.6 1.5 collective-permute-start.16
  45.1 4.1 %shard_map.102 = (bf16[4,384,256]{2,1,0:T(8,128)(2,1)S(1)}, bf16[1,384,256]{2,1,0:T(8,128)(2,1)S(1)}) custom-call(bf16[5,384,1024]{2,1,0:T(8,128)(2,1)S(1)} %copy-done.2, bf16[5,48,1024]{2,1,0:T(8,128)(2,1)S(1)} %get-tuple-element.46.before_ref, bf16[5,48,1024]{2,1,0:T(8,128)(2,1)S(1)} %get-tuple-element.45.after_ref, ...), custom_call_target="tpu_custom_call" | custom-call | flops 1024 | bytes 1024 | tf_op jit(solution)/shard_map/pallas_call | solution.py:164
  49.2 4.0 %shard_map.104 = (bf16[1,384,256]{2,1,0:T(8,128)(2,1)S(1)}, bf16[4,384,256]{2,1,0:T(8,128)(2,1)S(1)}) custom-call(bf16[5,384,1024]{2,1,0:T(8,128)(2,1)S(1)} %copy-done.2, bf16[5,48,1024]{2,1,0:T(8,128)(2,1)S(1)} %get-tuple-element.46.before_ref, bf16[5,48,1024]{2,1,0:T(8,128)(2,1)S(1)} %get-tuple-element.45.after_ref, ...), custom_call_target="tpu_custom_call" | custom-call | flops 1024 | bytes 1024 | tf_op jit(solution)/shard_map/pallas_call | solution.py:164
  53.2 2.9 %collective-permute-start.1 = (bf16[4,384,256]{2,1,0:T(8,128)(2,1)S(1)}, bf16[4,384,256]{2,1,0:T(8,128)(2,1)S(1)}, u32[]{:S(2)}, u32[]{:S(2)}) collective-permute-start(bf16[4,384,256]{2,1,0:T(8,128)(2,1)S(1)} %get-tuple-element.23), channel_id=1, source_target_pairs={{0,14},{1,15},{2,16},{3,17},{4,18},{5,19},{6,20},{7,21},{8,22},{9,... | collective-permute-start | bytes 2359304 | tf_op jit(solution)/shard_map/ppermute | solution.py:62
  56.1 1.3 collective-permute-start.5
  57.4 1.6 collective-permute-start.12
  59.0 4.2 %shard_map.107 = (bf16[3,384,256]{2,1,0:T(8,128)(2,1)S(1)}, bf16[2,384,256]{2,1,0:T(8,128)(2,1)S(1)}) custom-call(bf16[5,384,1024]{2,1,0:T(8,128)(2,1)S(1)} %copy-done.2, bf16[5,48,1024]{2,1,0:T(8,128)(2,1)S(1)} %get-tuple-element.46.before_ref, bf16[5,48,1024]{2,1,0:T(8,128)(2,1)S(1)} %get-tuple-element.45.after_ref, ...), custom_call_target="tpu_custom_call" | custom-call | flops 1024 | bytes 1024 | tf_op jit(solution)/shard_map/pallas_call | solution.py:164
  63.2 2.3 %collective-permute-done.5.refs_4_ = bf16[1,384,256]{2,1,0:T(8,128)(2,1)S(1)} collective-permute-done((bf16[1,384,256]{2,1,0:T(8,128)(2,1)S(1)}, bf16[1,384,256]{2,1,0:T(8,128)(2,1)S(1)}, u32[]{:S(2)}, u32[]{:S(2)}) %collective-permute-start.5) | collective-permute-done | bytes 196640 | tf_op jit(solution)/shard_map/ppermute | solution.py:62
  65.5 1.3 collective-permute-start.19
  66.8 1.3 collective-permute-start.4
  68.1 9.9 %collective-permute-start.8 = (bf16[4,384,256]{2,1,0:T(8,128)(2,1)}, bf16[4,384,256]{2,1,0:T(8,128)(2,1)S(1)}, u32[]{:S(2)}, u32[]{:S(2)}) collective-permute-start(bf16[4,384,256]{2,1,0:T(8,128)(2,1)} %collective-permute-done.7), channel_id=1, source_target_pairs={{2,10},{3,11},{4,12},{5,13},{6,14},{7,15},{0,16},{1,17},{10,18},{1... | collective-permute-start | bytes 2359304 | tf_op jit(solution)/shard_map/ppermute | solution.py:67
  78.1 1.3 collective-permute-start.13
  79.4 26.1 %collective-permute-start.9 = (bf16[1,384,256]{2,1,0:T(8,128)(2,1)S(1)}, bf16[1,384,256]{2,1,0:T(8,128)(2,1)S(1)}, u32[]{:S(2)}, u32[]{:S(2)}) collective-permute-start(bf16[1,384,256]{2,1,0:T(8,128)(2,1)S(1)} %get-tuple-element.31), channel_id=1, source_target_pairs={{0,8},{1,9},{2,10},{3,11},{4,12},{5,13},{6,14},{7,15},{8,16},{9,17... | collective-permute-start | bytes 589832 | tf_op jit(solution)/shard_map/ppermute | solution.py:62
  105.6 1.4 collective-permute-start.11
  107.0 15.4 %shard_map.101 = (f32[5,384,256]{2,1,0:T(8,128)}, f32[5,384,256]{2,1,0:T(8,128)}, f32[5,384,256]{2,1,0:T(8,128)}, f32[5,384,256]{2,1,0:T(8,128)}) custom-call(bf16[5,384,1024]{2,1,0:T(8,128)(2,1)} %x_ref.13, bf16[5,48,1024]{2,1,0:T(8,128)(2,1)} %copy-done.4, bf16[5,48,1024]{2,1,0:T(8,128)(2,1)} %copy-done.3, bf16[3,3,3,1024,256]{4,3,2,1,0:T(8,128)(2,1)} %refs_0_.13, ...), custom_call_target="tpu_custom_call" | custom-call | flops 1024 | bytes 1024 | tf_op jit(solution)/shard_map/pallas_call | solution.py:241
  122.5 1.3 collective-permute-start.17
  123.8 6.6 %collective-permute-start.20 = (bf16[3,384,256]{2,1,0:T(8,128)(2,1)}, bf16[3,384,256]{2,1,0:T(8,128)(2,1)S(1)}, u32[]{:S(2)}, u32[]{:S(2)}) collective-permute-start(bf16[3,384,256]{2,1,0:T(8,128)(2,1)} %collective-permute-done.19), channel_id=1, source_target_pairs={{4,0},{1,1},{6,2},{3,3},{0,4},{13,5},{2,6},{15,7},{12,8},{9,9},{14... | collective-permute-start | bytes 1769480 | tf_op jit(solution)/shard_map/ppermute | solution.py:67
  130.5 10.2 %collective-permute-start.15 = (bf16[2,384,256]{2,1,0:T(8,128)(2,1)S(1)}, bf16[2,384,256]{2,1,0:T(8,128)(2,1)}, u32[]{:S(2)}, u32[]{:S(2)}) collective-permute-start(bf16[2,384,256]{2,1,0:T(8,128)(2,1)S(1)} %get-tuple-element.35), channel_id=1, source_target_pairs={{0,6},{1,7},{2,8},{3,9},{4,10},{5,11},{6,12},{7,13},{8,14},{9,15},... | collective-permute-start | bytes 1179656 | tf_op jit(solution)/shard_map/ppermute | solution.py:62
  140.7 1.5 collective-permute-start.21
  142.2 1.3 copy.13
  143.5 1.8 fusion.4.refs_5_
  145.4 7.6 %shard_map.105.base_ref = f32[5,384,256]{2,1,0:T(8,128)} custom-call(f32[5,384,256]{2,1,0:T(8,128)} %get-tuple-element.24.base_ref, bf16[1280,256]{1,0:T(8,128)(2,1)} %w_project.3, f32[5,256]{1,0:T(8,128)} %gain.3, f32[5,256]{1,0:T(8,128)} %shift_term.3, f32[5,384,256]{2,1,0:T(8,128)} %get-tuple-element.25.refs_0_, bf16[1,384,256]{2,1,0:T(8,128)(2,1)} %copy-done.10, ...), custom_call_target="tpu_custom_call" | custom-call | flops 1024 | bytes 1024 | tf_op jit(solution)/shard_map/pallas_call | solution.py:335
  153.0 3.3 %collective-permute-done.15.refs_1_ = bf16[2,384,256]{2,1,0:T(8,128)(2,1)} collective-permute-done((bf16[2,384,256]{2,1,0:T(8,128)(2,1)S(1)}, bf16[2,384,256]{2,1,0:T(8,128)(2,1)}, u32[]{:S(2)}, u32[]{:S(2)}) %collective-permute-start.15) | collective-permute-done | bytes 393248 | tf_op jit(solution)/shard_map/ppermute | solution.py:62
  156.3 0.8 copy-done.8
  157.1 0.2 copy-done.9
  157.3 8.6 %shard_map.108 = bf16[1920,256]{1,0:T(8,128)(2,1)} custom-call(f32[5,384,256]{2,1,0:T(8,128)} %shard_map.105.base_ref, bf16[1280,256]{1,0:T(8,128)(2,1)} %w_project.3, f32[5,256]{1,0:T(8,128)} %gain.3, f32[5,256]{1,0:T(8,128)} %shift_term.3, f32[5,384,256]{2,1,0:T(8,128)} %get-tuple-element.34.refs_0_, bf16[2,384,256]{2,1,0:T(8,128)(2,1)} %collective-permute-done.15.refs_1_, ...), custom_call_target="tpu_custom_call" | custom-call | flops 1024 | bytes 1024 | tf_op jit(solution)/shard_map/pallas_call | solution.py:335
  166.0 1.3 reshape.18
  167.3 32.8 %all_to_all.5 = bf16[32,60,256]{2,1,0:T(8,128)(2,1)S(1)} all-to-all(bf16[32,60,256]{2,1,0:T(8,128)(2,1)S(1)} %reshape.18), channel_id=1, replica_groups=mesh['band'=16,'sample'=2] {'band','sample'}, dimensions={0} | all-to-all | bytes 1966080 | tf_op jit(solution)/shard_map/all_to_all | solution.py:406
  200.1 1.1 reshape.19
  (55 shorter events, 0.2 us)
Async XLA Ops:
  0.0 143.5 %copy-start = (bf16[1024,256]{1,0:T(8,128)(2,1)S(1)}, bf16[1024,256]{1,0:T(8,128)(2,1)}, u32[]{:S(2)}) copy-start(bf16[1024,256]{1,0:T(8,128)(2,1)} %param.13) | copy-start | bytes 1572868
  0.0 2.5 %copy-start.2 = (bf16[5,384,1024]{2,1,0:T(8,128)(2,1)S(1)}, bf16[5,384,1024]{2,1,0:T(8,128)(2,1)}, u32[]{:S(2)}) copy-start(bf16[5,384,1024]{2,1,0:T(8,128)(2,1)} %x_ref.13) | copy-start | bytes 11796484
  1.5 7.4 %collective-permute-start = (bf16[5,96,1024]{2,1,0:T(8,128)(2,1)S(1)}, bf16[5,96,1024]{2,1,0:T(8,128)(2,1)S(1)}, u32[]{:S(2)}, u32[]{:S(2)}) collective-permute-start(bf16[5,96,1024]{2,1,0:T(8,128)(2,1)S(1)} %pad_maximum_fusion), channel_id=1, source_target_pairs={{0,1},{1,0},{2,3},{3,2},{4,5},{5,4},{6,7},{7,6},{8,9},{9,8},{10,11... | collective-permute-start | bytes 2949128 | tf_op jit(solution)/shard_map/ppermute | solution.py:32
  3.2 1.3 collective-permute-start.3
  4.5 4.4 %collective-permute-start.6 = (f32[1024]{0:T(1024)S(1)}, f32[1024]{0:T(1024)S(1)}, u32[]{:S(2)}, u32[]{:S(2)}) collective-permute-start(f32[1024]{0:T(1024)S(1)} %add.18.refs_1_), channel_id=1, source_target_pairs={{0,2},{2,0},{4,6},{6,4},{8,10},{10,8},{12,14},{14,12},{16,18},{18,... | collective-permute-start | bytes 12296 | tf_op jit(solution)/shard_map/ppermute | solution.py:81
  9.0 50.0 %copy-start.3 = (bf16[5,48,1024]{2,1,0:T(8,128)(2,1)}, bf16[5,48,1024]{2,1,0:T(8,128)(2,1)S(1)}, u32[]{:S(2)}) copy-start(bf16[5,48,1024]{2,1,0:T(8,128)(2,1)S(1)} %get-tuple-element.45.after_ref) | copy-start | bytes 1474564
  9.0 50.0 %copy-start.4 = (bf16[5,48,1024]{2,1,0:T(8,128)(2,1)}, bf16[5,48,1024]{2,1,0:T(8,128)(2,1)S(1)}, u32[]{:S(2)}) copy-start(bf16[5,48,1024]{2,1,0:T(8,128)(2,1)S(1)} %get-tuple-element.46.before_ref) | copy-start | bytes 1474564
  9.0 5.4 %copy-start.1 = (bf16[3,3,3,1024,256]{4,3,2,1,0:T(8,128)(2,1)S(1)}, bf16[3,3,3,1024,256]{4,3,2,1,0:T(8,128)(2,1)}, u32[]{:S(2)}) copy-start(bf16[3,3,3,1024,256]{4,3,2,1,0:T(8,128)(2,1)} %refs_0_.13) | copy-start | bytes 42467332
  18.4 49.7 %collective-permute-start.7 = (bf16[4,384,256]{2,1,0:T(8,128)(2,1)S(1)}, bf16[4,384,256]{2,1,0:T(8,128)(2,1)}, u32[]{:S(2)}, u32[]{:S(2)}) collective-permute-start(bf16[4,384,256]{2,1,0:T(8,128)(2,1)S(1)} %get-tuple-element.30), channel_id=1, source_target_pairs={{0,2},{1,3},{2,4},{3,5},{4,6},{5,7},{6,0},{7,1},{8,10},{9,11},{10,... | collective-permute-start | bytes 2359304 | tf_op jit(solution)/shard_map/ppermute | solution.py:62
  26.4 31.0 %collective-permute-start.2 = (bf16[1,384,256]{2,1,0:T(8,128)(2,1)S(1)}, bf16[1,384,256]{2,1,0:T(8,128)(2,1)S(1)}, u32[]{:S(2)}, u32[]{:S(2)}) collective-permute-start(bf16[1,384,256]{2,1,0:T(8,128)(2,1)S(1)} %get-tuple-element.26), channel_id=1, source_target_pairs={{0,16},{1,17},{2,18},{3,19},{4,20},{5,21},{6,22},{7,23},{8,24},{9,... | collective-permute-start | bytes 589832 | tf_op jit(solution)/shard_map/ppermute | solution.py:62
  31.8 4.0 %collective-permute-start.10 = (f32[1024]{0:T(1024)S(1)}, f32[1024]{0:T(1024)S(1)}, u32[]{:S(2)}, u32[]{:S(2)}) collective-permute-start(f32[1024]{0:T(1024)S(1)} %add.19.refs_1_), channel_id=1, source_target_pairs={{0,4},{2,6},{4,0},{6,2},{8,12},{10,14},{12,8},{14,10},{16,20},{18,... | collective-permute-start | bytes 12296 | tf_op jit(solution)/shard_map/ppermute | solution.py:81
  35.9 3.6 %collective-permute-start.14 = (f32[1024]{0:T(1024)S(1)}, f32[1024]{0:T(1024)S(1)}, u32[]{:S(2)}, u32[]{:S(2)}) collective-permute-start(f32[1024]{0:T(1024)S(1)} %add.20.refs_1_), channel_id=1, source_target_pairs={{0,8},{2,10},{4,12},{6,14},{8,0},{10,2},{12,4},{14,6},{16,24},{18,... | collective-permute-start | bytes 12296 | tf_op jit(solution)/shard_map/ppermute | solution.py:81
  43.6 23.2 %collective-permute-start.16 = (bf16[3,384,256]{2,1,0:T(8,128)(2,1)S(1)}, bf16[3,384,256]{2,1,0:T(8,128)(2,1)}, u32[]{:S(2)}, u32[]{:S(2)}) collective-permute-start(bf16[3,384,256]{2,1,0:T(8,128)(2,1)S(1)} %get-tuple-element.36), channel_id=1, source_target_pairs={{0,0},{1,5},{2,2},{3,7},{4,12},{5,1},{6,14},{7,3},{8,8},{9,13},{10... | collective-permute-start | bytes 1769480 | tf_op jit(solution)/shard_map/ppermute | solution.py:62
  45.1 11.0 %collective-permute-start.18 = (f32[1024]{0:T(1024)S(1)}, f32[1024]{0:T(1024)S(1)}, u32[]{:S(2)}, u32[]{:S(2)}) collective-permute-start(f32[1024]{0:T(1024)S(1)} %add.21.refs_1_), channel_id=1, source_target_pairs={{0,16},{2,18},{4,20},{6,22},{8,24},{10,26},{12,28},{14,30},{16,0},... | collective-permute-start | bytes 12296 | tf_op jit(solution)/shard_map/ppermute | solution.py:81
  53.2 52.3 %collective-permute-start.1 = (bf16[4,384,256]{2,1,0:T(8,128)(2,1)S(1)}, bf16[4,384,256]{2,1,0:T(8,128)(2,1)S(1)}, u32[]{:S(2)}, u32[]{:S(2)}) collective-permute-start(bf16[4,384,256]{2,1,0:T(8,128)(2,1)S(1)} %get-tuple-element.23), channel_id=1, source_target_pairs={{0,14},{1,15},{2,16},{3,17},{4,18},{5,19},{6,20},{7,21},{8,22},{9,... | collective-permute-start | bytes 2359304 | tf_op jit(solution)/shard_map/ppermute | solution.py:62
  56.1 9.4 %collective-permute-start.5 = (bf16[1,384,256]{2,1,0:T(8,128)(2,1)S(1)}, bf16[1,384,256]{2,1,0:T(8,128)(2,1)S(1)}, u32[]{:S(2)}, u32[]{:S(2)}) collective-permute-start(bf16[1,384,256]{2,1,0:T(8,128)(2,1)S(1)} %get-tuple-element.28), channel_id=1, source_target_pairs={{16,0},{17,1},{18,2},{19,3},{20,4},{21,5},{22,6},{23,7},{24,8},{25... | collective-permute-start | bytes 589832 | tf_op jit(solution)/shard_map/ppermute | solution.py:62
  57.4 1.6 copy-start.10
  57.4 20.6 %collective-permute-start.12 = (bf16[4,384,256]{2,1,0:T(8,128)(2,1)S(1)}, bf16[4,384,256]{2,1,0:T(8,128)(2,1)}, u32[]{:S(2)}, u32[]{:S(2)}) collective-permute-start(bf16[4,384,256]{2,1,0:T(8,128)(2,1)S(1)} %get-tuple-element.33), channel_id=1, source_target_pairs={{10,8},{11,9},{12,10},{13,11},{14,12},{15,13},{16,22},{17,23},{18,... | collective-permute-start | bytes 2359304 | tf_op jit(solution)/shard_map/ppermute | solution.py:62
  65.5 40.0 %copy-start.11 = (bf16[1,384,256]{2,1,0:T(8,128)(2,1)}, bf16[1,384,256]{2,1,0:T(8,128)(2,1)S(1)}, u32[]{:S(2)}) copy-start(bf16[1,384,256]{2,1,0:T(8,128)(2,1)S(1)} %collective-permute-done.5.refs_4_) | copy-start | bytes 589828
  65.5 13.8 %collective-permute-start.19 = (bf16[3,384,256]{2,1,0:T(8,128)(2,1)S(1)}, bf16[3,384,256]{2,1,0:T(8,128)(2,1)}, u32[]{:S(2)}, u32[]{:S(2)}) collective-permute-start(bf16[3,384,256]{2,1,0:T(8,128)(2,1)S(1)} %get-tuple-element.38), channel_id=1, source_target_pairs={{4,4},{5,1},{6,6},{7,3},{8,0},{9,13},{10,2},{11,15},{12,12},{13,9}... | collective-permute-start | bytes 1769480 | tf_op jit(solution)/shard_map/ppermute | solution.py:62
  66.8 63.7 %collective-permute-start.4 = (bf16[4,384,256]{2,1,0:T(8,128)(2,1)S(1)}, bf16[4,384,256]{2,1,0:T(8,128)(2,1)S(1)}, u32[]{:S(2)}, u32[]{:S(2)}) collective-permute-start(bf16[4,384,256]{2,1,0:T(8,128)(2,1)S(1)} %get-tuple-element.27), channel_id=1, source_target_pairs={{14,0},{15,1},{16,2},{17,3},{18,4},{19,5},{20,6},{21,7},{22,8},{23... | collective-permute-start | bytes 2359304 | tf_op jit(solution)/shard_map/ppermute | solution.py:62
  68.1 72.6 %collective-permute-start.8 = (bf16[4,384,256]{2,1,0:T(8,128)(2,1)}, bf16[4,384,256]{2,1,0:T(8,128)(2,1)S(1)}, u32[]{:S(2)}, u32[]{:S(2)}) collective-permute-start(bf16[4,384,256]{2,1,0:T(8,128)(2,1)} %collective-permute-done.7), channel_id=1, source_target_pairs={{2,10},{3,11},{4,12},{5,13},{6,14},{7,15},{0,16},{1,17},{10,18},{1... | collective-permute-start | bytes 2359304 | tf_op jit(solution)/shard_map/ppermute | solution.py:67
  78.1 67.3 %collective-permute-start.13 = (bf16[4,384,256]{2,1,0:T(8,128)(2,1)}, bf16[4,384,256]{2,1,0:T(8,128)(2,1)}, u32[]{:S(2)}, u32[]{:S(2)}) collective-permute-start(bf16[4,384,256]{2,1,0:T(8,128)(2,1)} %collective-permute-done.12), channel_id=1, source_target_pairs={{8,0},{9,1},{10,2},{11,3},{12,4},{13,5},{22,6},{23,7},{16,8},{17,9... | collective-permute-start | bytes 2359304 | tf_op jit(solution)/shard_map/ppermute | solution.py:67
  79.4 43.1 %collective-permute-start.9 = (bf16[1,384,256]{2,1,0:T(8,128)(2,1)S(1)}, bf16[1,384,256]{2,1,0:T(8,128)(2,1)S(1)}, u32[]{:S(2)}, u32[]{:S(2)}) collective-permute-start(bf16[1,384,256]{2,1,0:T(8,128)(2,1)S(1)} %get-tuple-element.31), channel_id=1, source_target_pairs={{0,8},{1,9},{2,10},{3,11},{4,12},{5,13},{6,14},{7,15},{8,16},{9,17... | collective-permute-start | bytes 589832 | tf_op jit(solution)/shard_map/ppermute | solution.py:62
  105.5 1.5 copy-start.5
  105.5 36.6 %copy-start.16 = (s32[5,384]{1,0:T(8,128)S(1)}, s32[5,384]{1,0:T(8,128)}, u32[]{:S(2)}) copy-start(s32[5,384]{1,0:T(8,128)} %param.19) | copy-start | bytes 23044
  105.6 38.0 %copy-start.14 = (f32[5,256]{1,0:T(8,128)S(1)}, f32[5,256]{1,0:T(8,128)}, u32[]{:S(2)}) copy-start(f32[5,256]{1,0:T(8,128)} %gain.3) | copy-start | bytes 15364
  105.6 38.0 %copy-start.15 = (f32[5,256]{1,0:T(8,128)S(1)}, f32[5,256]{1,0:T(8,128)}, u32[]{:S(2)}) copy-start(f32[5,256]{1,0:T(8,128)} %shift_term.3) | copy-start | bytes 15364
  105.6 18.2 %collective-permute-start.11 = (bf16[1,384,256]{2,1,0:T(8,128)(2,1)S(1)}, bf16[1,384,256]{2,1,0:T(8,128)(2,1)S(1)}, u32[]{:S(2)}, u32[]{:S(2)}) collective-permute-start(bf16[1,384,256]{2,1,0:T(8,128)(2,1)S(1)} %get-tuple-element.32), channel_id=1, source_target_pairs={{8,0},{9,1},{10,2},{11,3},{12,4},{13,5},{14,6},{15,7},{16,8},{17,9... | collective-permute-start | bytes 589832 | tf_op jit(solution)/shard_map/ppermute | solution.py:62
  122.5 19.7 %copy-start.12 = (bf16[1,384,256]{2,1,0:T(8,128)(2,1)}, bf16[1,384,256]{2,1,0:T(8,128)(2,1)S(1)}, u32[]{:S(2)}) copy-start(bf16[1,384,256]{2,1,0:T(8,128)(2,1)S(1)} %collective-permute-done.9.refs_7_) | copy-start | bytes 589828
  122.5 33.8 %collective-permute-start.17 = (bf16[3,384,256]{2,1,0:T(8,128)(2,1)}, bf16[3,384,256]{2,1,0:T(8,128)(2,1)S(1)}, u32[]{:S(2)}, u32[]{:S(2)}) collective-permute-start(bf16[3,384,256]{2,1,0:T(8,128)(2,1)} %collective-permute-done.16), channel_id=1, source_target_pairs={{0,4},{5,5},{2,6},{7,7},{12,8},{1,9},{14,10},{3,11},{8,12},{13,13}... | collective-permute-start | bytes 1769480 | tf_op jit(solution)/shard_map/ppermute | solution.py:67
  123.8 18.4 %copy-start.13 = (bf16[1,384,256]{2,1,0:T(8,128)(2,1)}, bf16[1,384,256]{2,1,0:T(8,128)(2,1)S(1)}, u32[]{:S(2)}) copy-start(bf16[1,384,256]{2,1,0:T(8,128)(2,1)S(1)} %collective-permute-done.11.refs_8_) | copy-start | bytes 589828
  123.8 32.5 %collective-permute-start.20 = (bf16[3,384,256]{2,1,0:T(8,128)(2,1)}, bf16[3,384,256]{2,1,0:T(8,128)(2,1)S(1)}, u32[]{:S(2)}, u32[]{:S(2)}) collective-permute-start(bf16[3,384,256]{2,1,0:T(8,128)(2,1)} %collective-permute-done.19), channel_id=1, source_target_pairs={{4,0},{1,1},{6,2},{3,3},{0,4},{13,5},{2,6},{15,7},{12,8},{9,9},{14... | collective-permute-start | bytes 1769480 | tf_op jit(solution)/shard_map/ppermute | solution.py:67
  130.5 14.9 %copy-start.6 = (bf16[4,384,256]{2,1,0:T(8,128)(2,1)}, bf16[4,384,256]{2,1,0:T(8,128)(2,1)S(1)}, u32[]{:S(2)}) copy-start(bf16[4,384,256]{2,1,0:T(8,128)(2,1)S(1)} %collective-permute-done.4.refs_3_) | copy-start | bytes 2359300
  130.5 25.8 %collective-permute-start.15 = (bf16[2,384,256]{2,1,0:T(8,128)(2,1)S(1)}, bf16[2,384,256]{2,1,0:T(8,128)(2,1)}, u32[]{:S(2)}, u32[]{:S(2)}) collective-permute-start(bf16[2,384,256]{2,1,0:T(8,128)(2,1)S(1)} %get-tuple-element.35), channel_id=1, source_target_pairs={{0,6},{1,7},{2,8},{3,9},{4,10},{5,11},{6,12},{7,13},{8,14},{9,15},... | collective-permute-start | bytes 1179656 | tf_op jit(solution)/shard_map/ppermute | solution.py:62
  140.7 1.5 copy-start.7
  140.7 15.6 %collective-permute-start.21 = (bf16[2,384,256]{2,1,0:T(8,128)(2,1)S(1)}, bf16[2,384,256]{2,1,0:T(8,128)(2,1)}, u32[]{:S(2)}, u32[]{:S(2)}) collective-permute-start(bf16[2,384,256]{2,1,0:T(8,128)(2,1)S(1)} %get-tuple-element.40), channel_id=1, source_target_pairs={{6,0},{7,1},{8,2},{9,3},{10,4},{11,5},{12,6},{13,7},{14,8},{15,9},... | collective-permute-start | bytes 1179656 | tf_op jit(solution)/shard_map/ppermute | solution.py:62
  156.3 0.8 copy-start.8
  156.3 1.0 copy-start.9

commit v5 on v4

--- a/solution.py
+++ b/solution.py
@@ -373,7 +373,9 @@
         ways = (near_way, far_way) if near_way.shape[0] < far_way.shape[0] else (far_way, near_way)
         part_way[branch, row_tap] = ways
 
-    totals, steps = total_over_devices(jnp.sum(features, axis=(0, 1), dtype=jnp.float32))
+    totals, steps = total_over_devices(
+        lax.optimization_barrier((jnp.sum(features, axis=(0, 1), dtype=jnp.float32), before))[0]
+    )
     order = ((2, 0), (2, 2), (1, 0), (1, 2), (0, 0), (0, 2))
     centre, base = {}, None
     for place, (branch, row_tap) in enumerate(order):

time: 202 us -> 199 us (0.985)
  starting transfers between devices: 82.1 us -> 79.7 us
    ppermute x12, starting transfers between devices: 58.3 us -> 54.9 us  [passed_along(): array = lax.ppermute(array, ('band', 'sample'), first)]
  transfers between devices with their start and end apart: 22 -> 22, of which waited for: 6 -> 7; matrix products, arithmetic and copies ran while one was open for 2% -> 2% of each run, Pallas kernels for 22% -> 22%
where the time goes in v5:
time: 199 us; the launch traced here: 198 us
  starting transfers between devices  79.7 us (40%)
  Pallas kernels  56.2 us (28%)
  blocking collectives  31.7 us (16%)
  waiting for transfers between devices  16 us (8%)
  local copies, waits for them, and re-layouts  11.8 us (6%)
    ppermute x12, starting transfers between devices, passed_along(): array = lax.ppermute(array, ('band', 'sample'), first)  54.9 us
    all_to_all x1, blocking collectives, shards(): lax.all_to_all(outgoing, ('band', 'sample'), split_axis=0, concat_axis=0,...  31.7 us
    pallas_call x6, Pallas kernels, row_taps(): pl.pallas_call(functools.partial(taps_body, plan, row_count, len(tokens))...  24.5 us
    ppermute x4, starting transfers between devices, passed_along(): array = lax.ppermute(array, ('band', 'sample'), second)  20.2 us
    pallas_call x2, Pallas kernels, join(): pl.pallas_call(functools.partial(join_body, plan, remainders, tail is not...  16.3 us
    pallas_call x1, Pallas kernels, own_rows(): pl.pallas_call(functools.partial(own_body, plan, point_operands is not No...  15.4 us
    ppermute x5, waiting for transfers between devices, total_over_devices(): lax.ppermute(values, axis, [(i, i ^ step) for i in range(size)])  9.33 us
    unnamed x36, local copies, waits for them, and re-layouts  7.9 us
  transfers between devices with their start and end apart: 22, of which 7 were waited for; matrix products, arithmetic and copies ran while one was open for 2% of the time, Pallas kernels for 22%

profile of v5, /device:TPU:0, one launch (start us, length us, event | category | flops | bytes accessed | tf_op | source)
XLA Modules:
  0.0 198.4 jit_solution(13568060925774240028)
XLA Ops:
  0.0 1.4 fusion.10
  1.4 0.1 pad_maximum_fusion
  1.5 0.5 collective-permute-start
  2.0 0.5 copy-done.2
  2.5 0.7 convert_reduce_fusion
  3.2 1.0 collective-permute-done
  4.3 0.4 collective-permute-start.3
  4.7 0.8 collective-permute-done.3
  5.5 2.8 %collective-permute-start.6 = (f32[1024]{0:T(1024)S(1)}, f32[1024]{0:T(1024)S(1)}, u32[]{:S(2)}, u32[]{:S(2)}) collective-permute-start(f32[1024]{0:T(1024)S(1)} %add.18.refs_1_), channel_id=1, source_target_pairs={{0,2},{2,0},{4,6},{6,4},{8,10},{10,8},{12,14},{14,12},{16,18},{18,... | collective-permute-start | bytes 12296 | tf_op jit(solution)/shard_map/ppermute | solution.py:81
  8.4 1.6 collective-permute-done.6
  10.0 5.0 %copy-done.1 = bf16[3,3,3,1024,256]{4,3,2,1,0:T(8,128)(2,1)S(1)} copy-done((bf16[3,3,3,1024,256]{4,3,2,1,0:T(8,128)(2,1)S(1)}, bf16[3,3,3,1024,256]{4,3,2,1,0:T(8,128)(2,1)}, u32[]{:S(2)}) %copy-start.1) | copy-done | bytes 14155800
  15.0 4.0 %shard_map.103 = (bf16[4,384,256]{2,1,0:T(8,128)(2,1)S(1)}, bf16[1,384,256]{2,1,0:T(8,128)(2,1)S(1)}) custom-call(bf16[5,384,1024]{2,1,0:T(8,128)(2,1)S(1)} %copy-done.2, bf16[5,48,1024]{2,1,0:T(8,128)(2,1)S(1)} %get-tuple-element.48.before_ref, bf16[5,48,1024]{2,1,0:T(8,128)(2,1)S(1)} %get-tuple-element.47.after_ref, ...), custom_call_target="tpu_custom_call" | custom-call | flops 1024 | bytes 1024 | tf_op jit(solution)/shard_map/pallas_call | solution.py:164
  19.0 3.9 %collective-permute-start.7 = (bf16[4,384,256]{2,1,0:T(8,128)(2,1)S(1)}, bf16[4,384,256]{2,1,0:T(8,128)(2,1)}, u32[]{:S(2)}, u32[]{:S(2)}) collective-permute-start(bf16[4,384,256]{2,1,0:T(8,128)(2,1)S(1)} %get-tuple-element.32), channel_id=1, source_target_pairs={{0,2},{1,3},{2,4},{3,5},{4,6},{5,7},{6,0},{7,1},{8,10},{9,11},{10,... | collective-permute-start | bytes 2359304 | tf_op jit(solution)/shard_map/ppermute | solution.py:62
  22.9 4.1 %shard_map.100 = (bf16[1,384,256]{2,1,0:T(8,128)(2,1)S(1)}, bf16[4,384,256]{2,1,0:T(8,128)(2,1)S(1)}) custom-call(bf16[5,384,1024]{2,1,0:T(8,128)(2,1)S(1)} %copy-done.2, bf16[5,48,1024]{2,1,0:T(8,128)(2,1)S(1)} %get-tuple-element.48.before_ref, bf16[5,48,1024]{2,1,0:T(8,128)(2,1)S(1)} %get-tuple-element.47.after_ref, bf16[3,3,3,1024,256]{4,3,2,1,0:T(8,128)(2,1)S(1)} %copy-done.1), custom_call_target="tpu_custom_call" | custom-call | flops 1024 | bytes 1024 | tf_op jit(solution)/shard_map/pallas_call | solution.py:164
  27.0 5.4 %collective-permute-start.2 = (bf16[1,384,256]{2,1,0:T(8,128)(2,1)S(1)}, bf16[1,384,256]{2,1,0:T(8,128)(2,1)S(1)}, u32[]{:S(2)}, u32[]{:S(2)}) collective-permute-start(bf16[1,384,256]{2,1,0:T(8,128)(2,1)S(1)} %get-tuple-element.27), channel_id=1, source_target_pairs={{0,16},{1,17},{2,18},{3,19},{4,20},{5,21},{6,22},{7,23},{8,24},{9,... | collective-permute-start | bytes 589832 | tf_op jit(solution)/shard_map/ppermute | solution.py:62
  32.4 0.7 collective-permute-start.10
  33.1 3.3 %collective-permute-done.10 = f32[1024]{0:T(1024)S(1)} collective-permute-done((f32[1024]{0:T(1024)S(1)}, f32[1024]{0:T(1024)S(1)}, u32[]{:S(2)}, u32[]{:S(2)}) %collective-permute-start.10) | collective-permute-done | bytes 4128 | tf_op jit(solution)/shard_map/ppermute | solution.py:81
  36.5 3.6 %collective-permute-done.14 = f32[1024]{0:T(1024)S(1)} collective-permute-done((f32[1024]{0:T(1024)S(1)}, f32[1024]{0:T(1024)S(1)}, u32[]{:S(2)}, u32[]{:S(2)}) %collective-permute-start.14) | collective-permute-done | bytes 4128 | tf_op jit(solution)/shard_map/ppermute | solution.py:81
  40.1 4.2 %shard_map.106 = (bf16[2,384,256]{2,1,0:T(8,128)(2,1)S(1)}, bf16[3,384,256]{2,1,0:T(8,128)(2,1)S(1)}) custom-call(bf16[5,384,1024]{2,1,0:T(8,128)(2,1)S(1)} %copy-done.2, bf16[5,48,1024]{2,1,0:T(8,128)(2,1)S(1)} %get-tuple-element.48.before_ref, bf16[5,48,1024]{2,1,0:T(8,128)(2,1)S(1)} %get-tuple-element.47.after_ref, ...), custom_call_target="tpu_custom_call" | custom-call | flops 1024 | bytes 1024 | tf_op jit(solution)/shard_map/pallas_call | solution.py:164
  44.2 1.5 collective-permute-start.16
  45.7 2.8 %collective-permute-start.1 = (bf16[4,384,256]{2,1,0:T(8,128)(2,1)S(1)}, bf16[4,384,256]{2,1,0:T(8,128)(2,1)S(1)}, u32[]{:S(2)}, u32[]{:S(2)}) collective-permute-start(bf16[4,384,256]{2,1,0:T(8,128)(2,1)S(1)} %get-tuple-element.24), channel_id=1, source_target_pairs={{0,14},{1,15},{2,16},{3,17},{4,18},{5,19},{6,20},{7,21},{8,22},{9,... | collective-permute-start | bytes 2359304 | tf_op jit(solution)/shard_map/ppermute | solution.py:62
  48.6 4.1 %shard_map.102 = (bf16[4,384,256]{2,1,0:T(8,128)(2,1)S(1)}, bf16[1,384,256]{2,1,0:T(8,128)(2,1)S(1)}) custom-call(bf16[5,384,1024]{2,1,0:T(8,128)(2,1)S(1)} %copy-done.2, bf16[5,48,1024]{2,1,0:T(8,128)(2,1)S(1)} %get-tuple-element.48.before_ref, bf16[5,48,1024]{2,1,0:T(8,128)(2,1)S(1)} %get-tuple-element.47.after_ref, ...), custom_call_target="tpu_custom_call" | custom-call | flops 1024 | bytes 1024 | tf_op jit(solution)/shard_map/pallas_call | solution.py:164
  52.7 4.0 %shard_map.104 = (bf16[1,384,256]{2,1,0:T(8,128)(2,1)S(1)}, bf16[4,384,256]{2,1,0:T(8,128)(2,1)S(1)}) custom-call(bf16[5,384,1024]{2,1,0:T(8,128)(2,1)S(1)} %copy-done.2, bf16[5,48,1024]{2,1,0:T(8,128)(2,1)S(1)} %get-tuple-element.48.before_ref, bf16[5,48,1024]{2,1,0:T(8,128)(2,1)S(1)} %get-tuple-element.47.after_ref, ...), custom_call_target="tpu_custom_call" | custom-call | flops 1024 | bytes 1024 | tf_op jit(solution)/shard_map/pallas_call | solution.py:164
  56.7 1.3 collective-permute-start.5
  58.0 1.6 collective-permute-start.12
  59.6 4.2 %shard_map.107 = (bf16[3,384,256]{2,1,0:T(8,128)(2,1)S(1)}, bf16[2,384,256]{2,1,0:T(8,128)(2,1)S(1)}) custom-call(bf16[5,384,1024]{2,1,0:T(8,128)(2,1)S(1)} %copy-done.2, bf16[5,48,1024]{2,1,0:T(8,128)(2,1)S(1)} %get-tuple-element.48.before_ref, bf16[5,48,1024]{2,1,0:T(8,128)(2,1)S(1)} %get-tuple-element.47.after_ref, ...), custom_call_target="tpu_custom_call" | custom-call | flops 1024 | bytes 1024 | tf_op jit(solution)/shard_map/pallas_call | solution.py:164
  63.8 2.3 %collective-permute-done.5.refs_4_ = bf16[1,384,256]{2,1,0:T(8,128)(2,1)S(1)} collective-permute-done((bf16[1,384,256]{2,1,0:T(8,128)(2,1)S(1)}, bf16[1,384,256]{2,1,0:T(8,128)(2,1)S(1)}, u32[]{:S(2)}, u32[]{:S(2)}) %collective-permute-start.5) | collective-permute-done | bytes 196640 | tf_op jit(solution)/shard_map/ppermute | solution.py:62
  66.1 1.3 collective-permute-start.19
  67.4 1.3 collective-permute-start.4
  68.7 9.9 %collective-permute-start.8 = (bf16[4,384,256]{2,1,0:T(8,128)(2,1)}, bf16[4,384,256]{2,1,0:T(8,128)(2,1)S(1)}, u32[]{:S(2)}, u32[]{:S(2)}) collective-permute-start(bf16[4,384,256]{2,1,0:T(8,128)(2,1)} %collective-permute-done.7), channel_id=1, source_target_pairs={{2,10},{3,11},{4,12},{5,13},{6,14},{7,15},{0,16},{1,17},{10,18},{1... | collective-permute-start | bytes 2359304 | tf_op jit(solution)/shard_map/ppermute | solution.py:67
  78.7 1.3 collective-permute-start.13
  80.0 19.2 %collective-permute-start.9 = (bf16[1,384,256]{2,1,0:T(8,128)(2,1)S(1)}, bf16[1,384,256]{2,1,0:T(8,128)(2,1)S(1)}, u32[]{:S(2)}, u32[]{:S(2)}) collective-permute-start(bf16[1,384,256]{2,1,0:T(8,128)(2,1)S(1)} %get-tuple-element.33), channel_id=1, source_target_pairs={{0,8},{1,9},{2,10},{3,11},{4,12},{5,13},{6,14},{7,15},{8,16},{9,17... | collective-permute-start | bytes 589832 | tf_op jit(solution)/shard_map/ppermute | solution.py:62
  99.3 1.4 collective-permute-start.11
  100.7 15.4 %shard_map.101 = (f32[5,384,256]{2,1,0:T(8,128)}, f32[5,384,256]{2,1,0:T(8,128)}, f32[5,384,256]{2,1,0:T(8,128)}, f32[5,384,256]{2,1,0:T(8,128)}) custom-call(bf16[5,384,1024]{2,1,0:T(8,128)(2,1)} %x_ref.13, bf16[5,48,1024]{2,1,0:T(8,128)(2,1)} %copy-done.4, bf16[5,48,1024]{2,1,0:T(8,128)(2,1)} %copy-done.3, bf16[3,3,3,1024,256]{4,3,2,1,0:T(8,128)(2,1)} %refs_0_.13, ...), custom_call_target="tpu_custom_call" | custom-call | flops 1024 | bytes 1024 | tf_op jit(solution)/shard_map/pallas_call | solution.py:241
  116.2 4.9 %collective-permute-start.17 = (bf16[3,384,256]{2,1,0:T(8,128)(2,1)}, bf16[3,384,256]{2,1,0:T(8,128)(2,1)S(1)}, u32[]{:S(2)}, u32[]{:S(2)}) collective-permute-start(bf16[3,384,256]{2,1,0:T(8,128)(2,1)} %collective-permute-done.16), channel_id=1, source_target_pairs={{0,4},{5,5},{2,6},{7,7},{12,8},{1,9},{14,10},{3,11},{8,12},{13,13}... | collective-permute-start | bytes 1769480 | tf_op jit(solution)/shard_map/ppermute | solution.py:67
  121.0 4.2 %collective-permute-start.20 = (bf16[3,384,256]{2,1,0:T(8,128)(2,1)}, bf16[3,384,256]{2,1,0:T(8,128)(2,1)S(1)}, u32[]{:S(2)}, u32[]{:S(2)}) collective-permute-start(bf16[3,384,256]{2,1,0:T(8,128)(2,1)} %collective-permute-done.19), channel_id=1, source_target_pairs={{4,0},{1,1},{6,2},{3,3},{0,4},{13,5},{2,6},{15,7},{12,8},{9,9},{14... | collective-permute-start | bytes 1769480 | tf_op jit(solution)/shard_map/ppermute | solution.py:67
  125.2 13.8 %collective-permute-start.15 = (bf16[2,384,256]{2,1,0:T(8,128)(2,1)S(1)}, bf16[2,384,256]{2,1,0:T(8,128)(2,1)}, u32[]{:S(2)}, u32[]{:S(2)}) collective-permute-start(bf16[2,384,256]{2,1,0:T(8,128)(2,1)S(1)} %get-tuple-element.37), channel_id=1, source_target_pairs={{0,6},{1,7},{2,8},{3,9},{4,10},{5,11},{6,12},{7,13},{8,14},{9,15},... | collective-permute-start | bytes 1179656 | tf_op jit(solution)/shard_map/ppermute | solution.py:62
  139.0 1.5 collective-permute-start.21
  140.5 1.3 copy.13
  141.9 1.8 fusion.4.refs_5_
  143.7 7.6 %shard_map.105.base_ref = f32[5,384,256]{2,1,0:T(8,128)} custom-call(f32[5,384,256]{2,1,0:T(8,128)} %get-tuple-element.25.base_ref, bf16[1280,256]{1,0:T(8,128)(2,1)} %w_project.3, f32[5,256]{1,0:T(8,128)} %gain.3, f32[5,256]{1,0:T(8,128)} %shift_term.3, f32[5,384,256]{2,1,0:T(8,128)} %get-tuple-element.26.refs_0_, bf16[1,384,256]{2,1,0:T(8,128)(2,1)} %copy-done.10, ...), custom_call_target="tpu_custom_call" | custom-call | flops 1024 | bytes 1024 | tf_op jit(solution)/shard_map/pallas_call | solution.py:335
  151.3 3.3 %collective-permute-done.15.refs_1_ = bf16[2,384,256]{2,1,0:T(8,128)(2,1)} collective-permute-done((bf16[2,384,256]{2,1,0:T(8,128)(2,1)S(1)}, bf16[2,384,256]{2,1,0:T(8,128)(2,1)}, u32[]{:S(2)}, u32[]{:S(2)}) %collective-permute-start.15) | collective-permute-done | bytes 393248 | tf_op jit(solution)/shard_map/ppermute | solution.py:62
  154.7 0.8 copy-done.8
  155.5 0.2 copy-done.9
  155.7 8.6 %shard_map.108 = bf16[1920,256]{1,0:T(8,128)(2,1)} custom-call(f32[5,384,256]{2,1,0:T(8,128)} %shard_map.105.base_ref, bf16[1280,256]{1,0:T(8,128)(2,1)} %w_project.3, f32[5,256]{1,0:T(8,128)} %gain.3, f32[5,256]{1,0:T(8,128)} %shift_term.3, f32[5,384,256]{2,1,0:T(8,128)} %get-tuple-element.36.refs_0_, bf16[2,384,256]{2,1,0:T(8,128)(2,1)} %collective-permute-done.15.refs_1_, ...), custom_call_target="tpu_custom_call" | custom-call | flops 1024 | bytes 1024 | tf_op jit(solution)/shard_map/pallas_call | solution.py:335
  164.3 1.3 reshape.18
  165.6 31.7 %all_to_all.5 = bf16[32,60,256]{2,1,0:T(8,128)(2,1)S(1)} all-to-all(bf16[32,60,256]{2,1,0:T(8,128)(2,1)S(1)} %reshape.18), channel_id=1, replica_groups=mesh['band'=16,'sample'=2] {'band','sample'}, dimensions={0} | all-to-all | bytes 1966080 | tf_op jit(solution)/shard_map/all_to_all | solution.py:408
  197.3 1.1 reshape.19
  (55 shorter events, 0.2 us)
Async XLA Ops:
  0.0 141.8 %copy-start = (bf16[1024,256]{1,0:T(8,128)(2,1)S(1)}, bf16[1024,256]{1,0:T(8,128)(2,1)}, u32[]{:S(2)}) copy-start(bf16[1024,256]{1,0:T(8,128)(2,1)} %param.13) | copy-start | bytes 1572868
  0.0 2.5 %copy-start.2 = (bf16[5,384,1024]{2,1,0:T(8,128)(2,1)S(1)}, bf16[5,384,1024]{2,1,0:T(8,128)(2,1)}, u32[]{:S(2)}) copy-start(bf16[5,384,1024]{2,1,0:T(8,128)(2,1)} %x_ref.13) | copy-start | bytes 11796484
  1.5 2.7 %collective-permute-start = (bf16[5,96,1024]{2,1,0:T(8,128)(2,1)S(1)}, bf16[5,96,1024]{2,1,0:T(8,128)(2,1)S(1)}, u32[]{:S(2)}, u32[]{:S(2)}) collective-permute-start(bf16[5,96,1024]{2,1,0:T(8,128)(2,1)S(1)} %pad_maximum_fusion), channel_id=1, source_target_pairs={{0,1},{1,0},{2,3},{3,2},{4,5},{5,4},{6,7},{7,6},{8,9},{9,8},{10,11... | collective-permute-start | bytes 2949128 | tf_op jit(solution)/shard_map/ppermute | solution.py:32
  4.3 55.4 %copy-start.3 = (bf16[5,48,1024]{2,1,0:T(8,128)(2,1)}, bf16[5,48,1024]{2,1,0:T(8,128)(2,1)S(1)}, u32[]{:S(2)}) copy-start(bf16[5,48,1024]{2,1,0:T(8,128)(2,1)S(1)} %get-tuple-element.47.after_ref) | copy-start | bytes 1474564
  4.3 55.3 %copy-start.4 = (bf16[5,48,1024]{2,1,0:T(8,128)(2,1)}, bf16[5,48,1024]{2,1,0:T(8,128)(2,1)S(1)}, u32[]{:S(2)}) copy-start(bf16[5,48,1024]{2,1,0:T(8,128)(2,1)S(1)} %get-tuple-element.48.before_ref) | copy-start | bytes 1474564
  4.3 1.3 collective-permute-start.3
  5.5 4.4 %collective-permute-start.6 = (f32[1024]{0:T(1024)S(1)}, f32[1024]{0:T(1024)S(1)}, u32[]{:S(2)}, u32[]{:S(2)}) collective-permute-start(f32[1024]{0:T(1024)S(1)} %add.18.refs_1_), channel_id=1, source_target_pairs={{0,2},{2,0},{4,6},{6,4},{8,10},{10,8},{12,14},{14,12},{16,18},{18,... | collective-permute-start | bytes 12296 | tf_op jit(solution)/shard_map/ppermute | solution.py:81
  10.0 5.0 %copy-start.1 = (bf16[3,3,3,1024,256]{4,3,2,1,0:T(8,128)(2,1)S(1)}, bf16[3,3,3,1024,256]{4,3,2,1,0:T(8,128)(2,1)}, u32[]{:S(2)}) copy-start(bf16[3,3,3,1024,256]{4,3,2,1,0:T(8,128)(2,1)} %refs_0_.13) | copy-start | bytes 42467332
  19.0 49.7 %collective-permute-start.7 = (bf16[4,384,256]{2,1,0:T(8,128)(2,1)S(1)}, bf16[4,384,256]{2,1,0:T(8,128)(2,1)}, u32[]{:S(2)}, u32[]{:S(2)}) collective-permute-start(bf16[4,384,256]{2,1,0:T(8,128)(2,1)S(1)} %get-tuple-element.32), channel_id=1, source_target_pairs={{0,2},{1,3},{2,4},{3,5},{4,6},{5,7},{6,0},{7,1},{8,10},{9,11},{10,... | collective-permute-start | bytes 2359304 | tf_op jit(solution)/shard_map/ppermute | solution.py:62
  27.0 31.0 %collective-permute-start.2 = (bf16[1,384,256]{2,1,0:T(8,128)(2,1)S(1)}, bf16[1,384,256]{2,1,0:T(8,128)(2,1)S(1)}, u32[]{:S(2)}, u32[]{:S(2)}) collective-permute-start(bf16[1,384,256]{2,1,0:T(8,128)(2,1)S(1)} %get-tuple-element.27), channel_id=1, source_target_pairs={{0,16},{1,17},{2,18},{3,19},{4,20},{5,21},{6,22},{7,23},{8,24},{9,... | collective-permute-start | bytes 589832 | tf_op jit(solution)/shard_map/ppermute | solution.py:62
  32.4 4.0 %collective-permute-start.10 = (f32[1024]{0:T(1024)S(1)}, f32[1024]{0:T(1024)S(1)}, u32[]{:S(2)}, u32[]{:S(2)}) collective-permute-start(f32[1024]{0:T(1024)S(1)} %add.19.refs_1_), channel_id=1, source_target_pairs={{0,4},{2,6},{4,0},{6,2},{8,12},{10,14},{12,8},{14,10},{16,20},{18,... | collective-permute-start | bytes 12296 | tf_op jit(solution)/shard_map/ppermute | solution.py:81
  36.5 3.6 %collective-permute-start.14 = (f32[1024]{0:T(1024)S(1)}, f32[1024]{0:T(1024)S(1)}, u32[]{:S(2)}, u32[]{:S(2)}) collective-permute-start(f32[1024]{0:T(1024)S(1)} %add.20.refs_1_), channel_id=1, source_target_pairs={{0,8},{2,10},{4,12},{6,14},{8,0},{10,2},{12,4},{14,6},{16,24},{18,... | collective-permute-start | bytes 12296 | tf_op jit(solution)/shard_map/ppermute | solution.py:81
  44.2 23.2 %collective-permute-start.16 = (bf16[3,384,256]{2,1,0:T(8,128)(2,1)S(1)}, bf16[3,384,256]{2,1,0:T(8,128)(2,1)}, u32[]{:S(2)}, u32[]{:S(2)}) collective-permute-start(bf16[3,384,256]{2,1,0:T(8,128)(2,1)S(1)} %get-tuple-element.38), channel_id=1, source_target_pairs={{0,0},{1,5},{2,2},{3,7},{4,12},{5,1},{6,14},{7,3},{8,8},{9,13},{10... | collective-permute-start | bytes 1769480 | tf_op jit(solution)/shard_map/ppermute | solution.py:62
  45.7 11.0 %collective-permute-start.18 = (f32[1024]{0:T(1024)S(1)}, f32[1024]{0:T(1024)S(1)}, u32[]{:S(2)}, u32[]{:S(2)}) collective-permute-start(f32[1024]{0:T(1024)S(1)} %add.21.refs_1_), channel_id=1, source_target_pairs={{0,16},{2,18},{4,20},{6,22},{8,24},{10,26},{12,28},{14,30},{16,0},... | collective-permute-start | bytes 12296 | tf_op jit(solution)/shard_map/ppermute | solution.py:81
  45.7 53.5 %collective-permute-start.1 = (bf16[4,384,256]{2,1,0:T(8,128)(2,1)S(1)}, bf16[4,384,256]{2,1,0:T(8,128)(2,1)S(1)}, u32[]{:S(2)}, u32[]{:S(2)}) collective-permute-start(bf16[4,384,256]{2,1,0:T(8,128)(2,1)S(1)} %get-tuple-element.24), channel_id=1, source_target_pairs={{0,14},{1,15},{2,16},{3,17},{4,18},{5,19},{6,20},{7,21},{8,22},{9,... | collective-permute-start | bytes 2359304 | tf_op jit(solution)/shard_map/ppermute | solution.py:62
  56.7 9.4 %collective-permute-start.5 = (bf16[1,384,256]{2,1,0:T(8,128)(2,1)S(1)}, bf16[1,384,256]{2,1,0:T(8,128)(2,1)S(1)}, u32[]{:S(2)}, u32[]{:S(2)}) collective-permute-start(bf16[1,384,256]{2,1,0:T(8,128)(2,1)S(1)} %get-tuple-element.30), channel_id=1, source_target_pairs={{16,0},{17,1},{18,2},{19,3},{20,4},{21,5},{22,6},{23,7},{24,8},{25... | collective-permute-start | bytes 589832 | tf_op jit(solution)/shard_map/ppermute | solution.py:62
  58.0 5.8 %copy-start.10 = (bf16[1,384,256]{2,1,0:T(8,128)(2,1)}, bf16[1,384,256]{2,1,0:T(8,128)(2,1)S(1)}, u32[]{:S(2)}) copy-start(bf16[1,384,256]{2,1,0:T(8,128)(2,1)S(1)} %collective-permute-done.2.refs_1_) | copy-start | bytes 589828
  58.0 20.6 %collective-permute-start.12 = (bf16[4,384,256]{2,1,0:T(8,128)(2,1)S(1)}, bf16[4,384,256]{2,1,0:T(8,128)(2,1)}, u32[]{:S(2)}, u32[]{:S(2)}) collective-permute-start(bf16[4,384,256]{2,1,0:T(8,128)(2,1)S(1)} %get-tuple-element.35), channel_id=1, source_target_pairs={{10,8},{11,9},{12,10},{13,11},{14,12},{15,13},{16,22},{17,23},{18,... | collective-permute-start | bytes 2359304 | tf_op jit(solution)/shard_map/ppermute | solution.py:62
  66.1 33.1 %copy-start.11 = (bf16[1,384,256]{2,1,0:T(8,128)(2,1)}, bf16[1,384,256]{2,1,0:T(8,128)(2,1)S(1)}, u32[]{:S(2)}) copy-start(bf16[1,384,256]{2,1,0:T(8,128)(2,1)S(1)} %collective-permute-done.5.refs_4_) | copy-start | bytes 589828
  66.1 13.9 %collective-permute-start.19 = (bf16[3,384,256]{2,1,0:T(8,128)(2,1)S(1)}, bf16[3,384,256]{2,1,0:T(8,128)(2,1)}, u32[]{:S(2)}, u32[]{:S(2)}) collective-permute-start(bf16[3,384,256]{2,1,0:T(8,128)(2,1)S(1)} %get-tuple-element.40), channel_id=1, source_target_pairs={{4,4},{5,1},{6,6},{7,3},{8,0},{9,13},{10,2},{11,15},{12,12},{13,9}... | collective-permute-start | bytes 1769480 | tf_op jit(solution)/shard_map/ppermute | solution.py:62
  67.4 57.8 %collective-permute-start.4 = (bf16[4,384,256]{2,1,0:T(8,128)(2,1)S(1)}, bf16[4,384,256]{2,1,0:T(8,128)(2,1)S(1)}, u32[]{:S(2)}, u32[]{:S(2)}) collective-permute-start(bf16[4,384,256]{2,1,0:T(8,128)(2,1)S(1)} %get-tuple-element.29), channel_id=1, source_target_pairs={{14,0},{15,1},{16,2},{17,3},{18,4},{19,5},{20,6},{21,7},{22,8},{23... | collective-permute-start | bytes 2359304 | tf_op jit(solution)/shard_map/ppermute | solution.py:62
  68.7 70.3 %collective-permute-start.8 = (bf16[4,384,256]{2,1,0:T(8,128)(2,1)}, bf16[4,384,256]{2,1,0:T(8,128)(2,1)S(1)}, u32[]{:S(2)}, u32[]{:S(2)}) collective-permute-start(bf16[4,384,256]{2,1,0:T(8,128)(2,1)} %collective-permute-done.7), channel_id=1, source_target_pairs={{2,10},{3,11},{4,12},{5,13},{6,14},{7,15},{0,16},{1,17},{10,18},{1... | collective-permute-start | bytes 2359304 | tf_op jit(solution)/shard_map/ppermute | solution.py:67
  78.7 65.0 %collective-permute-start.13 = (bf16[4,384,256]{2,1,0:T(8,128)(2,1)}, bf16[4,384,256]{2,1,0:T(8,128)(2,1)}, u32[]{:S(2)}, u32[]{:S(2)}) collective-permute-start(bf16[4,384,256]{2,1,0:T(8,128)(2,1)} %collective-permute-done.12), channel_id=1, source_target_pairs={{8,0},{9,1},{10,2},{11,3},{12,4},{13,5},{22,6},{23,7},{16,8},{17,9... | collective-permute-start | bytes 2359304 | tf_op jit(solution)/shard_map/ppermute | solution.py:67
  80.0 36.2 %collective-permute-start.9 = (bf16[1,384,256]{2,1,0:T(8,128)(2,1)S(1)}, bf16[1,384,256]{2,1,0:T(8,128)(2,1)S(1)}, u32[]{:S(2)}, u32[]{:S(2)}) collective-permute-start(bf16[1,384,256]{2,1,0:T(8,128)(2,1)S(1)} %get-tuple-element.33), channel_id=1, source_target_pairs={{0,8},{1,9},{2,10},{3,11},{4,12},{5,13},{6,14},{7,15},{8,16},{9,17... | collective-permute-start | bytes 589832 | tf_op jit(solution)/shard_map/ppermute | solution.py:62
  99.2 1.5 copy-start.5
  99.2 41.3 %copy-start.16 = (s32[5,384]{1,0:T(8,128)S(1)}, s32[5,384]{1,0:T(8,128)}, u32[]{:S(2)}) copy-start(s32[5,384]{1,0:T(8,128)} %param.19) | copy-start | bytes 23044
  99.2 42.6 %copy-start.14 = (f32[5,256]{1,0:T(8,128)S(1)}, f32[5,256]{1,0:T(8,128)}, u32[]{:S(2)}) copy-start(f32[5,256]{1,0:T(8,128)} %gain.3) | copy-start | bytes 15364
  99.3 42.6 %copy-start.15 = (f32[5,256]{1,0:T(8,128)S(1)}, f32[5,256]{1,0:T(8,128)}, u32[]{:S(2)}) copy-start(f32[5,256]{1,0:T(8,128)} %shift_term.3) | copy-start | bytes 15364
  99.3 21.8 %collective-permute-start.11 = (bf16[1,384,256]{2,1,0:T(8,128)(2,1)S(1)}, bf16[1,384,256]{2,1,0:T(8,128)(2,1)S(1)}, u32[]{:S(2)}, u32[]{:S(2)}) collective-permute-start(bf16[1,384,256]{2,1,0:T(8,128)(2,1)S(1)} %get-tuple-element.34), channel_id=1, source_target_pairs={{8,0},{9,1},{10,2},{11,3},{12,4},{13,5},{14,6},{15,7},{16,8},{17,9... | collective-permute-start | bytes 589832 | tf_op jit(solution)/shard_map/ppermute | solution.py:62
  116.1 24.3 %copy-start.12 = (bf16[1,384,256]{2,1,0:T(8,128)(2,1)}, bf16[1,384,256]{2,1,0:T(8,128)(2,1)S(1)}, u32[]{:S(2)}) copy-start(bf16[1,384,256]{2,1,0:T(8,128)(2,1)S(1)} %collective-permute-done.9.refs_7_) | copy-start | bytes 589828
  116.2 38.5 %collective-permute-start.17 = (bf16[3,384,256]{2,1,0:T(8,128)(2,1)}, bf16[3,384,256]{2,1,0:T(8,128)(2,1)S(1)}, u32[]{:S(2)}, u32[]{:S(2)}) collective-permute-start(bf16[3,384,256]{2,1,0:T(8,128)(2,1)} %collective-permute-done.16), channel_id=1, source_target_pairs={{0,4},{5,5},{2,6},{7,7},{12,8},{1,9},{14,10},{3,11},{8,12},{13,13}... | collective-permute-start | bytes 1769480 | tf_op jit(solution)/shard_map/ppermute | solution.py:67
  121.0 19.5 %copy-start.13 = (bf16[1,384,256]{2,1,0:T(8,128)(2,1)}, bf16[1,384,256]{2,1,0:T(8,128)(2,1)S(1)}, u32[]{:S(2)}) copy-start(bf16[1,384,256]{2,1,0:T(8,128)(2,1)S(1)} %collective-permute-done.11.refs_8_) | copy-start | bytes 589828
  121.0 33.6 %collective-permute-start.20 = (bf16[3,384,256]{2,1,0:T(8,128)(2,1)}, bf16[3,384,256]{2,1,0:T(8,128)(2,1)S(1)}, u32[]{:S(2)}, u32[]{:S(2)}) collective-permute-start(bf16[3,384,256]{2,1,0:T(8,128)(2,1)} %collective-permute-done.19), channel_id=1, source_target_pairs={{4,0},{1,1},{6,2},{3,3},{0,4},{13,5},{2,6},{15,7},{12,8},{9,9},{14... | collective-permute-start | bytes 1769480 | tf_op jit(solution)/shard_map/ppermute | solution.py:67
  125.2 18.5 %copy-start.6 = (bf16[4,384,256]{2,1,0:T(8,128)(2,1)}, bf16[4,384,256]{2,1,0:T(8,128)(2,1)S(1)}, u32[]{:S(2)}) copy-start(bf16[4,384,256]{2,1,0:T(8,128)(2,1)S(1)} %collective-permute-done.4.refs_3_) | copy-start | bytes 2359300
  125.2 29.4 %collective-permute-start.15 = (bf16[2,384,256]{2,1,0:T(8,128)(2,1)S(1)}, bf16[2,384,256]{2,1,0:T(8,128)(2,1)}, u32[]{:S(2)}, u32[]{:S(2)}) collective-permute-start(bf16[2,384,256]{2,1,0:T(8,128)(2,1)S(1)} %get-tuple-element.37), channel_id=1, source_target_pairs={{0,6},{1,7},{2,8},{3,9},{4,10},{5,11},{6,12},{7,13},{8,14},{9,15},... | collective-permute-start | bytes 1179656 | tf_op jit(solution)/shard_map/ppermute | solution.py:62
  139.0 1.5 copy-start.7
  139.0 15.6 %collective-permute-start.21 = (bf16[2,384,256]{2,1,0:T(8,128)(2,1)S(1)}, bf16[2,384,256]{2,1,0:T(8,128)(2,1)}, u32[]{:S(2)}, u32[]{:S(2)}) collective-permute-start(bf16[2,384,256]{2,1,0:T(8,128)(2,1)S(1)} %get-tuple-element.42), channel_id=1, source_target_pairs={{6,0},{7,1},{8,2},{9,3},{10,4},{11,5},{12,6},{13,7},{14,8},{15,9},... | collective-permute-start | bytes 1179656 | tf_op jit(solution)/shard_map/ppermute | solution.py:62
  154.6 0.8 copy-start.8
  154.6 1.0 copy-start.9

commit v6 on v5

--- a/solution.py
+++ b/solution.py
@@ -376,7 +376,7 @@
     totals, steps = total_over_devices(
         lax.optimization_barrier((jnp.sum(features, axis=(0, 1), dtype=jnp.float32), before))[0]
     )
-    order = ((2, 0), (2, 2), (1, 0), (1, 2), (0, 0), (0, 2))
+    order = ((2, 2), (2, 0), (1, 2), (1, 0), (0, 2), (0, 0))
     centre, base = {}, None
     for place, (branch, row_tap) in enumerate(order):
         if place == own_place:
@@ -387,7 +387,7 @@
                 w_atrous,
                 (2, 1, 0),
                 (w_point, w_project, branch_gain, branch_bias),
-                [part_way[2, 0][1]],
+                [part_way[2, 2][1]],
             )
         send(branch, row_tap, steps[place - 1 : place] if place else (), base)
 

time: 199 us -> 197 us (0.990)
  starting transfers between devices: 79.7 us -> 59.5 us
  waiting for transfers between devices: 16 us -> 35.9 us
    ppermute x12, starting transfers between devices: 54.9 us -> 36.5 us  [passed_along(): array = lax.ppermute(array, ('band', 'sample'), first)]
    ppermute x5, waiting for transfers between devices: 9.33 us -> 24.2 us  [total_over_devices(): lax.ppermute(values, axis, [(i, i ^ step) for i in range(size)])]
    ppermute x4, starting transfers between devices: 20.2 us -> 8.45 us  [passed_along(): array = lax.ppermute(array, ('band', 'sample'), second)]
    ppermute x5, starting transfers between devices: 3.97 us -> 14 us  [total_over_devices(): lax.ppermute(values, axis, [(i, i ^ step) for i in range(size)])]
    ppermute x12, waiting for transfers between devices: 5.62 us -> 10.7 us  [passed_along(): array = lax.ppermute(array, ('band', 'sample'), first)]
  transfers between devices with their start and end apart: 22 -> 22, of which waited for: 7 -> 8; matrix products, arithmetic and copies ran while one was open for 2% -> 2% of each run, Pallas kernels for 22% -> 22%
where the time goes in v6:
time: 197 us
  starting transfers between devices  59.5 us (30%)
  Pallas kernels  56.2 us (29%)
  waiting for transfers between devices  35.9 us (18%)
  blocking collectives  30.2 us (15%)
  local copies, waits for them, and re-layouts  11.8 us (6%)
    ppermute x12, starting transfers between devices, passed_along(): array = lax.ppermute(array, ('band', 'sample'), first)  36.5 us
    all_to_all x1, blocking collectives, shards(): lax.all_to_all(outgoing, ('band', 'sample'), split_axis=0, concat_axis=0,...  30.2 us
    pallas_call x6, Pallas kernels, row_taps(): pl.pallas_call(functools.partial(taps_body, plan, row_count, len(tokens))...  24.5 us
    ppermute x5, waiting for transfers between devices, total_over_devices(): lax.ppermute(values, axis, [(i, i ^ step) for i in range(size)])  24.2 us
    pallas_call x2, Pallas kernels, join(): pl.pallas_call(functools.partial(join_body, plan, remainders, tail is not...  16.3 us
    pallas_call x1, Pallas kernels, own_rows(): pl.pallas_call(functools.partial(own_body, plan, point_operands is not No...  15.4 us
    ppermute x5, starting transfers between devices, total_over_devices(): lax.ppermute(values, axis, [(i, i ^ step) for i in range(size)])  14 us
    ppermute x12, waiting for transfers between devices, passed_along(): array = lax.ppermute(array, ('band', 'sample'), first)  10.7 us
  transfers between devices with their start and end apart: 22, of which 8 were waited for; matrix products, arithmetic and copies ran while one was open for 2% of the time, Pallas kernels for 22%

profile of v6, /device:TPU:0, one launch (start us, length us, event | category | flops | bytes accessed | tf_op | source)
XLA Modules:
  0.0 196.6 jit_solution(845430050562029857)
XLA Ops:
  0.0 1.4 fusion.10
  1.5 0.5 collective-permute-start
  2.0 0.5 copy-done.2
  2.5 0.7 convert_reduce_fusion
  3.2 1.0 collective-permute-done
  4.7 0.8 collective-permute-done.2
  5.5 2.8 %collective-permute-start.6 = (f32[1024]{0:T(1024)S(1)}, f32[1024]{0:T(1024)S(1)}, u32[]{:S(2)}, u32[]{:S(2)}) collective-permute-start(f32[1024]{0:T(1024)S(1)} %add.18.refs_1_), channel_id=1, source_target_pairs={{0,2},{2,0},{4,6},{6,4},{8,10},{10,8},{12,14},{14,12},{16,18},{18,... | collective-permute-start | bytes 12296 | tf_op jit(solution)/shard_map/ppermute | solution.py:81
  8.4 1.6 collective-permute-done.6
  10.0 5.0 %copy-done.1 = bf16[3,3,3,1024,256]{4,3,2,1,0:T(8,128)(2,1)S(1)} copy-done((bf16[3,3,3,1024,256]{4,3,2,1,0:T(8,128)(2,1)S(1)}, bf16[3,3,3,1024,256]{4,3,2,1,0:T(8,128)(2,1)}, u32[]{:S(2)}) %copy-start.1) | copy-done | bytes 14155800
  15.0 4.0 %shard_map.104 = (bf16[1,384,256]{2,1,0:T(8,128)(2,1)S(1)}, bf16[4,384,256]{2,1,0:T(8,128)(2,1)S(1)}) custom-call(bf16[5,384,1024]{2,1,0:T(8,128)(2,1)S(1)} %copy-done.2, bf16[5,48,1024]{2,1,0:T(8,128)(2,1)S(1)} %get-tuple-element.48.before_ref, bf16[5,48,1024]{2,1,0:T(8,128)(2,1)S(1)} %get-tuple-element.47.after_ref, ...), custom_call_target="tpu_custom_call" | custom-call | flops 1024 | bytes 1024 | tf_op jit(solution)/shard_map/pallas_call | solution.py:164
  19.0 1.6 collective-permute-start.12
  20.6 4.1 %shard_map.100 = (bf16[4,384,256]{2,1,0:T(8,128)(2,1)S(1)}, bf16[1,384,256]{2,1,0:T(8,128)(2,1)S(1)}) custom-call(bf16[5,384,1024]{2,1,0:T(8,128)(2,1)S(1)} %copy-done.2, bf16[5,48,1024]{2,1,0:T(8,128)(2,1)S(1)} %get-tuple-element.48.before_ref, bf16[5,48,1024]{2,1,0:T(8,128)(2,1)S(1)} %get-tuple-element.47.after_ref, bf16[3,3,3,1024,256]{4,3,2,1,0:T(8,128)(2,1)S(1)} %copy-done.1), custom_call_target="tpu_custom_call" | custom-call | flops 1024 | bytes 1024 | tf_op jit(solution)/shard_map/pallas_call | solution.py:164
  24.7 1.3 collective-permute-start.5
  26.0 2.1 %collective-permute-start.7 = (f32[1024]{0:T(1024)S(1)}, f32[1024]{0:T(1024)S(1)}, u32[]{:S(2)}, u32[]{:S(2)}) collective-permute-start(f32[1024]{0:T(1024)S(1)} %add.19.refs_1_), channel_id=1, source_target_pairs={{0,4},{2,6},{4,0},{6,2},{8,12},{10,14},{12,8},{14,10},{16,20},{18,... | collective-permute-start | bytes 12296 | tf_op jit(solution)/shard_map/ppermute | solution.py:81
  28.1 1.6 collective-permute-done.7
  29.7 3.4 %collective-permute-start.14 = (f32[1024]{0:T(1024)S(1)}, f32[1024]{0:T(1024)S(1)}, u32[]{:S(2)}, u32[]{:S(2)}) collective-permute-start(f32[1024]{0:T(1024)S(1)} %add.20.refs_1_), channel_id=1, source_target_pairs={{0,8},{2,10},{4,12},{6,14},{8,0},{10,2},{12,4},{14,6},{16,24},{18,... | collective-permute-start | bytes 12296 | tf_op jit(solution)/shard_map/ppermute | solution.py:81
  33.0 1.6 collective-permute-done.14
  34.6 4.2 %shard_map.107 = (bf16[3,384,256]{2,1,0:T(8,128)(2,1)S(1)}, bf16[2,384,256]{2,1,0:T(8,128)(2,1)S(1)}) custom-call(bf16[5,384,1024]{2,1,0:T(8,128)(2,1)S(1)} %copy-done.2, bf16[5,48,1024]{2,1,0:T(8,128)(2,1)S(1)} %get-tuple-element.48.before_ref, bf16[5,48,1024]{2,1,0:T(8,128)(2,1)S(1)} %get-tuple-element.47.after_ref, ...), custom_call_target="tpu_custom_call" | custom-call | flops 1024 | bytes 1024 | tf_op jit(solution)/shard_map/pallas_call | solution.py:164
  38.8 1.3 collective-permute-start.19
  40.1 5.3 %collective-permute-start.15 = (f32[1024]{0:T(1024)S(1)}, f32[1024]{0:T(1024)S(1)}, u32[]{:S(2)}, u32[]{:S(2)}) collective-permute-start(f32[1024]{0:T(1024)S(1)} %add.21.refs_1_), channel_id=1, source_target_pairs={{0,16},{2,18},{4,20},{6,22},{8,24},{10,26},{12,28},{14,30},{16,0},... | collective-permute-start | bytes 12296 | tf_op jit(solution)/shard_map/ppermute | solution.py:81
  45.4 1.3 collective-permute-start.1
  46.6 4.1 %shard_map.102 = (bf16[1,384,256]{2,1,0:T(8,128)(2,1)S(1)}, bf16[4,384,256]{2,1,0:T(8,128)(2,1)S(1)}) custom-call(bf16[5,384,1024]{2,1,0:T(8,128)(2,1)S(1)} %copy-done.2, bf16[5,48,1024]{2,1,0:T(8,128)(2,1)S(1)} %get-tuple-element.48.before_ref, bf16[5,48,1024]{2,1,0:T(8,128)(2,1)S(1)} %get-tuple-element.47.after_ref, ...), custom_call_target="tpu_custom_call" | custom-call | flops 1024 | bytes 1024 | tf_op jit(solution)/shard_map/pallas_call | solution.py:164
  50.8 4.0 %shard_map.103 = (bf16[4,384,256]{2,1,0:T(8,128)(2,1)S(1)}, bf16[1,384,256]{2,1,0:T(8,128)(2,1)S(1)}) custom-call(bf16[5,384,1024]{2,1,0:T(8,128)(2,1)S(1)} %copy-done.2, bf16[5,48,1024]{2,1,0:T(8,128)(2,1)S(1)} %get-tuple-element.48.before_ref, bf16[5,48,1024]{2,1,0:T(8,128)(2,1)S(1)} %get-tuple-element.47.after_ref, ...), custom_call_target="tpu_custom_call" | custom-call | flops 1024 | bytes 1024 | tf_op jit(solution)/shard_map/pallas_call | solution.py:164
  54.8 18.6 %collective-permute-done.15 = f32[1024]{0:T(1024)S(1)} collective-permute-done((f32[1024]{0:T(1024)S(1)}, f32[1024]{0:T(1024)S(1)}, u32[]{:S(2)}, u32[]{:S(2)}) %collective-permute-start.15) | collective-permute-done | bytes 4128 | tf_op jit(solution)/shard_map/ppermute | solution.py:81
  73.4 1.4 collective-permute-start.3
  74.9 2.9 %collective-permute-start.8 = (bf16[4,384,256]{2,1,0:T(8,128)(2,1)S(1)}, bf16[4,384,256]{2,1,0:T(8,128)(2,1)}, u32[]{:S(2)}, u32[]{:S(2)}) collective-permute-start(bf16[4,384,256]{2,1,0:T(8,128)(2,1)S(1)} %get-tuple-element.32), channel_id=1, source_target_pairs={{0,2},{1,3},{2,4},{3,5},{4,6},{5,7},{6,0},{7,1},{8,10},{9,11},{10,... | collective-permute-start | bytes 2359304 | tf_op jit(solution)/shard_map/ppermute | solution.py:62
  77.8 4.2 %shard_map.106 = (bf16[2,384,256]{2,1,0:T(8,128)(2,1)S(1)}, bf16[3,384,256]{2,1,0:T(8,128)(2,1)S(1)}) custom-call(bf16[5,384,1024]{2,1,0:T(8,128)(2,1)S(1)} %copy-done.2, bf16[5,48,1024]{2,1,0:T(8,128)(2,1)S(1)} %get-tuple-element.48.before_ref, bf16[5,48,1024]{2,1,0:T(8,128)(2,1)S(1)} %get-tuple-element.47.after_ref, ...), custom_call_target="tpu_custom_call" | custom-call | flops 1024 | bytes 1024 | tf_op jit(solution)/shard_map/pallas_call | solution.py:164
  82.0 1.5 collective-permute-start.17
  83.5 1.3 collective-permute-start.4
  84.9 1.3 collective-permute-start.13
  86.2 8.3 %collective-permute-done.8 = bf16[4,384,256]{2,1,0:T(8,128)(2,1)} collective-permute-done((bf16[4,384,256]{2,1,0:T(8,128)(2,1)S(1)}, bf16[4,384,256]{2,1,0:T(8,128)(2,1)}, u32[]{:S(2)}, u32[]{:S(2)}) %collective-permute-start.8) | collective-permute-done | bytes 786464 | tf_op jit(solution)/shard_map/ppermute | solution.py:62
  94.4 3.9 %collective-permute-start.9 = (bf16[4,384,256]{2,1,0:T(8,128)(2,1)}, bf16[4,384,256]{2,1,0:T(8,128)(2,1)}, u32[]{:S(2)}, u32[]{:S(2)}) collective-permute-start(bf16[4,384,256]{2,1,0:T(8,128)(2,1)} %collective-permute-done.8), channel_id=1, source_target_pairs={{2,10},{3,11},{4,12},{5,13},{6,14},{7,15},{0,16},{1,17},{10,18},{1... | collective-permute-start | bytes 2359304 | tf_op jit(solution)/shard_map/ppermute | solution.py:67
  98.3 1.3 collective-permute-start.11
  99.7 11.3 %collective-permute-start.10 = (bf16[1,384,256]{2,1,0:T(8,128)(2,1)S(1)}, bf16[1,384,256]{2,1,0:T(8,128)(2,1)S(1)}, u32[]{:S(2)}, u32[]{:S(2)}) collective-permute-start(bf16[1,384,256]{2,1,0:T(8,128)(2,1)S(1)} %get-tuple-element.33), channel_id=1, source_target_pairs={{0,8},{1,9},{2,10},{3,11},{4,12},{5,13},{6,14},{7,15},{8,16},{9,17... | collective-permute-start | bytes 589832 | tf_op jit(solution)/shard_map/ppermute | solution.py:62
  111.0 15.4 %shard_map.101 = (f32[5,384,256]{2,1,0:T(8,128)}, f32[5,384,256]{2,1,0:T(8,128)}, f32[5,384,256]{2,1,0:T(8,128)}, f32[5,384,256]{2,1,0:T(8,128)}) custom-call(bf16[5,384,1024]{2,1,0:T(8,128)(2,1)} %x_ref.13, bf16[5,48,1024]{2,1,0:T(8,128)(2,1)} %copy-done.4, bf16[5,48,1024]{2,1,0:T(8,128)(2,1)} %copy-done.3, bf16[3,3,3,1024,256]{4,3,2,1,0:T(8,128)(2,1)} %refs_0_.13, ...), custom_call_target="tpu_custom_call" | custom-call | flops 1024 | bytes 1024 | tf_op jit(solution)/shard_map/pallas_call | solution.py:241
  126.5 1.3 collective-permute-start.18
  127.8 1.9 collective-permute-start.20
  129.8 1.3 collective-permute-start.21
  131.1 10.0 %collective-permute-start.16 = (bf16[2,384,256]{2,1,0:T(8,128)(2,1)S(1)}, bf16[2,384,256]{2,1,0:T(8,128)(2,1)}, u32[]{:S(2)}, u32[]{:S(2)}) collective-permute-start(bf16[2,384,256]{2,1,0:T(8,128)(2,1)S(1)} %get-tuple-element.37), channel_id=1, source_target_pairs={{0,6},{1,7},{2,8},{3,9},{4,10},{5,11},{6,12},{7,13},{8,14},{9,15},... | collective-permute-start | bytes 1179656 | tf_op jit(solution)/shard_map/ppermute | solution.py:62
  141.1 1.3 copy.13
  142.4 1.8 fusion.4.refs_5_
  144.3 7.6 %shard_map.105.base_ref = f32[5,384,256]{2,1,0:T(8,128)} custom-call(f32[5,384,256]{2,1,0:T(8,128)} %get-tuple-element.25.base_ref, bf16[1280,256]{1,0:T(8,128)(2,1)} %w_project.3, f32[5,256]{1,0:T(8,128)} %gain.3, f32[5,256]{1,0:T(8,128)} %shift_term.3, f32[5,384,256]{2,1,0:T(8,128)} %get-tuple-element.26.refs_0_, bf16[1,384,256]{2,1,0:T(8,128)(2,1)} %copy-done.11, ...), custom_call_target="tpu_custom_call" | custom-call | flops 1024 | bytes 1024 | tf_op jit(solution)/shard_map/pallas_call | solution.py:335
  151.9 2.4 %collective-permute-done.16.refs_1_ = bf16[2,384,256]{2,1,0:T(8,128)(2,1)} collective-permute-done((bf16[2,384,256]{2,1,0:T(8,128)(2,1)S(1)}, bf16[2,384,256]{2,1,0:T(8,128)(2,1)}, u32[]{:S(2)}, u32[]{:S(2)}) %collective-permute-start.16) | collective-permute-done | bytes 393248 | tf_op jit(solution)/shard_map/ppermute | solution.py:62
  154.3 0.8 copy-done.8
  155.4 8.6 %shard_map.108 = bf16[1920,256]{1,0:T(8,128)(2,1)} custom-call(f32[5,384,256]{2,1,0:T(8,128)} %shard_map.105.base_ref, bf16[1280,256]{1,0:T(8,128)(2,1)} %w_project.3, f32[5,256]{1,0:T(8,128)} %gain.3, f32[5,256]{1,0:T(8,128)} %shift_term.3, f32[5,384,256]{2,1,0:T(8,128)} %get-tuple-element.36.refs_0_, bf16[2,384,256]{2,1,0:T(8,128)(2,1)} %collective-permute-done.16.refs_1_, ...), custom_call_target="tpu_custom_call" | custom-call | flops 1024 | bytes 1024 | tf_op jit(solution)/shard_map/pallas_call | solution.py:335
  164.0 1.3 reshape.18
  165.3 30.2 %all_to_all.5 = bf16[32,60,256]{2,1,0:T(8,128)(2,1)S(1)} all-to-all(bf16[32,60,256]{2,1,0:T(8,128)(2,1)S(1)} %reshape.18), channel_id=1, replica_groups=mesh['band'=16,'sample'=2] {'band','sample'}, dimensions={0} | all-to-all | bytes 1966080 | tf_op jit(solution)/shard_map/all_to_all | solution.py:408
  195.5 1.1 reshape.19
  (55 shorter events, 0.9 us)
Async XLA Ops:
  0.0 142.4 %copy-start = (bf16[1024,256]{1,0:T(8,128)(2,1)S(1)}, bf16[1024,256]{1,0:T(8,128)(2,1)}, u32[]{:S(2)}) copy-start(bf16[1024,256]{1,0:T(8,128)(2,1)} %param.13) | copy-start | bytes 1572868
  0.0 2.5 %copy-start.2 = (bf16[5,384,1024]{2,1,0:T(8,128)(2,1)S(1)}, bf16[5,384,1024]{2,1,0:T(8,128)(2,1)}, u32[]{:S(2)}) copy-start(bf16[5,384,1024]{2,1,0:T(8,128)(2,1)} %x_ref.13) | copy-start | bytes 11796484
  1.5 2.7 %collective-permute-start = (bf16[5,96,1024]{2,1,0:T(8,128)(2,1)S(1)}, bf16[5,96,1024]{2,1,0:T(8,128)(2,1)S(1)}, u32[]{:S(2)}, u32[]{:S(2)}) collective-permute-start(bf16[5,96,1024]{2,1,0:T(8,128)(2,1)S(1)} %pad_maximum_fusion), channel_id=1, source_target_pairs={{0,1},{1,0},{2,3},{3,2},{4,5},{5,4},{6,7},{7,6},{8,9},{9,8},{10,11... | collective-permute-start | bytes 2949128 | tf_op jit(solution)/shard_map/ppermute | solution.py:32
  4.3 73.6 %copy-start.3 = (bf16[5,48,1024]{2,1,0:T(8,128)(2,1)}, bf16[5,48,1024]{2,1,0:T(8,128)(2,1)S(1)}, u32[]{:S(2)}) copy-start(bf16[5,48,1024]{2,1,0:T(8,128)(2,1)S(1)} %get-tuple-element.47.after_ref) | copy-start | bytes 1474564
  4.3 73.6 %copy-start.4 = (bf16[5,48,1024]{2,1,0:T(8,128)(2,1)}, bf16[5,48,1024]{2,1,0:T(8,128)(2,1)S(1)}, u32[]{:S(2)}) copy-start(bf16[5,48,1024]{2,1,0:T(8,128)(2,1)S(1)} %get-tuple-element.48.before_ref) | copy-start | bytes 1474564
  4.3 1.3 collective-permute-start.2
  5.5 4.4 %collective-permute-start.6 = (f32[1024]{0:T(1024)S(1)}, f32[1024]{0:T(1024)S(1)}, u32[]{:S(2)}, u32[]{:S(2)}) collective-permute-start(f32[1024]{0:T(1024)S(1)} %add.18.refs_1_), channel_id=1, source_target_pairs={{0,2},{2,0},{4,6},{6,4},{8,10},{10,8},{12,14},{14,12},{16,18},{18,... | collective-permute-start | bytes 12296 | tf_op jit(solution)/shard_map/ppermute | solution.py:81
  10.0 5.0 %copy-start.1 = (bf16[3,3,3,1024,256]{4,3,2,1,0:T(8,128)(2,1)S(1)}, bf16[3,3,3,1024,256]{4,3,2,1,0:T(8,128)(2,1)}, u32[]{:S(2)}) copy-start(bf16[3,3,3,1024,256]{4,3,2,1,0:T(8,128)(2,1)} %refs_0_.13) | copy-start | bytes 42467332
  19.0 65.9 %collective-permute-start.12 = (bf16[4,384,256]{2,1,0:T(8,128)(2,1)S(1)}, bf16[4,384,256]{2,1,0:T(8,128)(2,1)}, u32[]{:S(2)}, u32[]{:S(2)}) collective-permute-start(bf16[4,384,256]{2,1,0:T(8,128)(2,1)S(1)} %get-tuple-element.35), channel_id=1, source_target_pairs={{10,8},{11,9},{12,10},{13,11},{14,12},{15,13},{16,22},{17,23},{18,... | collective-permute-start | bytes 2359304 | tf_op jit(solution)/shard_map/ppermute | solution.py:62
  24.7 50.2 %collective-permute-start.5 = (bf16[1,384,256]{2,1,0:T(8,128)(2,1)S(1)}, bf16[1,384,256]{2,1,0:T(8,128)(2,1)S(1)}, u32[]{:S(2)}, u32[]{:S(2)}) collective-permute-start(bf16[1,384,256]{2,1,0:T(8,128)(2,1)S(1)} %get-tuple-element.30), channel_id=1, source_target_pairs={{16,0},{17,1},{18,2},{19,3},{20,4},{21,5},{22,6},{23,7},{24,8},{25... | collective-permute-start | bytes 589832 | tf_op jit(solution)/shard_map/ppermute | solution.py:62
  26.0 3.7 %collective-permute-start.7 = (f32[1024]{0:T(1024)S(1)}, f32[1024]{0:T(1024)S(1)}, u32[]{:S(2)}, u32[]{:S(2)}) collective-permute-start(f32[1024]{0:T(1024)S(1)} %add.19.refs_1_), channel_id=1, source_target_pairs={{0,4},{2,6},{4,0},{6,2},{8,12},{10,14},{12,8},{14,10},{16,20},{18,... | collective-permute-start | bytes 12296 | tf_op jit(solution)/shard_map/ppermute | solution.py:81
  29.7 5.0 %collective-permute-start.14 = (f32[1024]{0:T(1024)S(1)}, f32[1024]{0:T(1024)S(1)}, u32[]{:S(2)}, u32[]{:S(2)}) collective-permute-start(f32[1024]{0:T(1024)S(1)} %add.20.refs_1_), channel_id=1, source_target_pairs={{0,8},{2,10},{4,12},{6,14},{8,0},{10,2},{12,4},{14,6},{16,24},{18,... | collective-permute-start | bytes 12296 | tf_op jit(solution)/shard_map/ppermute | solution.py:81
  38.8 44.7 %collective-permute-start.19 = (bf16[3,384,256]{2,1,0:T(8,128)(2,1)S(1)}, bf16[3,384,256]{2,1,0:T(8,128)(2,1)}, u32[]{:S(2)}, u32[]{:S(2)}) collective-permute-start(bf16[3,384,256]{2,1,0:T(8,128)(2,1)S(1)} %get-tuple-element.40), channel_id=1, source_target_pairs={{4,4},{5,1},{6,6},{7,3},{8,0},{9,13},{10,2},{11,15},{12,12},{13,9}... | collective-permute-start | bytes 1769480 | tf_op jit(solution)/shard_map/ppermute | solution.py:62
  40.1 33.3 %collective-permute-start.15 = (f32[1024]{0:T(1024)S(1)}, f32[1024]{0:T(1024)S(1)}, u32[]{:S(2)}, u32[]{:S(2)}) collective-permute-start(f32[1024]{0:T(1024)S(1)} %add.21.refs_1_), channel_id=1, source_target_pairs={{0,16},{2,18},{4,20},{6,22},{8,24},{10,26},{12,28},{14,30},{16,0},... | collective-permute-start | bytes 12296 | tf_op jit(solution)/shard_map/ppermute | solution.py:81
  45.4 54.3 %collective-permute-start.1 = (bf16[4,384,256]{2,1,0:T(8,128)(2,1)S(1)}, bf16[4,384,256]{2,1,0:T(8,128)(2,1)S(1)}, u32[]{:S(2)}, u32[]{:S(2)}) collective-permute-start(bf16[4,384,256]{2,1,0:T(8,128)(2,1)S(1)} %get-tuple-element.24), channel_id=1, source_target_pairs={{14,0},{15,1},{16,2},{17,3},{18,4},{19,5},{20,6},{21,7},{22,8},{23... | collective-permute-start | bytes 2359304 | tf_op jit(solution)/shard_map/ppermute | solution.py:62
  73.4 8.6 %collective-permute-start.3 = (bf16[1,384,256]{2,1,0:T(8,128)(2,1)S(1)}, bf16[1,384,256]{2,1,0:T(8,128)(2,1)S(1)}, u32[]{:S(2)}, u32[]{:S(2)}) collective-permute-start(bf16[1,384,256]{2,1,0:T(8,128)(2,1)S(1)} %get-tuple-element.28), channel_id=1, source_target_pairs={{0,16},{1,17},{2,18},{3,19},{4,20},{5,21},{6,22},{7,23},{8,24},{9,... | collective-permute-start | bytes 589832 | tf_op jit(solution)/shard_map/ppermute | solution.py:62
  74.9 7.2 %copy-start.10 = (bf16[1,384,256]{2,1,0:T(8,128)(2,1)}, bf16[1,384,256]{2,1,0:T(8,128)(2,1)S(1)}, u32[]{:S(2)}) copy-start(bf16[1,384,256]{2,1,0:T(8,128)(2,1)S(1)} %collective-permute-done.5.refs_4_) | copy-start | bytes 589828
  74.9 19.6 %collective-permute-start.8 = (bf16[4,384,256]{2,1,0:T(8,128)(2,1)S(1)}, bf16[4,384,256]{2,1,0:T(8,128)(2,1)}, u32[]{:S(2)}, u32[]{:S(2)}) collective-permute-start(bf16[4,384,256]{2,1,0:T(8,128)(2,1)S(1)} %get-tuple-element.32), channel_id=1, source_target_pairs={{0,2},{1,3},{2,4},{3,5},{4,6},{5,7},{6,0},{7,1},{8,10},{9,11},{10,... | collective-permute-start | bytes 2359304 | tf_op jit(solution)/shard_map/ppermute | solution.py:62
  82.0 17.6 %copy-start.11 = (bf16[1,384,256]{2,1,0:T(8,128)(2,1)}, bf16[1,384,256]{2,1,0:T(8,128)(2,1)S(1)}, u32[]{:S(2)}) copy-start(bf16[1,384,256]{2,1,0:T(8,128)(2,1)S(1)} %collective-permute-done.3.refs_1_) | copy-start | bytes 589828
  82.0 16.3 %collective-permute-start.17 = (bf16[3,384,256]{2,1,0:T(8,128)(2,1)S(1)}, bf16[3,384,256]{2,1,0:T(8,128)(2,1)}, u32[]{:S(2)}, u32[]{:S(2)}) collective-permute-start(bf16[3,384,256]{2,1,0:T(8,128)(2,1)S(1)} %get-tuple-element.38), channel_id=1, source_target_pairs={{0,0},{1,5},{2,2},{3,7},{4,12},{5,1},{6,14},{7,3},{8,8},{9,13},{10... | collective-permute-start | bytes 1769480 | tf_op jit(solution)/shard_map/ppermute | solution.py:62
  83.5 46.2 %collective-permute-start.4 = (bf16[4,384,256]{2,1,0:T(8,128)(2,1)S(1)}, bf16[4,384,256]{2,1,0:T(8,128)(2,1)S(1)}, u32[]{:S(2)}, u32[]{:S(2)}) collective-permute-start(bf16[4,384,256]{2,1,0:T(8,128)(2,1)S(1)} %get-tuple-element.29), channel_id=1, source_target_pairs={{0,14},{1,15},{2,16},{3,17},{4,18},{5,19},{6,20},{7,21},{8,22},{9,... | collective-permute-start | bytes 2359304 | tf_op jit(solution)/shard_map/ppermute | solution.py:62
  84.9 46.2 %collective-permute-start.13 = (bf16[4,384,256]{2,1,0:T(8,128)(2,1)}, bf16[4,384,256]{2,1,0:T(8,128)(2,1)S(1)}, u32[]{:S(2)}, u32[]{:S(2)}) collective-permute-start(bf16[4,384,256]{2,1,0:T(8,128)(2,1)} %collective-permute-done.12), channel_id=1, source_target_pairs={{8,0},{9,1},{10,2},{11,3},{12,4},{13,5},{22,6},{23,7},{16,8},{17,9... | collective-permute-start | bytes 2359304 | tf_op jit(solution)/shard_map/ppermute | solution.py:67
  94.4 49.8 %collective-permute-start.9 = (bf16[4,384,256]{2,1,0:T(8,128)(2,1)}, bf16[4,384,256]{2,1,0:T(8,128)(2,1)}, u32[]{:S(2)}, u32[]{:S(2)}) collective-permute-start(bf16[4,384,256]{2,1,0:T(8,128)(2,1)} %collective-permute-done.8), channel_id=1, source_target_pairs={{2,10},{3,11},{4,12},{5,13},{6,14},{7,15},{0,16},{1,17},{10,18},{1... | collective-permute-start | bytes 2359304 | tf_op jit(solution)/shard_map/ppermute | solution.py:67
  98.3 28.1 %collective-permute-start.11 = (bf16[1,384,256]{2,1,0:T(8,128)(2,1)S(1)}, bf16[1,384,256]{2,1,0:T(8,128)(2,1)S(1)}, u32[]{:S(2)}, u32[]{:S(2)}) collective-permute-start(bf16[1,384,256]{2,1,0:T(8,128)(2,1)S(1)} %get-tuple-element.34), channel_id=1, source_target_pairs={{8,0},{9,1},{10,2},{11,3},{12,4},{13,5},{14,6},{15,7},{16,8},{17,9... | collective-permute-start | bytes 589832 | tf_op jit(solution)/shard_map/ppermute | solution.py:62
  99.7 11.4 %copy-start.5 = (bf16[4,384,256]{2,1,0:T(8,128)(2,1)}, bf16[4,384,256]{2,1,0:T(8,128)(2,1)S(1)}, u32[]{:S(2)}) copy-start(bf16[4,384,256]{2,1,0:T(8,128)(2,1)S(1)} %collective-permute-done.1.refs_7_.refs_3_) | copy-start | bytes 2359300
  99.7 41.4 %copy-start.16 = (s32[5,384]{1,0:T(8,128)S(1)}, s32[5,384]{1,0:T(8,128)}, u32[]{:S(2)}) copy-start(s32[5,384]{1,0:T(8,128)} %param.19) | copy-start | bytes 23044
  99.7 42.7 %copy-start.14 = (f32[5,256]{1,0:T(8,128)S(1)}, f32[5,256]{1,0:T(8,128)}, u32[]{:S(2)}) copy-start(f32[5,256]{1,0:T(8,128)} %gain.3) | copy-start | bytes 15364
  99.7 42.7 %copy-start.15 = (f32[5,256]{1,0:T(8,128)S(1)}, f32[5,256]{1,0:T(8,128)}, u32[]{:S(2)}) copy-start(f32[5,256]{1,0:T(8,128)} %shift_term.3) | copy-start | bytes 15364
  99.7 28.1 %collective-permute-start.10 = (bf16[1,384,256]{2,1,0:T(8,128)(2,1)S(1)}, bf16[1,384,256]{2,1,0:T(8,128)(2,1)S(1)}, u32[]{:S(2)}, u32[]{:S(2)}) collective-permute-start(bf16[1,384,256]{2,1,0:T(8,128)(2,1)S(1)} %get-tuple-element.33), channel_id=1, source_target_pairs={{0,8},{1,9},{2,10},{3,11},{4,12},{5,13},{6,14},{7,15},{8,16},{9,17... | collective-permute-start | bytes 589832 | tf_op jit(solution)/shard_map/ppermute | solution.py:62
  126.5 14.6 %copy-start.12 = (bf16[1,384,256]{2,1,0:T(8,128)(2,1)}, bf16[1,384,256]{2,1,0:T(8,128)(2,1)S(1)}, u32[]{:S(2)}) copy-start(bf16[1,384,256]{2,1,0:T(8,128)(2,1)S(1)} %collective-permute-done.11.refs_8_) | copy-start | bytes 589828
  126.5 27.8 %collective-permute-start.18 = (bf16[3,384,256]{2,1,0:T(8,128)(2,1)}, bf16[3,384,256]{2,1,0:T(8,128)(2,1)S(1)}, u32[]{:S(2)}, u32[]{:S(2)}) collective-permute-start(bf16[3,384,256]{2,1,0:T(8,128)(2,1)} %collective-permute-done.17), channel_id=1, source_target_pairs={{0,4},{5,5},{2,6},{7,7},{12,8},{1,9},{14,10},{3,11},{8,12},{13,13}... | collective-permute-start | bytes 1769480 | tf_op jit(solution)/shard_map/ppermute | solution.py:67
  127.8 13.3 %copy-start.13 = (bf16[1,384,256]{2,1,0:T(8,128)(2,1)}, bf16[1,384,256]{2,1,0:T(8,128)(2,1)S(1)}, u32[]{:S(2)}) copy-start(bf16[1,384,256]{2,1,0:T(8,128)(2,1)S(1)} %collective-permute-done.10.refs_7_) | copy-start | bytes 589828
  127.8 26.5 %collective-permute-start.20 = (bf16[3,384,256]{2,1,0:T(8,128)(2,1)}, bf16[3,384,256]{2,1,0:T(8,128)(2,1)S(1)}, u32[]{:S(2)}, u32[]{:S(2)}) collective-permute-start(bf16[3,384,256]{2,1,0:T(8,128)(2,1)} %collective-permute-done.19), channel_id=1, source_target_pairs={{4,0},{1,1},{6,2},{3,3},{0,4},{13,5},{2,6},{15,7},{12,8},{9,9},{14... | collective-permute-start | bytes 1769480 | tf_op jit(solution)/shard_map/ppermute | solution.py:67
  129.8 14.5 %copy-start.6 = (bf16[4,384,256]{2,1,0:T(8,128)(2,1)}, bf16[4,384,256]{2,1,0:T(8,128)(2,1)S(1)}, u32[]{:S(2)}) copy-start(bf16[4,384,256]{2,1,0:T(8,128)(2,1)S(1)} %collective-permute-done.4.refs_2_) | copy-start | bytes 2359300
  129.8 22.1 %collective-permute-start.21 = (bf16[2,384,256]{2,1,0:T(8,128)(2,1)S(1)}, bf16[2,384,256]{2,1,0:T(8,128)(2,1)}, u32[]{:S(2)}, u32[]{:S(2)}) collective-permute-start(bf16[2,384,256]{2,1,0:T(8,128)(2,1)S(1)} %get-tuple-element.42), channel_id=1, source_target_pairs={{6,0},{7,1},{8,2},{9,3},{10,4},{11,5},{12,6},{13,7},{14,8},{15,9},... | collective-permute-start | bytes 1179656 | tf_op jit(solution)/shard_map/ppermute | solution.py:62
  131.1 10.0 %copy-start.7 = (bf16[4,384,256]{2,1,0:T(8,128)(2,1)}, bf16[4,384,256]{2,1,0:T(8,128)(2,1)S(1)}, u32[]{:S(2)}) copy-start(bf16[4,384,256]{2,1,0:T(8,128)(2,1)S(1)} %collective-permute-done.13.refs_9_) | copy-start | bytes 2359300
  131.1 23.2 %collective-permute-start.16 = (bf16[2,384,256]{2,1,0:T(8,128)(2,1)S(1)}, bf16[2,384,256]{2,1,0:T(8,128)(2,1)}, u32[]{:S(2)}, u32[]{:S(2)}) collective-permute-start(bf16[2,384,256]{2,1,0:T(8,128)(2,1)S(1)} %get-tuple-element.37), channel_id=1, source_target_pairs={{0,6},{1,7},{2,8},{3,9},{4,10},{5,11},{6,12},{7,13},{8,14},{9,15},... | collective-permute-start | bytes 1179656 | tf_op jit(solution)/shard_map/ppermute | solution.py:62
  154.3 0.8 copy-start.8
  154.3 1.0 copy-start.9

commit v7 on v6

--- a/solution.py
+++ b/solution.py
@@ -376,7 +376,7 @@
     totals, steps = total_over_devices(
         lax.optimization_barrier((jnp.sum(features, axis=(0, 1), dtype=jnp.float32), before))[0]
     )
-    order = ((2, 2), (2, 0), (1, 2), (1, 0), (0, 2), (0, 0))
+    order = ((2, 2), (2, 0), (1, 2), (1, 0), (0, 0), (0, 2))
     centre, base = {}, None
     for place, (branch, row_tap) in enumerate(order):
         if place == own_place:

time: 197 us -> 196 us (level)
  waiting for transfers between devices: 35.9 us -> 25.1 us
  starting transfers between devices: 59.5 us -> 65.1 us
  blocking collectives: 30.2 us -> 33.7 us
    ppermute x5, waiting for transfers between devices: 24.2 us -> 5.58 us  [total_over_devices(): lax.ppermute(values, axis, [(i, i ^ step) for i in range(size)])]
    ppermute x12, waiting for transfers between devices: 10.7 us -> 18.5 us  [passed_along(): array = lax.ppermute(array, ('band', 'sample'), first)]
    ppermute x12, starting transfers between devices: 36.5 us -> 42.3 us  [passed_along(): array = lax.ppermute(array, ('band', 'sample'), first)]
    all_to_all x1, blocking collectives: 30.2 us -> 33.7 us  [shards(): lax.all_to_all(outgoing, ('band', 'sample'), split_axis=0, concat_axis=0,...]
  transfers between devices with their start and end apart: 22 -> 22, of which waited for: 8 -> 7; matrix products, arithmetic and copies ran while one was open for 2% -> 2% of each run, Pallas kernels for 22% -> 22%
where the time goes in v7:
time: 196 us; the launch traced here: 195 us
  starting transfers between devices  65.1 us (33%)
  Pallas kernels  56.2 us (29%)
  blocking collectives  33.7 us (17%)
  waiting for transfers between devices  25.1 us (13%)
  local copies, waits for them, and re-layouts  11.8 us (6%)
    ppermute x12, starting transfers between devices, passed_along(): array = lax.ppermute(array, ('band', 'sample'), first)  42.3 us
    all_to_all x1, blocking collectives, shards(): lax.all_to_all(outgoing, ('band', 'sample'), split_axis=0, concat_axis=0,...  33.7 us
    pallas_call x6, Pallas kernels, row_taps(): pl.pallas_call(functools.partial(taps_body, plan, row_count, len(tokens))...  24.5 us
    ppermute x12, waiting for transfers between devices, passed_along(): array = lax.ppermute(array, ('band', 'sample'), first)  18.5 us
    pallas_call x2, Pallas kernels, join(): pl.pallas_call(functools.partial(join_body, plan, remainders, tail is not...  16.3 us
    pallas_call x1, Pallas kernels, own_rows(): pl.pallas_call(functools.partial(own_body, plan, point_operands is not No...  15.4 us
    ppermute x5, starting transfers between devices, total_over_devices(): lax.ppermute(values, axis, [(i, i ^ step) for i in range(size)])  13.3 us
    ppermute x4, starting transfers between devices, passed_along(): array = lax.ppermute(array, ('band', 'sample'), second)  8.95 us
  transfers between devices with their start and end apart: 22, of which 7 were waited for; matrix products, arithmetic and copies ran while one was open for 2% of the time, Pallas kernels for 22%

profile of v7, /device:TPU:0, one launch (start us, length us, event | category | flops | bytes accessed | tf_op | source)
XLA Modules:
  0.0 195.0 jit_solution(5444801849732365330)
XLA Ops:
  0.0 1.4 fusion.10
  1.5 0.5 collective-permute-start
  2.0 0.5 copy-done.2
  2.5 0.7 convert_reduce_fusion
  3.2 1.0 collective-permute-done
  4.3 0.4 collective-permute-start.2
  4.7 0.8 collective-permute-done.2
  5.5 2.8 %collective-permute-start.6 = (f32[1024]{0:T(1024)S(1)}, f32[1024]{0:T(1024)S(1)}, u32[]{:S(2)}, u32[]{:S(2)}) collective-permute-start(f32[1024]{0:T(1024)S(1)} %add.18.refs_1_), channel_id=1, source_target_pairs={{0,2},{2,0},{4,6},{6,4},{8,10},{10,8},{12,14},{14,12},{16,18},{18,... | collective-permute-start | bytes 12296 | tf_op jit(solution)/shard_map/ppermute | solution.py:81
  8.4 1.6 collective-permute-done.6
  10.0 5.0 %copy-done.1 = bf16[3,3,3,1024,256]{4,3,2,1,0:T(8,128)(2,1)S(1)} copy-done((bf16[3,3,3,1024,256]{4,3,2,1,0:T(8,128)(2,1)S(1)}, bf16[3,3,3,1024,256]{4,3,2,1,0:T(8,128)(2,1)}, u32[]{:S(2)}) %copy-start.1) | copy-done | bytes 14155800
  15.0 4.0 %shard_map.104 = (bf16[1,384,256]{2,1,0:T(8,128)(2,1)S(1)}, bf16[4,384,256]{2,1,0:T(8,128)(2,1)S(1)}) custom-call(bf16[5,384,1024]{2,1,0:T(8,128)(2,1)S(1)} %copy-done.2, bf16[5,48,1024]{2,1,0:T(8,128)(2,1)S(1)} %get-tuple-element.48.before_ref, bf16[5,48,1024]{2,1,0:T(8,128)(2,1)S(1)} %get-tuple-element.47.after_ref, ...), custom_call_target="tpu_custom_call" | custom-call | flops 1024 | bytes 1024 | tf_op jit(solution)/shard_map/pallas_call | solution.py:164
  19.0 1.6 collective-permute-start.12
  20.6 4.1 %shard_map.100 = (bf16[4,384,256]{2,1,0:T(8,128)(2,1)S(1)}, bf16[1,384,256]{2,1,0:T(8,128)(2,1)S(1)}) custom-call(bf16[5,384,1024]{2,1,0:T(8,128)(2,1)S(1)} %copy-done.2, bf16[5,48,1024]{2,1,0:T(8,128)(2,1)S(1)} %get-tuple-element.48.before_ref, bf16[5,48,1024]{2,1,0:T(8,128)(2,1)S(1)} %get-tuple-element.47.after_ref, bf16[3,3,3,1024,256]{4,3,2,1,0:T(8,128)(2,1)S(1)} %copy-done.1), custom_call_target="tpu_custom_call" | custom-call | flops 1024 | bytes 1024 | tf_op jit(solution)/shard_map/pallas_call | solution.py:164
  24.7 1.3 collective-permute-start.5
  26.0 2.1 %collective-permute-start.7 = (f32[1024]{0:T(1024)S(1)}, f32[1024]{0:T(1024)S(1)}, u32[]{:S(2)}, u32[]{:S(2)}) collective-permute-start(f32[1024]{0:T(1024)S(1)} %add.19.refs_1_), channel_id=1, source_target_pairs={{0,4},{2,6},{4,0},{6,2},{8,12},{10,14},{12,8},{14,10},{16,20},{18,... | collective-permute-start | bytes 12296 | tf_op jit(solution)/shard_map/ppermute | solution.py:81
  28.1 1.6 collective-permute-done.7
  29.7 3.4 %collective-permute-start.14 = (f32[1024]{0:T(1024)S(1)}, f32[1024]{0:T(1024)S(1)}, u32[]{:S(2)}, u32[]{:S(2)}) collective-permute-start(f32[1024]{0:T(1024)S(1)} %add.20.refs_1_), channel_id=1, source_target_pairs={{0,8},{2,10},{4,12},{6,14},{8,0},{10,2},{12,4},{14,6},{16,24},{18,... | collective-permute-start | bytes 12296 | tf_op jit(solution)/shard_map/ppermute | solution.py:81
  33.0 1.6 collective-permute-done.14
  34.6 4.2 %shard_map.106 = (bf16[2,384,256]{2,1,0:T(8,128)(2,1)S(1)}, bf16[3,384,256]{2,1,0:T(8,128)(2,1)S(1)}) custom-call(bf16[5,384,1024]{2,1,0:T(8,128)(2,1)S(1)} %copy-done.2, bf16[5,48,1024]{2,1,0:T(8,128)(2,1)S(1)} %get-tuple-element.48.before_ref, bf16[5,48,1024]{2,1,0:T(8,128)(2,1)S(1)} %get-tuple-element.47.after_ref, ...), custom_call_target="tpu_custom_call" | custom-call | flops 1024 | bytes 1024 | tf_op jit(solution)/shard_map/pallas_call | solution.py:164
  38.8 1.5 collective-permute-start.16
  40.3 4.6 %collective-permute-start.18 = (f32[1024]{0:T(1024)S(1)}, f32[1024]{0:T(1024)S(1)}, u32[]{:S(2)}, u32[]{:S(2)}) collective-permute-start(f32[1024]{0:T(1024)S(1)} %add.21.refs_1_), channel_id=1, source_target_pairs={{0,16},{2,18},{4,20},{6,22},{8,24},{10,26},{12,28},{14,30},{16,0},... | collective-permute-start | bytes 12296 | tf_op jit(solution)/shard_map/ppermute | solution.py:81
  44.8 1.3 collective-permute-start.1
  46.1 4.1 %shard_map.102 = (bf16[1,384,256]{2,1,0:T(8,128)(2,1)S(1)}, bf16[4,384,256]{2,1,0:T(8,128)(2,1)S(1)}) custom-call(bf16[5,384,1024]{2,1,0:T(8,128)(2,1)S(1)} %copy-done.2, bf16[5,48,1024]{2,1,0:T(8,128)(2,1)S(1)} %get-tuple-element.48.before_ref, bf16[5,48,1024]{2,1,0:T(8,128)(2,1)S(1)} %get-tuple-element.47.after_ref, ...), custom_call_target="tpu_custom_call" | custom-call | flops 1024 | bytes 1024 | tf_op jit(solution)/shard_map/pallas_call | solution.py:164
  50.2 4.0 %shard_map.103 = (bf16[4,384,256]{2,1,0:T(8,128)(2,1)S(1)}, bf16[1,384,256]{2,1,0:T(8,128)(2,1)S(1)}) custom-call(bf16[5,384,1024]{2,1,0:T(8,128)(2,1)S(1)} %copy-done.2, bf16[5,48,1024]{2,1,0:T(8,128)(2,1)S(1)} %get-tuple-element.48.before_ref, bf16[5,48,1024]{2,1,0:T(8,128)(2,1)S(1)} %get-tuple-element.47.after_ref, ...), custom_call_target="tpu_custom_call" | custom-call | flops 1024 | bytes 1024 | tf_op jit(solution)/shard_map/pallas_call | solution.py:164
  54.3 5.7 %collective-permute-start.3 = (bf16[1,384,256]{2,1,0:T(8,128)(2,1)S(1)}, bf16[1,384,256]{2,1,0:T(8,128)(2,1)S(1)}, u32[]{:S(2)}, u32[]{:S(2)}) collective-permute-start(bf16[1,384,256]{2,1,0:T(8,128)(2,1)S(1)} %get-tuple-element.28), channel_id=1, source_target_pairs={{0,16},{1,17},{2,18},{3,19},{4,20},{5,21},{6,22},{7,23},{8,24},{9,... | collective-permute-start | bytes 589832 | tf_op jit(solution)/shard_map/ppermute | solution.py:62
  60.0 6.1 %collective-permute-start.8 = (bf16[4,384,256]{2,1,0:T(8,128)(2,1)S(1)}, bf16[4,384,256]{2,1,0:T(8,128)(2,1)}, u32[]{:S(2)}, u32[]{:S(2)}) collective-permute-start(bf16[4,384,256]{2,1,0:T(8,128)(2,1)S(1)} %get-tuple-element.32), channel_id=1, source_target_pairs={{0,2},{1,3},{2,4},{3,5},{4,6},{5,7},{6,0},{7,1},{8,10},{9,11},{10,... | collective-permute-start | bytes 2359304 | tf_op jit(solution)/shard_map/ppermute | solution.py:62
  66.2 4.2 %shard_map.107 = (bf16[3,384,256]{2,1,0:T(8,128)(2,1)S(1)}, bf16[2,384,256]{2,1,0:T(8,128)(2,1)S(1)}) custom-call(bf16[5,384,1024]{2,1,0:T(8,128)(2,1)S(1)} %copy-done.2, bf16[5,48,1024]{2,1,0:T(8,128)(2,1)S(1)} %get-tuple-element.48.before_ref, bf16[5,48,1024]{2,1,0:T(8,128)(2,1)S(1)} %get-tuple-element.47.after_ref, ...), custom_call_target="tpu_custom_call" | custom-call | flops 1024 | bytes 1024 | tf_op jit(solution)/shard_map/pallas_call | solution.py:164
  70.4 1.3 collective-permute-start.19
  71.7 2.3 %collective-permute-start.4 = (bf16[4,384,256]{2,1,0:T(8,128)(2,1)S(1)}, bf16[4,384,256]{2,1,0:T(8,128)(2,1)S(1)}, u32[]{:S(2)}, u32[]{:S(2)}) collective-permute-start(bf16[4,384,256]{2,1,0:T(8,128)(2,1)S(1)} %get-tuple-element.29), channel_id=1, source_target_pairs={{0,14},{1,15},{2,16},{3,17},{4,18},{5,19},{6,20},{7,21},{8,22},{9,... | collective-permute-start | bytes 2359304 | tf_op jit(solution)/shard_map/ppermute | solution.py:62
  74.0 1.3 collective-permute-start.13
  75.3 17.8 %collective-permute-done.8 = bf16[4,384,256]{2,1,0:T(8,128)(2,1)} collective-permute-done((bf16[4,384,256]{2,1,0:T(8,128)(2,1)S(1)}, bf16[4,384,256]{2,1,0:T(8,128)(2,1)}, u32[]{:S(2)}, u32[]{:S(2)}) %collective-permute-start.8) | collective-permute-done | bytes 786464 | tf_op jit(solution)/shard_map/ppermute | solution.py:62
  93.1 4.4 %collective-permute-start.9 = (bf16[4,384,256]{2,1,0:T(8,128)(2,1)}, bf16[4,384,256]{2,1,0:T(8,128)(2,1)}, u32[]{:S(2)}, u32[]{:S(2)}) collective-permute-start(bf16[4,384,256]{2,1,0:T(8,128)(2,1)} %collective-permute-done.8), channel_id=1, source_target_pairs={{2,10},{3,11},{4,12},{5,13},{6,14},{7,15},{0,16},{1,17},{10,18},{1... | collective-permute-start | bytes 2359304 | tf_op jit(solution)/shard_map/ppermute | solution.py:67
  97.5 1.3 collective-permute-start.11
  98.9 9.2 %collective-permute-start.10 = (bf16[1,384,256]{2,1,0:T(8,128)(2,1)S(1)}, bf16[1,384,256]{2,1,0:T(8,128)(2,1)S(1)}, u32[]{:S(2)}, u32[]{:S(2)}) collective-permute-start(bf16[1,384,256]{2,1,0:T(8,128)(2,1)S(1)} %get-tuple-element.33), channel_id=1, source_target_pairs={{0,8},{1,9},{2,10},{3,11},{4,12},{5,13},{6,14},{7,15},{8,16},{9,17... | collective-permute-start | bytes 589832 | tf_op jit(solution)/shard_map/ppermute | solution.py:62
  108.1 15.4 %shard_map.101 = (f32[5,384,256]{2,1,0:T(8,128)}, f32[5,384,256]{2,1,0:T(8,128)}, f32[5,384,256]{2,1,0:T(8,128)}, f32[5,384,256]{2,1,0:T(8,128)}) custom-call(bf16[5,384,1024]{2,1,0:T(8,128)(2,1)} %x_ref.13, bf16[5,48,1024]{2,1,0:T(8,128)(2,1)} %copy-done.4, bf16[5,48,1024]{2,1,0:T(8,128)(2,1)} %copy-done.3, bf16[3,3,3,1024,256]{4,3,2,1,0:T(8,128)(2,1)} %refs_0_.13, ...), custom_call_target="tpu_custom_call" | custom-call | flops 1024 | bytes 1024 | tf_op jit(solution)/shard_map/pallas_call | solution.py:241
  123.5 1.3 collective-permute-start.17
  124.9 1.9 collective-permute-start.20
  126.8 9.3 %collective-permute-start.15 = (bf16[2,384,256]{2,1,0:T(8,128)(2,1)S(1)}, bf16[2,384,256]{2,1,0:T(8,128)(2,1)}, u32[]{:S(2)}, u32[]{:S(2)}) collective-permute-start(bf16[2,384,256]{2,1,0:T(8,128)(2,1)S(1)} %get-tuple-element.37), channel_id=1, source_target_pairs={{0,6},{1,7},{2,8},{3,9},{4,10},{5,11},{6,12},{7,13},{8,14},{9,15},... | collective-permute-start | bytes 1179656 | tf_op jit(solution)/shard_map/ppermute | solution.py:62
  136.2 1.5 collective-permute-start.21
  137.7 1.3 copy.13
  139.0 1.8 fusion.4.refs_5_
  140.9 7.6 %shard_map.105.base_ref = f32[5,384,256]{2,1,0:T(8,128)} custom-call(f32[5,384,256]{2,1,0:T(8,128)} %get-tuple-element.25.base_ref, bf16[1280,256]{1,0:T(8,128)(2,1)} %w_project.3, f32[5,256]{1,0:T(8,128)} %gain.3, f32[5,256]{1,0:T(8,128)} %shift_term.3, f32[5,384,256]{2,1,0:T(8,128)} %get-tuple-element.26.refs_0_, bf16[1,384,256]{2,1,0:T(8,128)(2,1)} %copy-done.11, ...), custom_call_target="tpu_custom_call" | custom-call | flops 1024 | bytes 1024 | tf_op jit(solution)/shard_map/pallas_call | solution.py:335
  148.5 0.7 collective-permute-done.15.refs_1_
  149.2 0.8 copy-done.8
  150.2 8.6 %shard_map.108 = bf16[1920,256]{1,0:T(8,128)(2,1)} custom-call(f32[5,384,256]{2,1,0:T(8,128)} %shard_map.105.base_ref, bf16[1280,256]{1,0:T(8,128)(2,1)} %w_project.3, f32[5,256]{1,0:T(8,128)} %gain.3, f32[5,256]{1,0:T(8,128)} %shift_term.3, f32[5,384,256]{2,1,0:T(8,128)} %get-tuple-element.36.refs_0_, bf16[2,384,256]{2,1,0:T(8,128)(2,1)} %collective-permute-done.15.refs_1_, ...), custom_call_target="tpu_custom_call" | custom-call | flops 1024 | bytes 1024 | tf_op jit(solution)/shard_map/pallas_call | solution.py:335
  158.9 1.3 reshape.18
  160.1 33.7 %all_to_all.5 = bf16[32,60,256]{2,1,0:T(8,128)(2,1)S(1)} all-to-all(bf16[32,60,256]{2,1,0:T(8,128)(2,1)S(1)} %reshape.18), channel_id=1, replica_groups=mesh['band'=16,'sample'=2] {'band','sample'}, dimensions={0} | all-to-all | bytes 1966080 | tf_op jit(solution)/shard_map/all_to_all | solution.py:408
  193.9 1.1 reshape.19
  (55 shorter events, 0.5 us)
Async XLA Ops:
  0.0 139.0 %copy-start = (bf16[1024,256]{1,0:T(8,128)(2,1)S(1)}, bf16[1024,256]{1,0:T(8,128)(2,1)}, u32[]{:S(2)}) copy-start(bf16[1024,256]{1,0:T(8,128)(2,1)} %param.13) | copy-start | bytes 1572868
  0.0 2.5 %copy-start.2 = (bf16[5,384,1024]{2,1,0:T(8,128)(2,1)S(1)}, bf16[5,384,1024]{2,1,0:T(8,128)(2,1)}, u32[]{:S(2)}) copy-start(bf16[5,384,1024]{2,1,0:T(8,128)(2,1)} %x_ref.13) | copy-start | bytes 11796484
  1.5 2.7 %collective-permute-start = (bf16[5,96,1024]{2,1,0:T(8,128)(2,1)S(1)}, bf16[5,96,1024]{2,1,0:T(8,128)(2,1)S(1)}, u32[]{:S(2)}, u32[]{:S(2)}) collective-permute-start(bf16[5,96,1024]{2,1,0:T(8,128)(2,1)S(1)} %pad_maximum_fusion), channel_id=1, source_target_pairs={{0,1},{1,0},{2,3},{3,2},{4,5},{5,4},{6,7},{7,6},{8,9},{9,8},{10,11... | collective-permute-start | bytes 2949128 | tf_op jit(solution)/shard_map/ppermute | solution.py:32
  4.3 61.9 %copy-start.3 = (bf16[5,48,1024]{2,1,0:T(8,128)(2,1)}, bf16[5,48,1024]{2,1,0:T(8,128)(2,1)S(1)}, u32[]{:S(2)}) copy-start(bf16[5,48,1024]{2,1,0:T(8,128)(2,1)S(1)} %get-tuple-element.47.after_ref) | copy-start | bytes 1474564
  4.3 61.9 %copy-start.4 = (bf16[5,48,1024]{2,1,0:T(8,128)(2,1)}, bf16[5,48,1024]{2,1,0:T(8,128)(2,1)S(1)}, u32[]{:S(2)}) copy-start(bf16[5,48,1024]{2,1,0:T(8,128)(2,1)S(1)} %get-tuple-element.48.before_ref) | copy-start | bytes 1474564
  4.3 1.3 collective-permute-start.2
  5.5 4.4 %collective-permute-start.6 = (f32[1024]{0:T(1024)S(1)}, f32[1024]{0:T(1024)S(1)}, u32[]{:S(2)}, u32[]{:S(2)}) collective-permute-start(f32[1024]{0:T(1024)S(1)} %add.18.refs_1_), channel_id=1, source_target_pairs={{0,2},{2,0},{4,6},{6,4},{8,10},{10,8},{12,14},{14,12},{16,18},{18,... | collective-permute-start | bytes 12296 | tf_op jit(solution)/shard_map/ppermute | solution.py:81
  10.0 5.0 %copy-start.1 = (bf16[3,3,3,1024,256]{4,3,2,1,0:T(8,128)(2,1)S(1)}, bf16[3,3,3,1024,256]{4,3,2,1,0:T(8,128)(2,1)}, u32[]{:S(2)}) copy-start(bf16[3,3,3,1024,256]{4,3,2,1,0:T(8,128)(2,1)} %refs_0_.13) | copy-start | bytes 42467332
  19.0 55.1 %collective-permute-start.12 = (bf16[4,384,256]{2,1,0:T(8,128)(2,1)S(1)}, bf16[4,384,256]{2,1,0:T(8,128)(2,1)}, u32[]{:S(2)}, u32[]{:S(2)}) collective-permute-start(bf16[4,384,256]{2,1,0:T(8,128)(2,1)S(1)} %get-tuple-element.35), channel_id=1, source_target_pairs={{10,8},{11,9},{12,10},{13,11},{14,12},{15,13},{16,22},{17,23},{18,... | collective-permute-start | bytes 2359304 | tf_op jit(solution)/shard_map/ppermute | solution.py:62
  24.7 35.3 %collective-permute-start.5 = (bf16[1,384,256]{2,1,0:T(8,128)(2,1)S(1)}, bf16[1,384,256]{2,1,0:T(8,128)(2,1)S(1)}, u32[]{:S(2)}, u32[]{:S(2)}) collective-permute-start(bf16[1,384,256]{2,1,0:T(8,128)(2,1)S(1)} %get-tuple-element.30), channel_id=1, source_target_pairs={{16,0},{17,1},{18,2},{19,3},{20,4},{21,5},{22,6},{23,7},{24,8},{25... | collective-permute-start | bytes 589832 | tf_op jit(solution)/shard_map/ppermute | solution.py:62
  26.0 3.7 %collective-permute-start.7 = (f32[1024]{0:T(1024)S(1)}, f32[1024]{0:T(1024)S(1)}, u32[]{:S(2)}, u32[]{:S(2)}) collective-permute-start(f32[1024]{0:T(1024)S(1)} %add.19.refs_1_), channel_id=1, source_target_pairs={{0,4},{2,6},{4,0},{6,2},{8,12},{10,14},{12,8},{14,10},{16,20},{18,... | collective-permute-start | bytes 12296 | tf_op jit(solution)/shard_map/ppermute | solution.py:81
  29.7 5.0 %collective-permute-start.14 = (f32[1024]{0:T(1024)S(1)}, f32[1024]{0:T(1024)S(1)}, u32[]{:S(2)}, u32[]{:S(2)}) collective-permute-start(f32[1024]{0:T(1024)S(1)} %add.20.refs_1_), channel_id=1, source_target_pairs={{0,8},{2,10},{4,12},{6,14},{8,0},{10,2},{12,4},{14,6},{16,24},{18,... | collective-permute-start | bytes 12296 | tf_op jit(solution)/shard_map/ppermute | solution.py:81
  38.8 32.9 %collective-permute-start.16 = (bf16[3,384,256]{2,1,0:T(8,128)(2,1)S(1)}, bf16[3,384,256]{2,1,0:T(8,128)(2,1)}, u32[]{:S(2)}, u32[]{:S(2)}) collective-permute-start(bf16[3,384,256]{2,1,0:T(8,128)(2,1)S(1)} %get-tuple-element.38), channel_id=1, source_target_pairs={{0,0},{1,5},{2,2},{3,7},{4,12},{5,1},{6,14},{7,3},{8,8},{9,13},{10... | collective-permute-start | bytes 1769480 | tf_op jit(solution)/shard_map/ppermute | solution.py:62
  40.3 14.0 %collective-permute-start.18 = (f32[1024]{0:T(1024)S(1)}, f32[1024]{0:T(1024)S(1)}, u32[]{:S(2)}, u32[]{:S(2)}) collective-permute-start(f32[1024]{0:T(1024)S(1)} %add.21.refs_1_), channel_id=1, source_target_pairs={{0,16},{2,18},{4,20},{6,22},{8,24},{10,26},{12,28},{14,30},{16,0},... | collective-permute-start | bytes 12296 | tf_op jit(solution)/shard_map/ppermute | solution.py:81
  44.8 54.0 %collective-permute-start.1 = (bf16[4,384,256]{2,1,0:T(8,128)(2,1)S(1)}, bf16[4,384,256]{2,1,0:T(8,128)(2,1)S(1)}, u32[]{:S(2)}, u32[]{:S(2)}) collective-permute-start(bf16[4,384,256]{2,1,0:T(8,128)(2,1)S(1)} %get-tuple-element.24), channel_id=1, source_target_pairs={{14,0},{15,1},{16,2},{17,3},{18,4},{19,5},{20,6},{21,7},{22,8},{23... | collective-permute-start | bytes 2359304 | tf_op jit(solution)/shard_map/ppermute | solution.py:62
  54.3 16.1 %collective-permute-start.3 = (bf16[1,384,256]{2,1,0:T(8,128)(2,1)S(1)}, bf16[1,384,256]{2,1,0:T(8,128)(2,1)S(1)}, u32[]{:S(2)}, u32[]{:S(2)}) collective-permute-start(bf16[1,384,256]{2,1,0:T(8,128)(2,1)S(1)} %get-tuple-element.28), channel_id=1, source_target_pairs={{0,16},{1,17},{2,18},{3,19},{4,20},{5,21},{6,22},{7,23},{8,24},{9,... | collective-permute-start | bytes 589832 | tf_op jit(solution)/shard_map/ppermute | solution.py:62
  60.0 10.4 %copy-start.10 = (bf16[1,384,256]{2,1,0:T(8,128)(2,1)}, bf16[1,384,256]{2,1,0:T(8,128)(2,1)S(1)}, u32[]{:S(2)}) copy-start(bf16[1,384,256]{2,1,0:T(8,128)(2,1)S(1)} %collective-permute-done.5.refs_4_) | copy-start | bytes 589828
  60.0 33.1 %collective-permute-start.8 = (bf16[4,384,256]{2,1,0:T(8,128)(2,1)S(1)}, bf16[4,384,256]{2,1,0:T(8,128)(2,1)}, u32[]{:S(2)}, u32[]{:S(2)}) collective-permute-start(bf16[4,384,256]{2,1,0:T(8,128)(2,1)S(1)} %get-tuple-element.32), channel_id=1, source_target_pairs={{0,2},{1,3},{2,4},{3,5},{4,6},{5,7},{6,0},{7,1},{8,10},{9,11},{10,... | collective-permute-start | bytes 2359304 | tf_op jit(solution)/shard_map/ppermute | solution.py:62
  70.4 28.5 %copy-start.11 = (bf16[1,384,256]{2,1,0:T(8,128)(2,1)}, bf16[1,384,256]{2,1,0:T(8,128)(2,1)S(1)}, u32[]{:S(2)}) copy-start(bf16[1,384,256]{2,1,0:T(8,128)(2,1)S(1)} %collective-permute-done.3.refs_1_) | copy-start | bytes 589828
  70.4 27.1 %collective-permute-start.19 = (bf16[3,384,256]{2,1,0:T(8,128)(2,1)S(1)}, bf16[3,384,256]{2,1,0:T(8,128)(2,1)}, u32[]{:S(2)}, u32[]{:S(2)}) collective-permute-start(bf16[3,384,256]{2,1,0:T(8,128)(2,1)S(1)} %get-tuple-element.40), channel_id=1, source_target_pairs={{4,4},{5,1},{6,6},{7,3},{8,0},{9,13},{10,2},{11,15},{12,12},{13,9}... | collective-permute-start | bytes 1769480 | tf_op jit(solution)/shard_map/ppermute | solution.py:62
  71.7 55.1 %collective-permute-start.4 = (bf16[4,384,256]{2,1,0:T(8,128)(2,1)S(1)}, bf16[4,384,256]{2,1,0:T(8,128)(2,1)S(1)}, u32[]{:S(2)}, u32[]{:S(2)}) collective-permute-start(bf16[4,384,256]{2,1,0:T(8,128)(2,1)S(1)} %get-tuple-element.29), channel_id=1, source_target_pairs={{0,14},{1,15},{2,16},{3,17},{4,18},{5,19},{6,20},{7,21},{8,22},{9,... | collective-permute-start | bytes 2359304 | tf_op jit(solution)/shard_map/ppermute | solution.py:62
  74.0 62.1 %collective-permute-start.13 = (bf16[4,384,256]{2,1,0:T(8,128)(2,1)}, bf16[4,384,256]{2,1,0:T(8,128)(2,1)S(1)}, u32[]{:S(2)}, u32[]{:S(2)}) collective-permute-start(bf16[4,384,256]{2,1,0:T(8,128)(2,1)} %collective-permute-done.12), channel_id=1, source_target_pairs={{8,0},{9,1},{10,2},{11,3},{12,4},{13,5},{22,6},{23,7},{16,8},{17,9... | collective-permute-start | bytes 2359304 | tf_op jit(solution)/shard_map/ppermute | solution.py:67
  93.1 47.7 %collective-permute-start.9 = (bf16[4,384,256]{2,1,0:T(8,128)(2,1)}, bf16[4,384,256]{2,1,0:T(8,128)(2,1)}, u32[]{:S(2)}, u32[]{:S(2)}) collective-permute-start(bf16[4,384,256]{2,1,0:T(8,128)(2,1)} %collective-permute-done.8), channel_id=1, source_target_pairs={{2,10},{3,11},{4,12},{5,13},{6,14},{7,15},{0,16},{1,17},{10,18},{1... | collective-permute-start | bytes 2359304 | tf_op jit(solution)/shard_map/ppermute | solution.py:67
  97.5 26.0 %collective-permute-start.11 = (bf16[1,384,256]{2,1,0:T(8,128)(2,1)S(1)}, bf16[1,384,256]{2,1,0:T(8,128)(2,1)S(1)}, u32[]{:S(2)}, u32[]{:S(2)}) collective-permute-start(bf16[1,384,256]{2,1,0:T(8,128)(2,1)S(1)} %get-tuple-element.34), channel_id=1, source_target_pairs={{8,0},{9,1},{10,2},{11,3},{12,4},{13,5},{14,6},{15,7},{16,8},{17,9... | collective-permute-start | bytes 589832 | tf_op jit(solution)/shard_map/ppermute | solution.py:62
  98.8 9.2 %copy-start.5 = (bf16[4,384,256]{2,1,0:T(8,128)(2,1)}, bf16[4,384,256]{2,1,0:T(8,128)(2,1)S(1)}, u32[]{:S(2)}) copy-start(bf16[4,384,256]{2,1,0:T(8,128)(2,1)S(1)} %collective-permute-done.1.refs_7_.refs_3_) | copy-start | bytes 2359300
  98.9 38.8 %copy-start.16 = (s32[5,384]{1,0:T(8,128)S(1)}, s32[5,384]{1,0:T(8,128)}, u32[]{:S(2)}) copy-start(s32[5,384]{1,0:T(8,128)} %param.19) | copy-start | bytes 23044
  98.9 40.1 %copy-start.14 = (f32[5,256]{1,0:T(8,128)S(1)}, f32[5,256]{1,0:T(8,128)}, u32[]{:S(2)}) copy-start(f32[5,256]{1,0:T(8,128)} %gain.3) | copy-start | bytes 15364
  98.9 40.1 %copy-start.15 = (f32[5,256]{1,0:T(8,128)S(1)}, f32[5,256]{1,0:T(8,128)}, u32[]{:S(2)}) copy-start(f32[5,256]{1,0:T(8,128)} %shift_term.3) | copy-start | bytes 15364
  98.9 26.0 %collective-permute-start.10 = (bf16[1,384,256]{2,1,0:T(8,128)(2,1)S(1)}, bf16[1,384,256]{2,1,0:T(8,128)(2,1)S(1)}, u32[]{:S(2)}, u32[]{:S(2)}) collective-permute-start(bf16[1,384,256]{2,1,0:T(8,128)(2,1)S(1)} %get-tuple-element.33), channel_id=1, source_target_pairs={{0,8},{1,9},{2,10},{3,11},{4,12},{5,13},{6,14},{7,15},{8,16},{9,17... | collective-permute-start | bytes 589832 | tf_op jit(solution)/shard_map/ppermute | solution.py:62
  123.5 14.1 %copy-start.12 = (bf16[1,384,256]{2,1,0:T(8,128)(2,1)}, bf16[1,384,256]{2,1,0:T(8,128)(2,1)S(1)}, u32[]{:S(2)}) copy-start(bf16[1,384,256]{2,1,0:T(8,128)(2,1)S(1)} %collective-permute-done.11.refs_8_) | copy-start | bytes 589828
  123.5 25.7 %collective-permute-start.17 = (bf16[3,384,256]{2,1,0:T(8,128)(2,1)}, bf16[3,384,256]{2,1,0:T(8,128)(2,1)S(1)}, u32[]{:S(2)}, u32[]{:S(2)}) collective-permute-start(bf16[3,384,256]{2,1,0:T(8,128)(2,1)} %collective-permute-done.16), channel_id=1, source_target_pairs={{0,4},{5,5},{2,6},{7,7},{12,8},{1,9},{14,10},{3,11},{8,12},{13,13}... | collective-permute-start | bytes 1769480 | tf_op jit(solution)/shard_map/ppermute | solution.py:67
  124.9 12.8 %copy-start.13 = (bf16[1,384,256]{2,1,0:T(8,128)(2,1)}, bf16[1,384,256]{2,1,0:T(8,128)(2,1)S(1)}, u32[]{:S(2)}) copy-start(bf16[1,384,256]{2,1,0:T(8,128)(2,1)S(1)} %collective-permute-done.10.refs_7_) | copy-start | bytes 589828
  124.9 24.3 %collective-permute-start.20 = (bf16[3,384,256]{2,1,0:T(8,128)(2,1)}, bf16[3,384,256]{2,1,0:T(8,128)(2,1)S(1)}, u32[]{:S(2)}, u32[]{:S(2)}) collective-permute-start(bf16[3,384,256]{2,1,0:T(8,128)(2,1)} %collective-permute-done.19), channel_id=1, source_target_pairs={{4,0},{1,1},{6,2},{3,3},{0,4},{13,5},{2,6},{15,7},{12,8},{9,9},{14... | collective-permute-start | bytes 1769480 | tf_op jit(solution)/shard_map/ppermute | solution.py:67
  126.8 14.0 %copy-start.6 = (bf16[4,384,256]{2,1,0:T(8,128)(2,1)}, bf16[4,384,256]{2,1,0:T(8,128)(2,1)S(1)}, u32[]{:S(2)}) copy-start(bf16[4,384,256]{2,1,0:T(8,128)(2,1)S(1)} %collective-permute-done.4.refs_2_) | copy-start | bytes 2359300
  126.8 22.4 %collective-permute-start.15 = (bf16[2,384,256]{2,1,0:T(8,128)(2,1)S(1)}, bf16[2,384,256]{2,1,0:T(8,128)(2,1)}, u32[]{:S(2)}, u32[]{:S(2)}) collective-permute-start(bf16[2,384,256]{2,1,0:T(8,128)(2,1)S(1)} %get-tuple-element.37), channel_id=1, source_target_pairs={{0,6},{1,7},{2,8},{3,9},{4,10},{5,11},{6,12},{7,13},{8,14},{9,15},... | collective-permute-start | bytes 1179656 | tf_op jit(solution)/shard_map/ppermute | solution.py:62
  136.1 1.5 copy-start.7
  136.2 13.0 %collective-permute-start.21 = (bf16[2,384,256]{2,1,0:T(8,128)(2,1)S(1)}, bf16[2,384,256]{2,1,0:T(8,128)(2,1)}, u32[]{:S(2)}, u32[]{:S(2)}) collective-permute-start(bf16[2,384,256]{2,1,0:T(8,128)(2,1)S(1)} %get-tuple-element.42), channel_id=1, source_target_pairs={{6,0},{7,1},{8,2},{9,3},{10,4},{11,5},{12,6},{13,7},{14,8},{15,9},... | collective-permute-start | bytes 1179656 | tf_op jit(solution)/shard_map/ppermute | solution.py:62
  149.2 0.8 copy-start.8
  149.2 1.0 copy-start.9
